TPU v7x, 32 devices: a whole 2x2x4 slice. The times are simulated.
32 devices in a mesh: grp: 2 (over x), row: 16 (over z, y, core).
Axes of the slice: x: 2, y: 2, z: 4, core: 2. Of those that a mesh axis runs over, the one named last changes fastest.
Arguments:
- object_slices: float32 [2, 2, 2048, 2048], P(None, None, ('grp', 'row')), parts along dimension 2
- probe_modes: float32 [8, 2, 128, 128], P('grp'), parts along dimension 0, may hold values from -2.1 to 2.1
- propagator_phase: float32 [128, 128], replicated, may hold values from -3.140625 to 3.140625
- measured: float32 [256, 128, 128], P(('grp', 'row')), parts along dimension 0, may hold values from 0.25 to 4
- offsets: int32 [256, 2], P(('grp', 'row')), parts along dimension 0, may hold values from 0 to 1920, as said below
- counts: int32 [32], P(('grp', 'row')), parts along dimension 0, may hold values from 1 to 8, 72 in all
Outputs:
- object_grad: float32 [2, 2, 2048, 2048], P(None, None, ('grp', 'row')), parts along dimension 2
- probe_step: float32 [8, 2, 128, 128], P('grp'), parts along dimension 0
There are 2 independent parts, one for each index of `grp`. A program takes and returns all parts, laid end to end along the dimension named above; an argument that names none is the same for every part. Nothing has to cross between parts.
Inputs may be any that keep to these rules, and one draw needn't show every extreme that they name: The slots of device d (slots d * 8 to d * 8 + 7) have row offsets d * 64 to d * 64 + 63 and column offsets 0 to 1920. `counts`: counts sum to 72; some device holds 8.
All inputs are finite; a program needn't handle non-finite values.
Results may differ from a plain program's by a relative error of at most 0.0003.
Values sent between devices are 32-bit elements; how exact they have to be, the bound alone decides.
No kernel may reach another device: no remote copies, remote signals or barrier semaphores. Data moves between devices by JAX's collectives and lax.ppermute only.
A program may use at most 64 MiB of HBM per device.

v0:
```python
import functools

import jax
import jax.numpy as jnp
import numpy as np
from jax import lax
from jax.experimental import pallas as pl
from jax.experimental.pallas import tpu as pltpu
from jax.sharding import PartitionSpec as P

CHUNKS = (4, 4)
BATCH = 2
VMEM_LIMIT = 48 * 1024 * 1024
F32 = jnp.float32
BF16 = jnp.bfloat16


def shifted(array, axis, by):
    peers = lax.axis_size(axis)
    return lax.ppermute(array, axis, [(i, (i + by) % peers) for i in range(peers)])


def fourier_tables(pixels):
    indices = np.arange(pixels)
    angles = 2.0 * np.pi * (indices[:, None] * indices[None, :] % pixels) / pixels
    re = np.cos(angles) / np.sqrt(pixels)
    im = -np.sin(angles) / np.sqrt(pixels)
    left = np.block([[re, -im], [im, re]]).astype(np.float32)
    high = left.astype(BF16)
    low = (left - high.astype(np.float32)).astype(BF16)
    return np.stack([high, low, high.T, low.T])


def pieces(array):
    high = array.astype(BF16)
    return high, (array - high.astype(F32)).astype(BF16)


def transform(tables, conj, groups):
    at_left, at_right = (2, 0) if conj else (0, 2)
    left = jnp.concatenate([tables[at_left], tables[at_left + 1], tables[at_left]], axis=1)
    right = jnp.concatenate([tables[at_right], tables[at_right], tables[at_right + 1]], axis=0)
    pixels = left.shape[0] // 2
    halves = []
    for waves in groups:
        stacked = jnp.concatenate([jnp.concatenate(wave, axis=0) for wave in waves], axis=1)
        high, low = pieces(stacked)
        half = jnp.dot(left, jnp.concatenate([high, high, low], axis=0), preferred_element_type=F32)
        turned = [
            jnp.concatenate([half[:pixels, at : at + pixels], half[pixels:, at : at + pixels]], axis=1)
            for at in range(0, half.shape[1], pixels)
        ]
        halves.append(pieces(jnp.concatenate(turned, axis=0)))
    wholes = []
    for high, low in halves:
        whole = jnp.dot(jnp.concatenate([high, low, high], axis=1), right, preferred_element_type=F32)
        wholes.append(
            [
                (whole[at : at + pixels, :pixels], whole[at : at + pixels, pixels:])
                for at in range(0, whole.shape[0], pixels)
            ]
        )
    return wholes


def times(one, two):
    return one[0] * two[0] - one[1] * two[1], one[0] * two[1] + one[1] * two[0]


def conj_times(one, two):
    return one[0] * two[0] + one[1] * two[1], one[0] * two[1] - one[1] * two[0]


def place(column, columns, pixels):
    base = jnp.minimum(column // pixels * pixels, columns - 2 * pixels)
    return pl.multiple_of(base, pixels), column - base


def cut(tile, column, pixels):
    base, shift = place(column, tile.shape[-1], pixels)
    rows = tile.shape[1]
    wide = tile[:, :, pl.ds(base, 2 * pixels)].reshape(-1, 2 * pixels)
    turned = pltpu.roll(wide, 2 * pixels - shift, 1)
    return turned[:, :pixels].reshape(-1, rows, pixels)


def is_even(offsets, rows):
    return lax.rem(offsets[0, 0] // rows, 2) == 0


def cut_kernel(pixels, chunks, own, far, tile, *outs):
    planes, rows, _ = tile.shape
    even = is_even(own, rows)
    for (first, size), near, cross in zip(chunks, outs[::2], outs[1::2], strict=True):
        for at in range(size):
            slot = first + at
            strip = at * planes
            near[strip : strip + planes] = cut(tile, jnp.where(even, own[slot, 1], far[slot, 1]), pixels)
            cross[strip : strip + planes] = cut(tile, jnp.where(even, far[slot, 1], own[slot, 1]), pixels)
        if first == 0:
            for slot in range(own.shape[0]):
                for entry in range(2):
                    line = jnp.full((1, pixels), own[slot, entry], jnp.int32).astype(F32)
                    near[near.shape[0] - 1, 2 * slot + entry : 2 * slot + entry + 1] = line
                    cross[cross.shape[0] - 1, 2 * slot + entry : 2 * slot + entry + 1] = line


def add_kernel(pixels, groups, own, middle, far, *refs):
    *parts, out = refs
    planes, rows, _ = out.shape
    even = is_even(own, rows)
    out[...] = jnp.zeros_like(out)
    lane = lax.broadcasted_iota(jnp.int32, (1, 1, pixels), 2)
    for (kind, first, size, unit), strips in zip(groups, parts):

        def add(at, carry, kind=kind, first=first, unit=unit, strips=strips):
            slot = first + at
            if kind == "mid":
                column = middle[slot, 1]
            elif kind == "near":
                column = jnp.where(even, own[slot, 1], far[slot, 1])
            else:
                column = jnp.where(even, far[slot, 1], own[slot, 1])
            base, shift = place(column, out.shape[-1], pixels)
            part = strips[pl.ds(unit + at * planes, planes)]
            turned = pltpu.roll(part.reshape(-1, pixels), lax.rem(shift, pixels), 1).reshape(part.shape)
            out[:, :, pl.ds(base, pixels)] += jnp.where(lane >= shift, turned, 0.0)
            out[:, :, pl.ds(pl.multiple_of(base + pixels, pixels), pixels)] += jnp.where(
                lane < shift, turned, 0.0
            )
            return carry

        lax.fori_loop(0, size, add, 0)


def slot_kernel(
    first, size, ahead, own_offsets, *refs
):
    if first == 0:
        offsets, refs = refs[-6], refs[:-6] + refs[-5:]
    else:
        offsets, *refs = refs
    tile, near, cross, target, probe, prop, tables, so_far, *refs = refs
    given, refs = refs[:ahead], refs[ahead:]
    out_near, out_mid, out_cross, total, *shares = refs[:-5]
    window, patch, grads, exit_wave, far = refs[-5:]
    modes, _, pixels, _ = probe.shape
    planes, rows, _ = tile.shape
    behind = given[0].shape[0] if given else 0
    for message, out in zip(given, (out_near, out_cross)):
        out[:behind] = message[...]
    even = is_even(own_offsets, rows)
    if first == 0:
        for slot in range(offsets.shape[0]):
            for entry in range(2):
                line = pl.ds(2 * slot + entry, 1)
                value = jnp.where(even, cross[cross.shape[0] - 1, line], near[near.shape[0] - 1, line])
                offsets[slot, entry] = jnp.max(value).astype(jnp.int32)
    total[...] = so_far[...]
    held = range(BATCH)

    def is_live(at):
        return jnp.max(target[first + at, :8]) > 0.0

    def leave(slots):
        for at in slots:
            for out, unit in ((out_near, behind), (out_mid, 0), (out_cross, behind)):
                out[pl.ds(unit + at * planes, planes)] = jnp.zeros((planes, rows, pixels), F32)

    def visit(slots):
        starts = [lax.rem(offsets[first + at, 0], rows) for at in slots]
        live = [jnp.where(is_live(at), 1.0, 0.0).astype(F32) for at in slots]
        for s, at in enumerate(slots):
            strip = pl.ds(at * planes, planes)
            window[:, :rows] = jnp.where(even, cross[strip], near[strip])
            window[:, rows : 2 * rows] = cut(tile, offsets[first + at, 1], pixels)
            window[:, 2 * rows :] = jnp.where(even, near[strip], cross[strip])
            patch[s] = window[:, pl.ds(starts[s], pixels), :]
            total[2 * modes] += live[s] * (patch[s, 0] * patch[s, 0] + patch[s, 1] * patch[s, 1])
        all_modes = range(modes)
        groups = [
            [times((probe[m, 0], probe[m, 1]), (patch[s, 0], patch[s, 1])) for m in all_modes] for s in held
        ]
        groups = transform(tables, False, groups)
        groups = [[times((prop[0], prop[1]), wave) for wave in waves] for waves in groups]
        groups = transform(tables, True, groups)
        for s in held:
            for m in all_modes:
                exit_wave[s, m, 0], exit_wave[s, m, 1] = groups[s][m]
            groups[s] = [times(wave, (patch[s, 2], patch[s, 3])) for wave in groups[s]]
        groups = transform(tables, False, groups)
        for s, at in enumerate(slots):
            intensity = jnp.zeros((pixels, pixels), F32)
            for m in all_modes:
                wave = groups[s][m]
                far[s, m, 0], far[s, m, 1] = wave
                intensity = intensity + wave[0] * wave[0] + wave[1] * wave[1]
            misfit = 2.0 * live[s] * (intensity - target[first + at])
            groups[s] = [(misfit * far[s, m, 0], misfit * far[s, m, 1]) for m in all_modes]
        groups = transform(tables, True, groups)
        for s in held:
            grad_re, grad_im = jnp.zeros((pixels, pixels), F32), jnp.zeros((pixels, pixels), F32)
            for m in all_modes:
                re, im = conj_times((exit_wave[s, m, 0], exit_wave[s, m, 1]), groups[s][m])
                grad_re, grad_im = grad_re + re, grad_im + im
            grads[s, 2], grads[s, 3] = grad_re, grad_im
            groups[s] = [conj_times((patch[s, 2], patch[s, 3]), wave) for wave in groups[s]]
        groups = transform(tables, False, groups)
        groups = [[conj_times((prop[0], prop[1]), wave) for wave in waves] for waves in groups]
        groups = transform(tables, True, groups)
        for s in held:
            grad_re, grad_im = jnp.zeros((pixels, pixels), F32), jnp.zeros((pixels, pixels), F32)
            for m in all_modes:
                re, im = conj_times((patch[s, 0], patch[s, 1]), groups[s][m])
                total[2 * m] += re
                total[2 * m + 1] += im
                re, im = conj_times((probe[m, 0], probe[m, 1]), groups[s][m])
                grad_re, grad_im = grad_re + re, grad_im + im
            grads[s, 0], grads[s, 1] = grad_re, grad_im
        for s, at in enumerate(slots):
            window[...] = jnp.zeros_like(window)
            window[:, pl.ds(starts[s], pixels), :] = grads[s]
            strip = pl.ds(behind + at * planes, planes)
            out_near[strip] = jnp.where(even, window[:, 2 * rows :], window[:, :rows])
            out_mid[pl.ds(at * planes, planes)] = window[:, rows : 2 * rows]
            out_cross[strip] = jnp.where(even, window[:, :rows], window[:, 2 * rows :])

    def step(index, carry):
        slots = [index * BATCH + s for s in range(BATCH)]
        some = is_live(slots[0])
        pl.when(some)(lambda: visit(slots))
        pl.when(jnp.logical_not(some))(lambda: leave(slots))
        return carry

    lax.fori_loop(0, size // BATCH, step, 0)

    if shares:
        own, other = shares
        chips, _, share, _ = own.shape
        core = jnp.where(even, 0, 1)
        for chip in range(chips):
            for plane in range(2 * modes + 1):
                own[chip, plane] = total[plane, pl.ds((2 * chip + core) * share, share)]
                other[chip, plane] = total[plane, pl.ds((2 * chip + 1 - core) * share, share)]


def step_kernel(parts, out):
    summed = parts[0]
    for at in range(1, parts.shape[0]):
        summed = summed + parts[at]
    step = summed[:-1] / (summed[-1:] + 1.0)
    for at in range(out.shape[0]):
        out[at] = step


def order_kernel(rows, offsets, own, other, out):
    chips, _, share, _ = own.shape
    core = jnp.where(is_even(offsets, rows), 0, 1)
    for chip in range(chips):
        out[:, pl.ds((2 * chip + core) * share, share)] = own[chip]
        out[:, pl.ds((2 * chip + 1 - core) * share, share)] = other[chip]


def in_smem():
    return pl.BlockSpec(memory_space=pltpu.SMEM)


def in_vmem():
    return pl.BlockSpec(memory_space=pltpu.VMEM)


def local(object_slices, probe_modes, propagator_phase, measured, offsets, counts):
    slices, _, tile_rows, columns = object_slices.shape
    modes, _, pixels, _ = probe_modes.shape
    planes = 2 * slices
    peers = lax.axis_size("row")
    params = pltpu.CompilerParams(vmem_limit_bytes=VMEM_LIMIT)
    tile = object_slices.reshape(planes, tile_rows, columns)
    starts = [sum(CHUNKS[:i]) for i in range(len(CHUNKS))]

    pair = [(i, i ^ 1) for i in range(peers)]
    other_pair = [(i, (i - 1) % peers if i % 2 == 0 else (i + 1) % peers) for i in range(peers)]
    far = shifted(offsets, "row", 2)

    live = lax.broadcasted_iota(jnp.int32, (measured.shape[0], 1, 1), 0) < counts[0]
    target = jnp.where(live, measured, 0.0)
    far, target = lax.optimization_barrier((far, target))
    target = shifted(target, "row", 1)

    def units(count):
        return jax.ShapeDtypeStruct((count, tile_rows, pixels), F32)

    def strips(chunks):
        shapes = [units(size * planes + (first == 0)) for first, size in chunks for _ in range(2)]
        outs = pl.pallas_call(
            functools.partial(cut_kernel, pixels, chunks),
            out_shape=shapes,
            in_specs=[in_smem()] * 2 + [in_vmem()],
            out_specs=[in_vmem()] * len(shapes),
            compiler_params=params,
            cost_estimate=pl.CostEstimate(flops=0, bytes_accessed=4 << 20, transcendentals=0),
        )(offsets, far, tile)
        return list(zip(outs[::2], outs[1::2]))

    def swapped(to_near, to_cross):
        return lax.ppermute(to_near, "row", pair), lax.ppermute(to_cross, "row", other_pair)

    chunks = list(zip(starts, CHUNKS))
    waiting = strips(chunks[:1]) + strips(chunks[1:])
    arrived = [swapped(*waiting[0])]
    if len(waiting) > 1:
        arrived[0], following = lax.optimization_barrier((arrived[0], waiting[1]))
        arrived.append(swapped(*following))
    prop = jnp.stack([jnp.cos(propagator_phase), jnp.sin(propagator_phase)])
    tables = jnp.asarray(fourier_tables(pixels))

    share = pixels // peers
    total = jnp.zeros((2 * modes + 1, pixels, pixels), F32)
    mid, back, mid_groups, back_groups, places = [], [], [], [], [offsets]
    for index, (first, size) in enumerate(chunks):
        given = waiting[index + 2] if index + 2 < len(chunks) else ()
        ahead = CHUNKS[index + 2] * planes if given else 0
        part = jax.ShapeDtypeStruct((peers // 2, 2 * modes + 1, share, pixels), F32)
        shares = [part, part] if index == len(CHUNKS) - 1 else []
        message = units(ahead + size * planes)
        field = pltpu.VMEM((BATCH, planes, pixels, pixels), F32)
        kept = pltpu.VMEM((BATCH, modes, 2, pixels, pixels), F32)
        to_near, to_mid, to_cross, total, *shares = pl.pallas_call(
            functools.partial(slot_kernel, first, size, len(given)),
            out_shape=[message, units(size * planes), message, jax.ShapeDtypeStruct(total.shape, F32)]
            + shares
            + ([] if index else [jax.ShapeDtypeStruct(offsets.shape, jnp.int32)]),
            in_specs=[in_smem()] * len(places) + [in_vmem()] * (8 + len(given)),
            out_specs=[in_vmem()] * (4 + len(shares)) + ([] if index else [in_smem()]),
            scratch_shapes=[pltpu.VMEM((planes, 3 * tile_rows, pixels), F32), field, field, kept, kept],
            compiler_params=params,
            cost_estimate=pl.CostEstimate(
                flops=size * 6 * modes * 3 * 16 * pixels**3, bytes_accessed=8 << 20, transcendentals=0
            ),
        )(*places, tile, *arrived[index], target, probe_modes, prop, tables, total, *given)
        if index == 0:
            middle = shares.pop()
            places.append(middle)
        mid_groups.append(("mid", first, size, 0))
        mid.append(to_mid)
        message = swapped(to_near, to_cross)
        if given:
            arrived.append(message)
        back_groups += [(kind, first, size, ahead) for kind in ("near", "cross")]
        back.append(message)

    def added(groups, strips):
        return pl.pallas_call(
            functools.partial(add_kernel, pixels, groups),
            out_shape=jax.ShapeDtypeStruct(tile.shape, F32),
            in_specs=[in_smem()] * 3 + [in_vmem()] * len(strips),
            out_specs=in_vmem(),
            compiler_params=params,
            cost_estimate=pl.CostEstimate(flops=0, bytes_accessed=5 << 20, transcendentals=0),
        )(offsets, middle, far, *strips)

    cores = [list(range(core, peers, 2)) for core in range(2)]
    own, other = shares
    own, other, back[:-1] = lax.optimization_barrier((own, other, back[:-1]))
    both = own + lax.ppermute(other, "row", pair)
    parts = lax.all_to_all(both, "row", 0, 0, axis_index_groups=cores)
    spread = pl.pallas_call(
        step_kernel,
        out_shape=jax.ShapeDtypeStruct((peers // 2, 2 * modes, share, pixels), F32),
        in_specs=[in_vmem()],
        out_specs=in_vmem(),
        compiler_params=params,
    )(parts)
    groups = mid_groups + back_groups
    strips = mid + [part for message in back for part in message]
    spread, strips = lax.optimization_barrier((spread, strips))
    gathered = lax.all_to_all(spread, "row", 0, 0, axis_index_groups=cores)
    gathered, strips = lax.optimization_barrier((gathered, strips))

    object_grad = added(groups, strips)
    object_grad = object_grad.reshape(object_slices.shape)

    probe_step = pl.pallas_call(
        functools.partial(order_kernel, tile_rows),
        out_shape=jax.ShapeDtypeStruct((2 * modes, pixels, pixels), F32),
        in_specs=[in_smem()] + [in_vmem()] * 2,
        out_specs=in_vmem(),
        compiler_params=params,
    )(offsets, gathered, lax.ppermute(gathered, "row", pair)).reshape(probe_modes.shape)
    return (object_grad, probe_step)


def solution(mesh):
    in_specs = (
        P(None, None, ("grp", "row"), None),
        P("grp", None, None, None),
        P(),
        P(("grp", "row"), None, None),
        P(("grp", "row"), None),
        P(("grp", "row")),
    )
    out_specs = (P(None, None, ("grp", "row"), None), P("grp", None, None, None))
    return jax.shard_map(local, mesh=mesh, in_specs=in_specs, out_specs=out_specs, check_vma=False)
```

profile of v0, /device:TPU:1, one launch (start us, length us, event | category | flops | bytes accessed | tf_op | source)
XLA Modules:
  0.0 104.1 jit_solution(16900285819614517832)
XLA Ops:
  0.6 0.0 copy-start.3
  0.6 0.8 copy.14.own.own_offsets.offsets
  1.4 2.1 %collective-permute-start = (s32[8,2]{1,0:T(8,128)S(1)}, s32[8,2]{1,0:T(8,128)S(1)}, u32[]{:S(2)}, u32[]{:S(2)}) collective-permute-start(s32[8,2]{1,0:T(8,128)S(1)} %copy.14.own.own_offsets.offsets), channel_id=1, source_target_pairs={{0,2},{1,3},{2,4},{3,5},{4,6},{5,7},{6,8},{7,9},{8,10},{9,11},{10,... | collective-permute-start | bytes 200 | tf_op jit(solution)/shard_map/ppermute | solution.py:20
  4.2 1.1 %broadcast_select_fusion = f32[8,128,128]{2,1,0:T(8,128)S(1)} fusion(f32[8,128,128]{2,1,0:T(8,128)} %param.10, pred[8]{0:T(512)(128)(4,1)S(1)} %iota_compare_fusion), kind=kLoop, calls=%fused_computation | loop fusion | flops 131072 | bytes 1048584 | tf_op jit(solution)/shard_map/jit(_where)/select_n | solution.py:286
  5.3 2.2 %collective-permute-done.far = s32[8,2]{1,0:T(8,128)S(1)} collective-permute-done((s32[8,2]{1,0:T(8,128)S(1)}, s32[8,2]{1,0:T(8,128)S(1)}, u32[]{:S(2)}, u32[]{:S(2)}) %collective-permute-start) | collective-permute-done | bytes 96 | tf_op jit(solution)/shard_map/ppermute | solution.py:20
  7.5 0.0 copy-start
  7.5 1.6 %copy-done = f32[2,2,64,2048]{3,2,1,0:T(8,128)S(1)} copy-done((f32[2,2,64,2048]{3,2,1,0:T(8,128)S(1)}, f32[2,2,64,2048]{3,2,1,0:T(8,128)}, u32[]{:S(2)}) %copy-start) | copy-done | bytes 2097176
  9.1 1.3 %shard_map.86 = (f32[17,64,128]{2,1,0:T(8,128)S(1)}, f32[17,64,128]{2,1,0:T(8,128)S(1)}) custom-call(s32[8,2]{1,0:T(8,128)S(1)} %copy.14.own.own_offsets.offsets, s32[8,2]{1,0:T(8,128)S(1)} %collective-permute-done.far, f32[4,64,2048]{2,1,0:T(8,128)S(1)} %bitcast.11), custom_call_target="tpu_custom_call" | custom-call | bytes 4194304 | tf_op jit(solution)/shard_map/pallas_call | solution.py:295
  10.4 0.0 copy-start.1
  10.4 0.0 copy-start.2
  10.4 1.6 %collective-permute-start.1 = (f32[17,64,128]{2,1,0:T(8,128)S(1)}, f32[17,64,128]{2,1,0:T(8,128)S(1)}, u32[]{:S(2)}, u32[]{:S(2)}) collective-permute-start(f32[17,64,128]{2,1,0:T(8,128)S(1)} %get-tuple-element.41), channel_id=1, source_target_pairs={{0,1},{1,0},{2,3},{3,2},{4,5},{5,4},{6,7},{7,6},{8,9},{9,8},{10,11... | collective-permute-start | bytes 1671176 | tf_op jit(solution)/shard_map/ppermute | solution.py:306
  12.0 0.0 collective-permute-start.2
  12.1 1.7 %collective-permute-start.3 = (f32[8,128,128]{2,1,0:T(8,128)S(1)}, f32[8,128,128]{2,1,0:T(8,128)S(1)}, u32[]{:S(2)}, u32[]{:S(2)}) collective-permute-start(f32[8,128,128]{2,1,0:T(8,128)S(1)} %broadcast_select_fusion), channel_id=1, source_target_pairs={{0,1},{1,2},{2,3},{3,4},{4,5},{5,6},{6,7},{7,8},{8,9},{9,10},{10,1... | collective-permute-start | bytes 1572872 | tf_op jit(solution)/shard_map/ppermute | solution.py:20
  13.8 0.0 copy-done.3
  13.8 0.2 cosine_bitcast_fusion
  14.1 1.3 %shard_map.87 = (f32[16,64,128]{2,1,0:T(8,128)S(1)}, f32[16,64,128]{2,1,0:T(8,128)S(1)}) custom-call(s32[8,2]{1,0:T(8,128)S(1)} %copy.14.own.own_offsets.offsets, s32[8,2]{1,0:T(8,128)S(1)} %collective-permute-done.far, f32[4,64,2048]{2,1,0:T(8,128)S(1)} %bitcast.12), custom_call_target="tpu_custom_call" | custom-call | bytes 4194304 | tf_op jit(solution)/shard_map/pallas_call | solution.py:295
  15.4 0.0 collective-permute-done.1.refs_1_
  15.4 17.2 %collective-permute-done.2.refs_2_ = f32[17,64,128]{2,1,0:T(8,128)S(1)} collective-permute-done((f32[17,64,128]{2,1,0:T(8,128)S(1)}, f32[17,64,128]{2,1,0:T(8,128)S(1)}, u32[]{:S(2)}, u32[]{:S(2)}) %collective-permute-start.2) | collective-permute-done | bytes 557088 | tf_op jit(solution)/shard_map/ppermute | solution.py:306
  32.6 0.0 collective-permute-start.4
  32.6 0.0 collective-permute-start.5
  32.6 0.0 collective-permute-done.3.refs_3_.refs_4_
  32.7 0.0 copy-done.1
  32.7 0.0 copy-done.2
  32.7 15.9 %shard_map.88 = (f32[16,64,128]{2,1,0:T(8,128)S(1)}, f32[16,64,128]{2,1,0:T(8,128)S(1)}, f32[16,64,128]{2,1,0:T(8,128)S(1)}, f32[9,128,128]{2,1,0:T(8,128)S(1)}, s32[8,2]{1,0:T(8,128)S(1)}) custom-call(s32[8,2]{1,0:T(8,128)S(1)} %copy.14.own.own_offsets.offsets, f32[4,64,2048]{2,1,0:T(8,128)} %bitcast.9, f32[17,64,128]{2,1,0:T(8,128)S(1)} %collective-permute-done.1.refs_1_, ...), custom_call_target="tpu_custom_call" | custom-call | flops 9663676416 | bytes 8388608 | tf_op jit(solution)/shard_map/pallas_call | solution.py:328
  48.5 1.8 %collective-permute-start.6 = (f32[16,64,128]{2,1,0:T(8,128)S(1)}, f32[16,64,128]{2,1,0:T(8,128)S(1)}, u32[]{:S(2)}, u32[]{:S(2)}) collective-permute-start(f32[16,64,128]{2,1,0:T(8,128)S(1)} %get-tuple-element.54), channel_id=1, source_target_pairs={{0,1},{1,0},{2,3},{3,2},{4,5},{5,4},{6,7},{7,6},{8,9},{9,8},{10,11... | collective-permute-start | bytes 1572872 | tf_op jit(solution)/shard_map/ppermute | solution.py:306
  50.3 0.1 collective-permute-start.7
  50.4 0.0 collective-permute-done.4.refs_2_
  50.4 0.0 collective-permute-done.5.refs_3_
  50.4 16.0 %shard_map.89 = (f32[16,64,128]{2,1,0:T(8,128)S(1)}, f32[16,64,128]{2,1,0:T(8,128)S(1)}, f32[16,64,128]{2,1,0:T(8,128)S(1)}, f32[9,128,128]{2,1,0:T(8,128)}, f32...) custom-call(s32[8,2]{1,0:T(8,128)S(1)} %copy.14.own.own_offsets.offsets, ...), custom_call_target="tpu_custom_call" | custom-call | flops 9663676416 | bytes 8388608 | tf_op jit(solution)/shard_map/pallas_call | solution.py:328
  66.4 0.0 collective-permute-done.6.refs_2_
  66.4 0.0 collective-permute-done.7.refs_3_
  66.4 0.1 collective-permute-start.8
  66.5 0.5 collective-permute-start.9
  67.0 1.7 %collective-permute-start.10 = (f32[16,64,128]{2,1,0:T(8,128)S(1)}, f32[16,64,128]{2,1,0:T(8,128)S(1)}, u32[]{:S(2)}, u32[]{:S(2)}) collective-permute-start(f32[16,64,128]{2,1,0:T(8,128)S(1)} %get-tuple-element.63), channel_id=1, source_target_pairs={{0,15},{1,2},{2,1},{3,4},{4,3},{5,6},{6,5},{7,8},{8,7},{9,10},{10,... | collective-permute-start | bytes 1572872 | tf_op jit(solution)/shard_map/ppermute | solution.py:306
  68.6 0.0 collective-permute-done.8
  68.7 15.4 %all_to_all.10.parts = f32[8,9,8,128]{3,2,1,0:T(8,128)S(1)} all-to-all(f32[8,9,8,128]{3,2,1,0:T(8,128)S(1)} %add.3), channel_id=1, replica_groups={{0,2,4,6,8,10,12,14},{1,3,5,7,9,11,13,15},{16,18,20,22,24,26,28,30},{17..., dimensions={0} | all-to-all | bytes 589824 | tf_op jit(solution)/shard_map/all_to_all | solution.py:366
  84.1 0.0 collective-permute-done.9.refs_4_
  84.2 0.0 collective-permute-done.10.refs_5_
  84.2 10.2 %all_to_all.11.own = f32[8,8,8,128]{3,2,1,0:T(8,128)S(1)} all-to-all(f32[8,8,8,128]{3,2,1,0:T(8,128)S(1)} %shard_map.90), channel_id=1, replica_groups={{0,2,4,6,8,10,12,14},{1,3,5,7,9,11,13,15},{16,18,20,22,24,26,28,30},{17..., dimensions={0} | all-to-all | bytes 524288 | tf_op jit(solution)/shard_map/all_to_all | solution.py:377
  94.3 2.8 %collective-permute-start.11 = (f32[8,8,8,128]{3,2,1,0:T(8,128)S(1)}, f32[8,8,8,128]{3,2,1,0:T(8,128)S(1)}, u32[]{:S(2)}, u32[]{:S(2)}) collective-permute-start(f32[8,8,8,128]{3,2,1,0:T(8,128)S(1)} %all_to_all.11.own), channel_id=1, source_target_pairs={{0,1},{1,0},{2,3},{3,2},{4,5},{5,4},{6,7},{7,6},{8,9},{9,8},{10,11... | collective-permute-start | bytes 786440 | tf_op jit(solution)/shard_map/ppermute | solution.py:389
  97.1 5.5 %shard_map.91 = f32[4,64,2048]{2,1,0:T(8,128)} custom-call(s32[8,2]{1,0:T(8,128)S(1)} %copy.14.own.own_offsets.offsets, s32[8,2]{1,0:T(8,128)S(1)} %get-tuple-element.48.refs_0_.middle, s32[8,2]{1,0:T(8,128)S(1)} %collective-permute-done.far, f32[16,64,128]{2,1,0:T(8,128)S(1)} %get-tuple-element.71.refs_0_, f32[16,64,128]{2,1,0:T(8,128)S(1)} %get-tuple-element.72.refs_1_, ...), custom_call_target="tpu_custom_call" | custom-call | bytes 5242880 | tf_op jit(solution)/shard_map/pallas_call | solution.py:353
  102.6 0.0 collective-permute-done.11.other
  102.6 1.5 %shard_map.92 = f32[8,128,128]{2,1,0:T(8,128)} custom-call(s32[8,2]{1,0:T(8,128)S(1)} %copy.14.own.own_offsets.offsets, f32[8,8,8,128]{3,2,1,0:T(8,128)S(1)} %all_to_all.11.own, f32[8,8,8,128]{3,2,1,0:T(8,128)S(1)} %collective-permute-done.11.other), custom_call_target="tpu_custom_call" | custom-call | tf_op jit(solution)/shard_map/pallas_call | solution.py:383
  (5 shorter events, 0.1 us)
Async XLA Ops:
  0.6 13.2 %copy-start.3 = (f32[128,128]{1,0:T(8,128)S(1)}, f32[128,128]{1,0:T(8,128)}, u32[]{:S(2)}) copy-start(f32[128,128]{1,0:T(8,128)} %param.9) | copy-start | bytes 196612
  1.4 6.1 %collective-permute-start = (s32[8,2]{1,0:T(8,128)S(1)}, s32[8,2]{1,0:T(8,128)S(1)}, u32[]{:S(2)}, u32[]{:S(2)}) collective-permute-start(s32[8,2]{1,0:T(8,128)S(1)} %copy.14.own.own_offsets.offsets), channel_id=1, source_target_pairs={{0,2},{1,3},{2,4},{3,5},{4,6},{5,7},{6,8},{7,9},{8,10},{9,11},{10,... | collective-permute-start | bytes 200 | tf_op jit(solution)/shard_map/ppermute | solution.py:20
  7.5 1.6 %copy-start = (f32[2,2,64,2048]{3,2,1,0:T(8,128)S(1)}, f32[2,2,64,2048]{3,2,1,0:T(8,128)}, u32[]{:S(2)}) copy-start(f32[2,2,64,2048]{3,2,1,0:T(8,128)} %param.7) | copy-start | bytes 6291460
  10.4 22.2 %copy-start.1 = (f32[4,2,128,128]{3,2,1,0:T(8,128)S(1)}, f32[4,2,128,128]{3,2,1,0:T(8,128)}, u32[]{:S(2)}) copy-start(f32[4,2,128,128]{3,2,1,0:T(8,128)} %refs_5_.1) | copy-start | bytes 1572868
  10.4 22.2 %copy-start.2 = (bf16[4,256,256]{2,1,0:T(8,128)(2,1)S(1)}, bf16[4,256,256]{2,1,0:T(8,128)(2,1)}, u32[]{:S(2)}) copy-start(bf16[4,256,256]{2,1,0:T(8,128)(2,1)} %constant.1.clone.refs_6_.refs_7_) | copy-start | bytes 1572868
  10.4 4.9 %collective-permute-start.1 = (f32[17,64,128]{2,1,0:T(8,128)S(1)}, f32[17,64,128]{2,1,0:T(8,128)S(1)}, u32[]{:S(2)}, u32[]{:S(2)}) collective-permute-start(f32[17,64,128]{2,1,0:T(8,128)S(1)} %get-tuple-element.41), channel_id=1, source_target_pairs={{0,1},{1,0},{2,3},{3,2},{4,5},{5,4},{6,7},{7,6},{8,9},{9,8},{10,11... | collective-permute-start | bytes 1671176 | tf_op jit(solution)/shard_map/ppermute | solution.py:306
  12.0 20.5 %collective-permute-start.2 = (f32[17,64,128]{2,1,0:T(8,128)S(1)}, f32[17,64,128]{2,1,0:T(8,128)S(1)}, u32[]{:S(2)}, u32[]{:S(2)}) collective-permute-start(f32[17,64,128]{2,1,0:T(8,128)S(1)} %get-tuple-element.42), channel_id=1, source_target_pairs={{0,15},{1,2},{2,1},{3,4},{4,3},{5,6},{6,5},{7,8},{8,7},{9,10},{10,... | collective-permute-start | bytes 1671176 | tf_op jit(solution)/shard_map/ppermute | solution.py:306
  12.1 20.6 %collective-permute-start.3 = (f32[8,128,128]{2,1,0:T(8,128)S(1)}, f32[8,128,128]{2,1,0:T(8,128)S(1)}, u32[]{:S(2)}, u32[]{:S(2)}) collective-permute-start(f32[8,128,128]{2,1,0:T(8,128)S(1)} %broadcast_select_fusion), channel_id=1, source_target_pairs={{0,1},{1,2},{2,3},{3,4},{4,5},{5,6},{6,7},{7,8},{8,9},{9,10},{10,1... | collective-permute-start | bytes 1572872 | tf_op jit(solution)/shard_map/ppermute | solution.py:20
  32.6 17.8 %collective-permute-start.4 = (f32[16,64,128]{2,1,0:T(8,128)S(1)}, f32[16,64,128]{2,1,0:T(8,128)S(1)}, u32[]{:S(2)}, u32[]{:S(2)}) collective-permute-start(f32[16,64,128]{2,1,0:T(8,128)S(1)} %get-tuple-element.49), channel_id=1, source_target_pairs={{0,1},{1,0},{2,3},{3,2},{4,5},{5,4},{6,7},{7,6},{8,9},{9,8},{10,11... | collective-permute-start | bytes 1572872 | tf_op jit(solution)/shard_map/ppermute | solution.py:306
  32.6 17.8 %collective-permute-start.5 = (f32[16,64,128]{2,1,0:T(8,128)S(1)}, f32[16,64,128]{2,1,0:T(8,128)S(1)}, u32[]{:S(2)}, u32[]{:S(2)}) collective-permute-start(f32[16,64,128]{2,1,0:T(8,128)S(1)} %get-tuple-element.50), channel_id=1, source_target_pairs={{0,15},{1,2},{2,1},{3,4},{4,3},{5,6},{6,5},{7,8},{8,7},{9,10},{10,... | collective-permute-start | bytes 1572872 | tf_op jit(solution)/shard_map/ppermute | solution.py:306
  48.5 17.8 %collective-permute-start.6 = (f32[16,64,128]{2,1,0:T(8,128)S(1)}, f32[16,64,128]{2,1,0:T(8,128)S(1)}, u32[]{:S(2)}, u32[]{:S(2)}) collective-permute-start(f32[16,64,128]{2,1,0:T(8,128)S(1)} %get-tuple-element.54), channel_id=1, source_target_pairs={{0,1},{1,0},{2,3},{3,2},{4,5},{5,4},{6,7},{7,6},{8,9},{9,8},{10,11... | collective-permute-start | bytes 1572872 | tf_op jit(solution)/shard_map/ppermute | solution.py:306
  50.3 16.0 %collective-permute-start.7 = (f32[16,64,128]{2,1,0:T(8,128)S(1)}, f32[16,64,128]{2,1,0:T(8,128)S(1)}, u32[]{:S(2)}, u32[]{:S(2)}) collective-permute-start(f32[16,64,128]{2,1,0:T(8,128)S(1)} %get-tuple-element.55), channel_id=1, source_target_pairs={{0,15},{1,2},{2,1},{3,4},{4,3},{5,6},{6,5},{7,8},{8,7},{9,10},{10,... | collective-permute-start | bytes 1572872 | tf_op jit(solution)/shard_map/ppermute | solution.py:306
  66.4 2.2 %collective-permute-start.8 = (f32[8,9,8,128]{3,2,1,0:T(8,128)S(1)}, f32[8,9,8,128]{3,2,1,0:T(8,128)S(1)}, u32[]{:S(2)}, u32[]{:S(2)}) collective-permute-start(f32[8,9,8,128]{3,2,1,0:T(8,128)S(1)} %get-tuple-element.57), channel_id=1, source_target_pairs={{0,1},{1,0},{2,3},{3,2},{4,5},{5,4},{6,7},{7,6},{8,9},{9,8},{10,11... | collective-permute-start | bytes 884744 | tf_op jit(solution)/shard_map/ppermute | solution.py:365
  66.5 17.7 %collective-permute-start.9 = (f32[16,64,128]{2,1,0:T(8,128)S(1)}, f32[16,64,128]{2,1,0:T(8,128)S(1)}, u32[]{:S(2)}, u32[]{:S(2)}) collective-permute-start(f32[16,64,128]{2,1,0:T(8,128)S(1)} %get-tuple-element.62), channel_id=1, source_target_pairs={{0,1},{1,0},{2,3},{3,2},{4,5},{5,4},{6,7},{7,6},{8,9},{9,8},{10,11... | collective-permute-start | bytes 1572872 | tf_op jit(solution)/shard_map/ppermute | solution.py:306
  67.0 17.2 %collective-permute-start.10 = (f32[16,64,128]{2,1,0:T(8,128)S(1)}, f32[16,64,128]{2,1,0:T(8,128)S(1)}, u32[]{:S(2)}, u32[]{:S(2)}) collective-permute-start(f32[16,64,128]{2,1,0:T(8,128)S(1)} %get-tuple-element.63), channel_id=1, source_target_pairs={{0,15},{1,2},{2,1},{3,4},{4,3},{5,6},{6,5},{7,8},{8,7},{9,10},{10,... | collective-permute-start | bytes 1572872 | tf_op jit(solution)/shard_map/ppermute | solution.py:306
  94.3 8.3 %collective-permute-start.11 = (f32[8,8,8,128]{3,2,1,0:T(8,128)S(1)}, f32[8,8,8,128]{3,2,1,0:T(8,128)S(1)}, u32[]{:S(2)}, u32[]{:S(2)}) collective-permute-start(f32[8,8,8,128]{3,2,1,0:T(8,128)S(1)} %all_to_all.11.own), channel_id=1, source_target_pairs={{0,1},{1,0},{2,3},{3,2},{4,5},{5,4},{6,7},{7,6},{8,9},{9,8},{10,11... | collective-permute-start | bytes 786440 | tf_op jit(solution)/shard_map/ppermute | solution.py:389
where the time goes:
time: 105 us; the launch traced here: 104 us
  Pallas kernels  41.4 us (39%)
  blocking collectives  25.6 us (24%)
  waiting for transfers between devices  19.5 us (19%)
  starting transfers between devices  12.3 us (12%)
  local copies, waits for them, and re-layouts  2.67 us (3%)
  between operations  1.43 us (1%)
  other arithmetic  1.2 us (1%)
    pallas_call x2, Pallas kernels, local(): pl.pallas_call(functools.partial(slot_kernel, first, size, len(given)), o...  31.8 us
    ppermute x4, waiting for transfers between devices, swapped(): lax.ppermute(to_cross, 'row', other_pair)  17.2 us
    all_to_all x1, blocking collectives, local(): parts = lax.all_to_all(both, 'row', 0, 0, axis_index_groups=cores)  15.4 us
    all_to_all x1, blocking collectives, local(): gathered = lax.all_to_all(spread, 'row', 0, 0, axis_index_groups=cores)  10.2 us
    pallas_call x1, Pallas kernels, added(): pl.pallas_call(functools.partial(add_kernel, pixels, groups), out_shape=j...  5.53 us
    ppermute x4, starting transfers between devices, swapped(): lax.ppermute(to_near, 'row', pair)  3.91 us
    ppermute x2, starting transfers between devices, shifted(): lax.ppermute(array, axis, [(i, (i + by) % peers) for i in range(peers)])  3.81 us
    ppermute x1, starting transfers between devices, local(): lax.ppermute(gathered, 'row', pair)  2.78 us
  transfers between devices with their start and end apart: 12, of which 2 were waited for; matrix products, arithmetic and copies ran while one was open for 1% of the time, Pallas kernels for 37%

commit v1 on v0

--- a/solution.py
+++ b/solution.py
@@ -88,6 +88,16 @@
     return lax.rem(offsets[0, 0] // rows, 2) == 0
 
 
+def pack_kernel(offsets, counts, measured, out):
+    slots, _, pixels = measured.shape
+    for slot in range(slots):
+        live = jnp.where(slot < counts[0], 1.0, 0.0).astype(F32)
+        out[slot] = measured[slot] * live
+        for entry in range(2):
+            line = jnp.full((1, pixels), offsets[slot, entry], jnp.int32).astype(F32)
+            out[slots, 2 * slot + entry : 2 * slot + entry + 1] = line
+
+
 def cut_kernel(pixels, chunks, own, far, tile, *outs):
     planes, rows, _ = tile.shape
     even = is_even(own, rows)
@@ -97,12 +107,6 @@
             strip = at * planes
             near[strip : strip + planes] = cut(tile, jnp.where(even, own[slot, 1], far[slot, 1]), pixels)
             cross[strip : strip + planes] = cut(tile, jnp.where(even, far[slot, 1], own[slot, 1]), pixels)
-        if first == 0:
-            for slot in range(own.shape[0]):
-                for entry in range(2):
-                    line = jnp.full((1, pixels), own[slot, entry], jnp.int32).astype(F32)
-                    near[near.shape[0] - 1, 2 * slot + entry : 2 * slot + entry + 1] = line
-                    cross[cross.shape[0] - 1, 2 * slot + entry : 2 * slot + entry + 1] = line
 
 
 def add_kernel(pixels, groups, own, middle, far, *refs):
@@ -153,8 +157,8 @@
     if first == 0:
         for slot in range(offsets.shape[0]):
             for entry in range(2):
-                line = pl.ds(2 * slot + entry, 1)
-                value = jnp.where(even, cross[cross.shape[0] - 1, line], near[near.shape[0] - 1, line])
+                line = 2 * slot + entry
+                value = target[target.shape[0] - 1, line : line + 1]
                 offsets[slot, entry] = jnp.max(value).astype(jnp.int32)
     total[...] = so_far[...]
     held = range(BATCH)
@@ -282,16 +286,22 @@
     other_pair = [(i, (i - 1) % peers if i % 2 == 0 else (i + 1) % peers) for i in range(peers)]
     far = shifted(offsets, "row", 2)
 
-    live = lax.broadcasted_iota(jnp.int32, (measured.shape[0], 1, 1), 0) < counts[0]
-    target = jnp.where(live, measured, 0.0)
+    target = pl.pallas_call(
+        pack_kernel,
+        out_shape=jax.ShapeDtypeStruct((measured.shape[0] + 1, pixels, pixels), F32),
+        in_specs=[in_smem()] * 2 + [in_vmem()],
+        out_specs=in_vmem(),
+        compiler_params=params,
+        cost_estimate=pl.CostEstimate(flops=0, bytes_accessed=1 << 20, transcendentals=0),
+    )(offsets, counts, measured)
     far, target = lax.optimization_barrier((far, target))
     target = shifted(target, "row", 1)
 
     def units(count):
         return jax.ShapeDtypeStruct((count, tile_rows, pixels), F32)
 
-    def strips(chunks):
-        shapes = [units(size * planes + (first == 0)) for first, size in chunks for _ in range(2)]
+    def strips(chunks, far):
+        shapes = [units(size * planes) for _, size in chunks for _ in range(2)]
         outs = pl.pallas_call(
             functools.partial(cut_kernel, pixels, chunks),
             out_shape=shapes,
@@ -306,7 +316,8 @@
         return lax.ppermute(to_near, "row", pair), lax.ppermute(to_cross, "row", other_pair)
 
     chunks = list(zip(starts, CHUNKS))
-    waiting = strips(chunks[:1]) + strips(chunks[1:])
+    far_later, target = lax.optimization_barrier((far, target))
+    waiting = strips(chunks[:1], far) + strips(chunks[1:], far_later)
     arrived = [swapped(*waiting[0])]
     if len(waiting) > 1:
         arrived[0], following = lax.optimization_barrier((arrived[0], waiting[1]))

time: 105 us -> 102 us (0.971)
  Pallas kernels: 41.4 us -> 34.9 us
  waiting for transfers between devices: 19.5 us -> 22.6 us
  other arithmetic: 1.2 us -> 0.04 us
    pallas_call x2, Pallas kernels: 31.8 us -> 24.7 us  [local(): pl.pallas_call(functools.partial(slot_kernel, first, size, len(given)), o...]
    ppermute x4, starting transfers between devices: 1.75 us -> 5.59 us  [swapped(): lax.ppermute(to_cross, 'row', other_pair)]
    ppermute x4, waiting for transfers between devices: 17.2 us -> 19.5 us  [swapped(): lax.ppermute(to_cross, 'row', other_pair)]
    ppermute x4, starting transfers between devices: 3.91 us -> 2.25 us  [swapped(): lax.ppermute(to_near, 'row', pair)]
    ppermute x2, starting transfers between devices: 3.81 us -> 2.53 us  [shifted(): lax.ppermute(array, axis, [(i, (i + by) % peers) for i in range(peers)])]
    select_n x1 -> x0, other arithmetic: 1.15 us -> none  [local(): target = jnp.where(live, measured, 0.0)]
    unnamed x9 -> x11, local copies, waits for them, and re-layouts: 2.39 us -> 3.4 us
  transfers between devices with their start and end apart: 12 -> 12, of which waited for: 2 -> 5; matrix products, arithmetic and copies ran while one was open for 1% -> 0% of each run, Pallas kernels for 37% -> 33%
where the time goes in v1:
time: 102 us; the launch traced here: 101 us
  Pallas kernels  34.9 us (34%)
  blocking collectives  25.3 us (25%)
  waiting for transfers between devices  22.6 us (22%)
  starting transfers between devices  13.2 us (13%)
  local copies, waits for them, and re-layouts  3.68 us (4%)
  between operations  1.41 us (1%)
    pallas_call x2, Pallas kernels, local(): pl.pallas_call(functools.partial(slot_kernel, first, size, len(given)), o...  24.7 us
    ppermute x4, waiting for transfers between devices, swapped(): lax.ppermute(to_cross, 'row', other_pair)  19.5 us
    all_to_all x1, blocking collectives, local(): parts = lax.all_to_all(both, 'row', 0, 0, axis_index_groups=cores)  14.9 us
    all_to_all x1, blocking collectives, local(): gathered = lax.all_to_all(spread, 'row', 0, 0, axis_index_groups=cores)  10.4 us
    ppermute x4, starting transfers between devices, swapped(): lax.ppermute(to_cross, 'row', other_pair)  5.59 us
    pallas_call x1, Pallas kernels, added(): pl.pallas_call(functools.partial(add_kernel, pixels, groups), out_shape=j...  5.53 us
    unnamed x11, local copies, waits for them, and re-layouts  3.4 us
    ppermute x2, waiting for transfers between devices, shifted(): lax.ppermute(array, axis, [(i, (i + by) % peers) for i in range(peers)])  3.06 us
  transfers between devices with their start and end apart: 12, of which 5 were waited for; matrix products, arithmetic and copies ran while one was open for 0% of the time, Pallas kernels for 33%

profile of v1, /device:TPU:1, one launch (start us, length us, event | category | flops | bytes accessed | tf_op | source)
XLA Modules:
  0.0 101.0 jit_solution(13559232909790363130)
XLA Ops:
  0.6 0.8 copy.15.offsets.own.own_offsets
  1.4 2.1 %collective-permute-start = (s32[8,2]{1,0:T(8,128)S(1)}, s32[8,2]{1,0:T(8,128)S(1)}, u32[]{:S(2)}, u32[]{:S(2)}) collective-permute-start(s32[8,2]{1,0:T(8,128)S(1)} %copy.15.offsets.own.own_offsets), channel_id=1, source_target_pairs={{0,2},{1,3},{2,4},{3,5},{4,6},{5,7},{6,8},{7,9},{8,10},{9,11},{10,... | collective-permute-start | bytes 200 | tf_op jit(solution)/shard_map/ppermute | solution.py:20
  4.1 0.0 copy-start.1
  4.1 1.0 %copy-done.1 = f32[8,128,128]{2,1,0:T(8,128)S(1)} copy-done((f32[8,128,128]{2,1,0:T(8,128)S(1)}, f32[8,128,128]{2,1,0:T(8,128)}, u32[]{:S(2)}) %copy-start.1) | copy-done | bytes 524312
  5.1 0.0 copy-start.4
  5.2 0.6 shard_map.86
  5.8 1.7 %collective-permute-done.far = s32[8,2]{1,0:T(8,128)S(1)} collective-permute-done((s32[8,2]{1,0:T(8,128)S(1)}, s32[8,2]{1,0:T(8,128)S(1)}, u32[]{:S(2)}, u32[]{:S(2)}) %collective-permute-start) | collective-permute-done | bytes 96 | tf_op jit(solution)/shard_map/ppermute | solution.py:20
  7.5 0.5 collective-permute-start.3
  7.9 0.0 copy-start
  7.9 1.6 %copy-done = f32[2,2,64,2048]{3,2,1,0:T(8,128)S(1)} copy-done((f32[2,2,64,2048]{3,2,1,0:T(8,128)S(1)}, f32[2,2,64,2048]{3,2,1,0:T(8,128)}, u32[]{:S(2)}) %copy-start) | copy-done | bytes 2097176
  9.5 1.3 %shard_map.87 = (f32[16,64,128]{2,1,0:T(8,128)S(1)}, f32[16,64,128]{2,1,0:T(8,128)S(1)}) custom-call(s32[8,2]{1,0:T(8,128)S(1)} %copy.15.offsets.own.own_offsets, s32[8,2]{1,0:T(8,128)S(1)} %collective-permute-done.far, f32[4,64,2048]{2,1,0:T(8,128)S(1)} %bitcast.9), custom_call_target="tpu_custom_call" | custom-call | bytes 4194304 | tf_op jit(solution)/shard_map/pallas_call | solution.py:305
  10.8 0.0 copy-start.2
  10.8 0.0 copy-start.3
  10.9 1.2 %collective-permute-start.1 = (f32[16,64,128]{2,1,0:T(8,128)S(1)}, f32[16,64,128]{2,1,0:T(8,128)S(1)}, u32[]{:S(2)}, u32[]{:S(2)}) collective-permute-start(f32[16,64,128]{2,1,0:T(8,128)S(1)} %get-tuple-element.43), channel_id=1, source_target_pairs={{0,1},{1,0},{2,3},{3,2},{4,5},{5,4},{6,7},{7,6},{8,9},{9,8},{10,11... | collective-permute-start | bytes 1572872 | tf_op jit(solution)/shard_map/ppermute | solution.py:316
  12.0 1.1 %collective-permute-start.2 = (f32[16,64,128]{2,1,0:T(8,128)S(1)}, f32[16,64,128]{2,1,0:T(8,128)S(1)}, u32[]{:S(2)}, u32[]{:S(2)}) collective-permute-start(f32[16,64,128]{2,1,0:T(8,128)S(1)} %get-tuple-element.44), channel_id=1, source_target_pairs={{0,15},{1,2},{2,1},{3,4},{4,3},{5,6},{6,5},{7,8},{8,7},{9,10},{10,... | collective-permute-start | bytes 1572872 | tf_op jit(solution)/shard_map/ppermute | solution.py:316
  13.1 0.0 copy-done.4
  13.1 0.2 cosine_bitcast_fusion
  13.4 1.4 %collective-permute-done.3.refs_3_.refs_4_ = f32[9,128,128]{2,1,0:T(8,128)S(1)} collective-permute-done((f32[9,128,128]{2,1,0:T(8,128)S(1)}, f32[9,128,128]{2,1,0:T(8,128)S(1)}, u32[]{:S(2)}, u32[]{:S(2)}) %collective-permute-start.3) | collective-permute-done | bytes 589856 | tf_op jit(solution)/shard_map/ppermute | solution.py:20
  14.8 1.3 %shard_map.88 = (f32[16,64,128]{2,1,0:T(8,128)S(1)}, f32[16,64,128]{2,1,0:T(8,128)S(1)}) custom-call(s32[8,2]{1,0:T(8,128)S(1)} %copy.15.offsets.own.own_offsets, s32[8,2]{1,0:T(8,128)S(1)} %collective-permute-done.far, f32[4,64,2048]{2,1,0:T(8,128)S(1)} %bitcast.10), custom_call_target="tpu_custom_call" | custom-call | bytes 4194304 | tf_op jit(solution)/shard_map/pallas_call | solution.py:305
  16.1 0.0 collective-permute-done.1.refs_1_
  16.1 15.5 %collective-permute-done.2.refs_2_ = f32[16,64,128]{2,1,0:T(8,128)S(1)} collective-permute-done((f32[16,64,128]{2,1,0:T(8,128)S(1)}, f32[16,64,128]{2,1,0:T(8,128)S(1)}, u32[]{:S(2)}, u32[]{:S(2)}) %collective-permute-start.2) | collective-permute-done | bytes 524320 | tf_op jit(solution)/shard_map/ppermute | solution.py:316
  31.6 0.0 collective-permute-start.4
  31.6 0.0 collective-permute-start.5
  31.6 0.0 copy-done.2
  31.6 0.0 copy-done.3
  31.7 15.5 %shard_map.89 = (f32[16,64,128]{2,1,0:T(8,128)S(1)}, f32[16,64,128]{2,1,0:T(8,128)S(1)}, f32[16,64,128]{2,1,0:T(8,128)S(1)}, f32[9,128,128]{2,1,0:T(8,128)S(1)}, s32[8,2]{1,0:T(8,128)S(1)}) custom-call(s32[8,2]{1,0:T(8,128)S(1)} %copy.15.offsets.own.own_offsets, f32[4,64,2048]{2,1,0:T(8,128)} %bitcast.7, f32[16,64,128]{2,1,0:T(8,128)S(1)} %collective-permute-done.1.refs_1_, ...), custom_call_target="tpu_custom_call" | custom-call | flops 9663676416 | bytes 8388608 | tf_op jit(solution)/shard_map/pallas_call | solution.py:339
  47.1 0.6 collective-permute-start.6
  47.7 1.3 %collective-permute-start.7 = (f32[16,64,128]{2,1,0:T(8,128)S(1)}, f32[16,64,128]{2,1,0:T(8,128)S(1)}, u32[]{:S(2)}, u32[]{:S(2)}) collective-permute-start(f32[16,64,128]{2,1,0:T(8,128)S(1)} %get-tuple-element.59), channel_id=1, source_target_pairs={{0,15},{1,2},{2,1},{3,4},{4,3},{5,6},{6,5},{7,8},{8,7},{9,10},{10,... | collective-permute-start | bytes 1572872 | tf_op jit(solution)/shard_map/ppermute | solution.py:316
  49.0 0.0 collective-permute-done.4.refs_2_
  49.0 0.0 collective-permute-done.5.refs_3_
  49.0 9.2 %shard_map.90 = (f32[16,64,128]{2,1,0:T(8,128)S(1)}, f32[16,64,128]{2,1,0:T(8,128)S(1)}, f32[16,64,128]{2,1,0:T(8,128)S(1)}, f32[9,128,128]{2,1,0:T(8,128)}, f32...) custom-call(s32[8,2]{1,0:T(8,128)S(1)} %copy.15.offsets.own.own_offsets, ...), custom_call_target="tpu_custom_call" | custom-call | flops 9663676416 | bytes 8388608 | tf_op jit(solution)/shard_map/pallas_call | solution.py:339
  58.2 0.0 collective-permute-done.6.refs_2_
  58.2 3.7 %collective-permute-done.7.refs_3_ = f32[16,64,128]{2,1,0:T(8,128)S(1)} collective-permute-done((f32[16,64,128]{2,1,0:T(8,128)S(1)}, f32[16,64,128]{2,1,0:T(8,128)S(1)}, u32[]{:S(2)}, u32[]{:S(2)}) %collective-permute-start.7) | collective-permute-done | bytes 524320 | tf_op jit(solution)/shard_map/ppermute | solution.py:316
  61.9 0.0 collective-permute-start.8
  61.9 0.5 collective-permute-start.9
  62.5 3.2 %collective-permute-start.10 = (f32[16,64,128]{2,1,0:T(8,128)S(1)}, f32[16,64,128]{2,1,0:T(8,128)S(1)}, u32[]{:S(2)}, u32[]{:S(2)}) collective-permute-start(f32[16,64,128]{2,1,0:T(8,128)S(1)} %get-tuple-element.67), channel_id=1, source_target_pairs={{0,15},{1,2},{2,1},{3,4},{4,3},{5,6},{6,5},{7,8},{8,7},{9,10},{10,... | collective-permute-start | bytes 1572872 | tf_op jit(solution)/shard_map/ppermute | solution.py:316
  65.6 0.0 collective-permute-done.8
  65.6 14.9 %all_to_all.10.parts = f32[8,9,8,128]{3,2,1,0:T(8,128)S(1)} all-to-all(f32[8,9,8,128]{3,2,1,0:T(8,128)S(1)} %add.3), channel_id=1, replica_groups={{0,2,4,6,8,10,12,14},{1,3,5,7,9,11,13,15},{16,18,20,22,24,26,28,30},{17..., dimensions={0} | all-to-all | bytes 589824 | tf_op jit(solution)/shard_map/all_to_all | solution.py:377
  80.6 0.0 collective-permute-done.9.refs_4_
  80.6 0.3 collective-permute-done.10.refs_5_
  80.9 10.4 %all_to_all.11.own = f32[8,8,8,128]{3,2,1,0:T(8,128)S(1)} all-to-all(f32[8,8,8,128]{3,2,1,0:T(8,128)S(1)} %shard_map.91), channel_id=1, replica_groups={{0,2,4,6,8,10,12,14},{1,3,5,7,9,11,13,15},{16,18,20,22,24,26,28,30},{17..., dimensions={0} | all-to-all | bytes 524288 | tf_op jit(solution)/shard_map/all_to_all | solution.py:388
  91.3 2.8 %collective-permute-start.11 = (f32[8,8,8,128]{3,2,1,0:T(8,128)S(1)}, f32[8,8,8,128]{3,2,1,0:T(8,128)S(1)}, u32[]{:S(2)}, u32[]{:S(2)}) collective-permute-start(f32[8,8,8,128]{3,2,1,0:T(8,128)S(1)} %all_to_all.11.own), channel_id=1, source_target_pairs={{0,1},{1,0},{2,3},{3,2},{4,5},{5,4},{6,7},{7,6},{8,9},{9,8},{10,11... | collective-permute-start | bytes 786440 | tf_op jit(solution)/shard_map/ppermute | solution.py:400
  94.0 5.5 %shard_map.92 = f32[4,64,2048]{2,1,0:T(8,128)} custom-call(s32[8,2]{1,0:T(8,128)S(1)} %copy.15.offsets.own.own_offsets, s32[8,2]{1,0:T(8,128)S(1)} %get-tuple-element.52.refs_0_.middle, s32[8,2]{1,0:T(8,128)S(1)} %collective-permute-done.far, f32[16,64,128]{2,1,0:T(8,128)S(1)} %get-tuple-element.75.refs_0_, f32[16,64,128]{2,1,0:T(8,128)S(1)} %get-tuple-element.76.refs_1_, ...), custom_call_target="tpu_custom_call" | custom-call | bytes 5242880 | tf_op jit(solution)/shard_map/pallas_call | solution.py:364
  99.6 0.0 collective-permute-done.11.other
  99.6 1.5 %shard_map.93 = f32[8,128,128]{2,1,0:T(8,128)} custom-call(s32[8,2]{1,0:T(8,128)S(1)} %copy.15.offsets.own.own_offsets, f32[8,8,8,128]{3,2,1,0:T(8,128)S(1)} %all_to_all.11.own, f32[8,8,8,128]{3,2,1,0:T(8,128)S(1)} %collective-permute-done.11.other), custom_call_target="tpu_custom_call" | custom-call | tf_op jit(solution)/shard_map/pallas_call | solution.py:394
  (4 shorter events, 0.1 us)
Async XLA Ops:
  1.4 6.1 %collective-permute-start = (s32[8,2]{1,0:T(8,128)S(1)}, s32[8,2]{1,0:T(8,128)S(1)}, u32[]{:S(2)}, u32[]{:S(2)}) collective-permute-start(s32[8,2]{1,0:T(8,128)S(1)} %copy.15.offsets.own.own_offsets), channel_id=1, source_target_pairs={{0,2},{1,3},{2,4},{3,5},{4,6},{5,7},{6,8},{7,9},{8,10},{9,11},{10,... | collective-permute-start | bytes 200 | tf_op jit(solution)/shard_map/ppermute | solution.py:20
  4.1 1.0 %copy-start.1 = (f32[8,128,128]{2,1,0:T(8,128)S(1)}, f32[8,128,128]{2,1,0:T(8,128)}, u32[]{:S(2)}) copy-start(f32[8,128,128]{2,1,0:T(8,128)} %measured.1) | copy-start | bytes 1572868
  5.1 8.0 %copy-start.4 = (f32[128,128]{1,0:T(8,128)S(1)}, f32[128,128]{1,0:T(8,128)}, u32[]{:S(2)}) copy-start(f32[128,128]{1,0:T(8,128)} %param.9) | copy-start | bytes 196612
  7.5 7.3 %collective-permute-start.3 = (f32[9,128,128]{2,1,0:T(8,128)S(1)}, f32[9,128,128]{2,1,0:T(8,128)S(1)}, u32[]{:S(2)}, u32[]{:S(2)}) collective-permute-start(f32[9,128,128]{2,1,0:T(8,128)S(1)} %shard_map.86), channel_id=1, source_target_pairs={{0,1},{1,2},{2,3},{3,4},{4,5},{5,6},{6,7},{7,8},{8,9},{9,10},{10,1... | collective-permute-start | bytes 1769480 | tf_op jit(solution)/shard_map/ppermute | solution.py:20
  7.9 1.6 %copy-start = (f32[2,2,64,2048]{3,2,1,0:T(8,128)S(1)}, f32[2,2,64,2048]{3,2,1,0:T(8,128)}, u32[]{:S(2)}) copy-start(f32[2,2,64,2048]{3,2,1,0:T(8,128)} %param.7) | copy-start | bytes 6291460
  10.8 20.8 %copy-start.2 = (f32[4,2,128,128]{3,2,1,0:T(8,128)S(1)}, f32[4,2,128,128]{3,2,1,0:T(8,128)}, u32[]{:S(2)}) copy-start(f32[4,2,128,128]{3,2,1,0:T(8,128)} %refs_5_.1) | copy-start | bytes 1572868
  10.8 20.8 %copy-start.3 = (bf16[4,256,256]{2,1,0:T(8,128)(2,1)S(1)}, bf16[4,256,256]{2,1,0:T(8,128)(2,1)}, u32[]{:S(2)}) copy-start(bf16[4,256,256]{2,1,0:T(8,128)(2,1)} %constant.4.clone.refs_6_.refs_7_) | copy-start | bytes 1572868
  10.9 5.2 %collective-permute-start.1 = (f32[16,64,128]{2,1,0:T(8,128)S(1)}, f32[16,64,128]{2,1,0:T(8,128)S(1)}, u32[]{:S(2)}, u32[]{:S(2)}) collective-permute-start(f32[16,64,128]{2,1,0:T(8,128)S(1)} %get-tuple-element.43), channel_id=1, source_target_pairs={{0,1},{1,0},{2,3},{3,2},{4,5},{5,4},{6,7},{7,6},{8,9},{9,8},{10,11... | collective-permute-start | bytes 1572872 | tf_op jit(solution)/shard_map/ppermute | solution.py:316
  12.0 19.6 %collective-permute-start.2 = (f32[16,64,128]{2,1,0:T(8,128)S(1)}, f32[16,64,128]{2,1,0:T(8,128)S(1)}, u32[]{:S(2)}, u32[]{:S(2)}) collective-permute-start(f32[16,64,128]{2,1,0:T(8,128)S(1)} %get-tuple-element.44), channel_id=1, source_target_pairs={{0,15},{1,2},{2,1},{3,4},{4,3},{5,6},{6,5},{7,8},{8,7},{9,10},{10,... | collective-permute-start | bytes 1572872 | tf_op jit(solution)/shard_map/ppermute | solution.py:316
  31.6 17.4 %collective-permute-start.4 = (f32[16,64,128]{2,1,0:T(8,128)S(1)}, f32[16,64,128]{2,1,0:T(8,128)S(1)}, u32[]{:S(2)}, u32[]{:S(2)}) collective-permute-start(f32[16,64,128]{2,1,0:T(8,128)S(1)} %get-tuple-element.53), channel_id=1, source_target_pairs={{0,1},{1,0},{2,3},{3,2},{4,5},{5,4},{6,7},{7,6},{8,9},{9,8},{10,11... | collective-permute-start | bytes 1572872 | tf_op jit(solution)/shard_map/ppermute | solution.py:316
  31.6 17.4 %collective-permute-start.5 = (f32[16,64,128]{2,1,0:T(8,128)S(1)}, f32[16,64,128]{2,1,0:T(8,128)S(1)}, u32[]{:S(2)}, u32[]{:S(2)}) collective-permute-start(f32[16,64,128]{2,1,0:T(8,128)S(1)} %get-tuple-element.54), channel_id=1, source_target_pairs={{0,15},{1,2},{2,1},{3,4},{4,3},{5,6},{6,5},{7,8},{8,7},{9,10},{10,... | collective-permute-start | bytes 1572872 | tf_op jit(solution)/shard_map/ppermute | solution.py:316
  47.1 11.1 %collective-permute-start.6 = (f32[16,64,128]{2,1,0:T(8,128)S(1)}, f32[16,64,128]{2,1,0:T(8,128)S(1)}, u32[]{:S(2)}, u32[]{:S(2)}) collective-permute-start(f32[16,64,128]{2,1,0:T(8,128)S(1)} %get-tuple-element.58), channel_id=1, source_target_pairs={{0,1},{1,0},{2,3},{3,2},{4,5},{5,4},{6,7},{7,6},{8,9},{9,8},{10,11... | collective-permute-start | bytes 1572872 | tf_op jit(solution)/shard_map/ppermute | solution.py:316
  47.7 14.2 %collective-permute-start.7 = (f32[16,64,128]{2,1,0:T(8,128)S(1)}, f32[16,64,128]{2,1,0:T(8,128)S(1)}, u32[]{:S(2)}, u32[]{:S(2)}) collective-permute-start(f32[16,64,128]{2,1,0:T(8,128)S(1)} %get-tuple-element.59), channel_id=1, source_target_pairs={{0,15},{1,2},{2,1},{3,4},{4,3},{5,6},{6,5},{7,8},{8,7},{9,10},{10,... | collective-permute-start | bytes 1572872 | tf_op jit(solution)/shard_map/ppermute | solution.py:316
  61.9 3.7 %collective-permute-start.8 = (f32[8,9,8,128]{3,2,1,0:T(8,128)S(1)}, f32[8,9,8,128]{3,2,1,0:T(8,128)S(1)}, u32[]{:S(2)}, u32[]{:S(2)}) collective-permute-start(f32[8,9,8,128]{3,2,1,0:T(8,128)S(1)} %get-tuple-element.61), channel_id=1, source_target_pairs={{0,1},{1,0},{2,3},{3,2},{4,5},{5,4},{6,7},{7,6},{8,9},{9,8},{10,11... | collective-permute-start | bytes 884744 | tf_op jit(solution)/shard_map/ppermute | solution.py:376
  61.9 18.6 %collective-permute-start.9 = (f32[16,64,128]{2,1,0:T(8,128)S(1)}, f32[16,64,128]{2,1,0:T(8,128)S(1)}, u32[]{:S(2)}, u32[]{:S(2)}) collective-permute-start(f32[16,64,128]{2,1,0:T(8,128)S(1)} %get-tuple-element.66), channel_id=1, source_target_pairs={{0,1},{1,0},{2,3},{3,2},{4,5},{5,4},{6,7},{7,6},{8,9},{9,8},{10,11... | collective-permute-start | bytes 1572872 | tf_op jit(solution)/shard_map/ppermute | solution.py:316
  62.5 18.4 %collective-permute-start.10 = (f32[16,64,128]{2,1,0:T(8,128)S(1)}, f32[16,64,128]{2,1,0:T(8,128)S(1)}, u32[]{:S(2)}, u32[]{:S(2)}) collective-permute-start(f32[16,64,128]{2,1,0:T(8,128)S(1)} %get-tuple-element.67), channel_id=1, source_target_pairs={{0,15},{1,2},{2,1},{3,4},{4,3},{5,6},{6,5},{7,8},{8,7},{9,10},{10,... | collective-permute-start | bytes 1572872 | tf_op jit(solution)/shard_map/ppermute | solution.py:316
  91.3 8.3 %collective-permute-start.11 = (f32[8,8,8,128]{3,2,1,0:T(8,128)S(1)}, f32[8,8,8,128]{3,2,1,0:T(8,128)S(1)}, u32[]{:S(2)}, u32[]{:S(2)}) collective-permute-start(f32[8,8,8,128]{3,2,1,0:T(8,128)S(1)} %all_to_all.11.own), channel_id=1, source_target_pairs={{0,1},{1,0},{2,3},{3,2},{4,5},{5,4},{6,7},{7,6},{8,9},{9,8},{10,11... | collective-permute-start | bytes 786440 | tf_op jit(solution)/shard_map/ppermute | solution.py:400

commit v2 on v1

--- a/solution.py
+++ b/solution.py
@@ -9,7 +9,7 @@
 from jax.sharding import PartitionSpec as P
 
 CHUNKS = (4, 4)
-BATCH = 2
+BATCH = 4
 VMEM_LIMIT = 48 * 1024 * 1024
 F32 = jnp.float32
 BF16 = jnp.bfloat16
@@ -84,18 +84,25 @@
     return turned[:, :pixels].reshape(-1, rows, pixels)
 
 
+def rows_of(index, share):
+    return pl.ds(pl.multiple_of(index * share, share), share)
+
+
 def is_even(offsets, rows):
     return lax.rem(offsets[0, 0] // rows, 2) == 0
 
 
-def pack_kernel(offsets, counts, measured, out):
+def pack_kernel(chunks, offsets, counts, measured, *outs):
     slots, _, pixels = measured.shape
+    for (first, size), out in zip(chunks, outs):
+        for at in range(size):
+            live = jnp.where(first + at < counts[0], 1.0, 0.0).astype(F32)
+            out[at] = measured[first + at] * live
+    first_out = outs[0]
     for slot in range(slots):
-        live = jnp.where(slot < counts[0], 1.0, 0.0).astype(F32)
-        out[slot] = measured[slot] * live
         for entry in range(2):
             line = jnp.full((1, pixels), offsets[slot, entry], jnp.int32).astype(F32)
-            out[slots, 2 * slot + entry : 2 * slot + entry + 1] = line
+            first_out[chunks[0][1], 2 * slot + entry : 2 * slot + entry + 1] = line
 
 
 def cut_kernel(pixels, chunks, own, far, tile, *outs):
@@ -117,7 +124,8 @@
     lane = lax.broadcasted_iota(jnp.int32, (1, 1, pixels), 2)
     for (kind, first, size, unit), strips in zip(groups, parts):
 
-        def add(at, carry, kind=kind, first=first, unit=unit, strips=strips):
+        turned = []
+        for at in range(size):
             slot = first + at
             if kind == "mid":
                 column = middle[slot, 1]
@@ -126,15 +134,13 @@
             else:
                 column = jnp.where(even, far[slot, 1], own[slot, 1])
             base, shift = place(column, out.shape[-1], pixels)
-            part = strips[pl.ds(unit + at * planes, planes)]
-            turned = pltpu.roll(part.reshape(-1, pixels), lax.rem(shift, pixels), 1).reshape(part.shape)
-            out[:, :, pl.ds(base, pixels)] += jnp.where(lane >= shift, turned, 0.0)
-            out[:, :, pl.ds(pl.multiple_of(base + pixels, pixels), pixels)] += jnp.where(
-                lane < shift, turned, 0.0
-            )
-            return carry
-
-        lax.fori_loop(0, size, add, 0)
+            part = strips[unit + at * planes : unit + (at + 1) * planes].reshape(-1, pixels)
+            part = pltpu.roll(part, lax.rem(shift, pixels), 1).reshape(planes, rows, pixels)
+            turned.append((base, shift, part))
+        for base, shift, part in turned:
+            out[:, :, pl.ds(base, pixels)] += jnp.where(lane >= shift, part, 0.0)
+            beside = pl.ds(pl.multiple_of(base + pixels, pixels), pixels)
+            out[:, :, beside] += jnp.where(lane < shift, part, 0.0)
 
 
 def slot_kernel(
@@ -164,7 +170,7 @@
     held = range(BATCH)
 
     def is_live(at):
-        return jnp.max(target[first + at, :8]) > 0.0
+        return jnp.max(target[at, :8]) > 0.0
 
     def leave(slots):
         for at in slots:
@@ -199,7 +205,7 @@
                 wave = groups[s][m]
                 far[s, m, 0], far[s, m, 1] = wave
                 intensity = intensity + wave[0] * wave[0] + wave[1] * wave[1]
-            misfit = 2.0 * live[s] * (intensity - target[first + at])
+            misfit = 2.0 * live[s] * (intensity - target[at])
             groups[s] = [(misfit * far[s, m, 0], misfit * far[s, m, 1]) for m in all_modes]
         groups = transform(tables, True, groups)
         for s in held:
@@ -244,8 +250,8 @@
         core = jnp.where(even, 0, 1)
         for chip in range(chips):
             for plane in range(2 * modes + 1):
-                own[chip, plane] = total[plane, pl.ds((2 * chip + core) * share, share)]
-                other[chip, plane] = total[plane, pl.ds((2 * chip + 1 - core) * share, share)]
+                own[chip, plane] = total[plane, rows_of(2 * chip + core, share)]
+                other[chip, plane] = total[plane, rows_of(2 * chip + 1 - core, share)]
 
 
 def step_kernel(parts, out):
@@ -261,8 +267,8 @@
     chips, _, share, _ = own.shape
     core = jnp.where(is_even(offsets, rows), 0, 1)
     for chip in range(chips):
-        out[:, pl.ds((2 * chip + core) * share, share)] = own[chip]
-        out[:, pl.ds((2 * chip + 1 - core) * share, share)] = other[chip]
+        out[:, rows_of(2 * chip + core, share)] = own[chip]
+        out[:, rows_of(2 * chip + 1 - core, share)] = other[chip]
 
 
 def in_smem():
@@ -286,16 +292,16 @@
     other_pair = [(i, (i - 1) % peers if i % 2 == 0 else (i + 1) % peers) for i in range(peers)]
     far = shifted(offsets, "row", 2)
 
-    target = pl.pallas_call(
-        pack_kernel,
-        out_shape=jax.ShapeDtypeStruct((measured.shape[0] + 1, pixels, pixels), F32),
+    chunks = list(zip(starts, CHUNKS))
+    packed = pl.pallas_call(
+        functools.partial(pack_kernel, chunks),
+        out_shape=[jax.ShapeDtypeStruct((size + (first == 0), pixels, pixels), F32) for first, size in chunks],
         in_specs=[in_smem()] * 2 + [in_vmem()],
-        out_specs=in_vmem(),
+        out_specs=[in_vmem()] * len(chunks),
         compiler_params=params,
         cost_estimate=pl.CostEstimate(flops=0, bytes_accessed=1 << 20, transcendentals=0),
     )(offsets, counts, measured)
-    far, target = lax.optimization_barrier((far, target))
-    target = shifted(target, "row", 1)
+    far, packed = lax.optimization_barrier((far, packed))
 
     def units(count):
         return jax.ShapeDtypeStruct((count, tile_rows, pixels), F32)
@@ -315,13 +321,13 @@
     def swapped(to_near, to_cross):
         return lax.ppermute(to_near, "row", pair), lax.ppermute(to_cross, "row", other_pair)
 
-    chunks = list(zip(starts, CHUNKS))
-    far_later, target = lax.optimization_barrier((far, target))
-    waiting = strips(chunks[:1], far) + strips(chunks[1:], far_later)
+    waiting = strips(chunks[:1], far) + strips(chunks[1:], far)
     arrived = [swapped(*waiting[0])]
+    targets = [shifted(packed[0], "row", 1)]
     if len(waiting) > 1:
-        arrived[0], following = lax.optimization_barrier((arrived[0], waiting[1]))
+        arrived[0], following, packed = lax.optimization_barrier((arrived[0], waiting[1], packed))
         arrived.append(swapped(*following))
+        targets += [shifted(part, "row", 1) for part in packed[1:]]
     prop = jnp.stack([jnp.cos(propagator_phase), jnp.sin(propagator_phase)])
     tables = jnp.asarray(fourier_tables(pixels))
 
@@ -348,7 +354,7 @@
             cost_estimate=pl.CostEstimate(
                 flops=size * 6 * modes * 3 * 16 * pixels**3, bytes_accessed=8 << 20, transcendentals=0
             ),
-        )(*places, tile, *arrived[index], target, probe_modes, prop, tables, total, *given)
+        )(*places, tile, *arrived[index], targets[index], probe_modes, prop, tables, total, *given)
         if index == 0:
             middle = shares.pop()
             places.append(middle)

time: 102 us -> 102 us (level)
  waiting for transfers between devices: 22.6 us -> 19.4 us
  Pallas kernels: 34.9 us -> 37.5 us
  blocking collectives: 25.3 us -> 26.5 us
    pallas_call x2, Pallas kernels: 24.7 us -> 29 us  [local(): pl.pallas_call(functools.partial(slot_kernel, first, size, len(given)), o...]
    ppermute x4, starting transfers between devices: 5.59 us -> 1.73 us  [swapped(): lax.ppermute(to_cross, 'row', other_pair)]
    ppermute x4, waiting for transfers between devices: 19.5 us -> 17.7 us  [swapped(): lax.ppermute(to_cross, 'row', other_pair)]
    pallas_call x1, Pallas kernels: 5.53 us -> 3.78 us  [added(): pl.pallas_call(functools.partial(add_kernel, pixels, groups), out_shape=j...]
    ppermute x4, starting transfers between devices: 2.25 us -> 3.93 us  [swapped(): lax.ppermute(to_near, 'row', pair)]
    ppermute x2 -> x3, waiting for transfers between devices: 3.06 us -> 1.69 us  [shifted(): lax.ppermute(array, axis, [(i, (i + by) % peers) for i in range(peers)])]
    ppermute x2 -> x3, starting transfers between devices: 2.53 us -> 3.81 us  [shifted(): lax.ppermute(array, axis, [(i, (i + by) % peers) for i in range(peers)])]
  transfers between devices with their start and end apart: 12 -> 13, of which waited for: 5 -> 3; matrix products, arithmetic and copies ran while one was open for 0% -> 0% of each run, Pallas kernels for 33% -> 35%
where the time goes in v2:
time: 102 us; the launch traced here: 101 us
  Pallas kernels  37.5 us (37%)
  blocking collectives  26.5 us (26%)
  waiting for transfers between devices  19.4 us (19%)
  starting transfers between devices  12.3 us (12%)
  local copies, waits for them, and re-layouts  3.68 us (4%)
  between operations  1.42 us (1%)
    pallas_call x2, Pallas kernels, local(): pl.pallas_call(functools.partial(slot_kernel, first, size, len(given)), o...  29 us
    ppermute x4, waiting for transfers between devices, swapped(): lax.ppermute(to_cross, 'row', other_pair)  17.7 us
    all_to_all x1, blocking collectives, local(): parts = lax.all_to_all(both, 'row', 0, 0, axis_index_groups=cores)  15.6 us
    all_to_all x1, blocking collectives, local(): gathered = lax.all_to_all(spread, 'row', 0, 0, axis_index_groups=cores)  10.9 us
    ppermute x4, starting transfers between devices, swapped(): lax.ppermute(to_near, 'row', pair)  3.93 us
    ppermute x3, starting transfers between devices, shifted(): lax.ppermute(array, axis, [(i, (i + by) % peers) for i in range(peers)])  3.81 us
    pallas_call x1, Pallas kernels, added(): pl.pallas_call(functools.partial(add_kernel, pixels, groups), out_shape=j...  3.78 us
    unnamed x11, local copies, waits for them, and re-layouts  3.4 us
  transfers between devices with their start and end apart: 13, of which 3 were waited for; matrix products, arithmetic and copies ran while one was open for 0% of the time, Pallas kernels for 35%

profile of v2, /device:TPU:1, one launch (start us, length us, event | category | flops | bytes accessed | tf_op | source)
XLA Modules:
  0.0 100.8 jit_solution(13426813241103011318)
XLA Ops:
  0.6 0.8 copy.15.offsets.own.own_offsets
  1.4 2.1 %collective-permute-start = (s32[8,2]{1,0:T(8,128)S(1)}, s32[8,2]{1,0:T(8,128)S(1)}, u32[]{:S(2)}, u32[]{:S(2)}) collective-permute-start(s32[8,2]{1,0:T(8,128)S(1)} %copy.15.offsets.own.own_offsets), channel_id=1, source_target_pairs={{0,2},{1,3},{2,4},{3,5},{4,6},{5,7},{6,8},{7,9},{8,10},{9,11},{10,... | collective-permute-start | bytes 200 | tf_op jit(solution)/shard_map/ppermute | solution.py:20
  4.1 0.0 copy-start.1
  4.1 1.0 %copy-done.1 = f32[8,128,128]{2,1,0:T(8,128)S(1)} copy-done((f32[8,128,128]{2,1,0:T(8,128)S(1)}, f32[8,128,128]{2,1,0:T(8,128)}, u32[]{:S(2)}) %copy-start.1) | copy-done | bytes 524312
  5.1 0.0 copy-start.4
  5.2 0.6 shard_map.86
  5.8 1.7 %collective-permute-done.far = s32[8,2]{1,0:T(8,128)S(1)} collective-permute-done((s32[8,2]{1,0:T(8,128)S(1)}, s32[8,2]{1,0:T(8,128)S(1)}, u32[]{:S(2)}, u32[]{:S(2)}) %collective-permute-start) | collective-permute-done | bytes 96 | tf_op jit(solution)/shard_map/ppermute | solution.py:20
  7.5 0.0 copy-start
  7.5 1.6 %copy-done = f32[2,2,64,2048]{3,2,1,0:T(8,128)S(1)} copy-done((f32[2,2,64,2048]{3,2,1,0:T(8,128)S(1)}, f32[2,2,64,2048]{3,2,1,0:T(8,128)}, u32[]{:S(2)}) %copy-start) | copy-done | bytes 2097176
  9.1 1.3 %shard_map.87 = (f32[16,64,128]{2,1,0:T(8,128)S(1)}, f32[16,64,128]{2,1,0:T(8,128)S(1)}) custom-call(s32[8,2]{1,0:T(8,128)S(1)} %copy.15.offsets.own.own_offsets, s32[8,2]{1,0:T(8,128)S(1)} %collective-permute-done.far, f32[4,64,2048]{2,1,0:T(8,128)S(1)} %bitcast.9), custom_call_target="tpu_custom_call" | custom-call | bytes 4194304 | tf_op jit(solution)/shard_map/pallas_call | solution.py:311
  10.4 0.0 copy-start.2
  10.4 0.0 copy-start.3
  10.4 1.6 %collective-permute-start.1 = (f32[16,64,128]{2,1,0:T(8,128)S(1)}, f32[16,64,128]{2,1,0:T(8,128)S(1)}, u32[]{:S(2)}, u32[]{:S(2)}) collective-permute-start(f32[16,64,128]{2,1,0:T(8,128)S(1)} %get-tuple-element.47), channel_id=1, source_target_pairs={{0,1},{1,0},{2,3},{3,2},{4,5},{5,4},{6,7},{7,6},{8,9},{9,8},{10,11... | collective-permute-start | bytes 1572872 | tf_op jit(solution)/shard_map/ppermute | solution.py:322
  12.0 0.0 collective-permute-start.2
  12.0 1.7 %collective-permute-start.3 = (f32[5,128,128]{2,1,0:T(8,128)S(1)}, f32[5,128,128]{2,1,0:T(8,128)S(1)}, u32[]{:S(2)}, u32[]{:S(2)}) collective-permute-start(f32[5,128,128]{2,1,0:T(8,128)S(1)} %get-tuple-element.51), channel_id=1, source_target_pairs={{0,1},{1,2},{2,3},{3,4},{4,5},{5,6},{6,7},{7,8},{8,9},{9,10},{10,1... | collective-permute-start | bytes 983048 | tf_op jit(solution)/shard_map/ppermute | solution.py:20
  13.8 0.0 copy-done.4
  13.8 0.2 cosine_bitcast_fusion
  14.0 1.3 %shard_map.88 = (f32[16,64,128]{2,1,0:T(8,128)S(1)}, f32[16,64,128]{2,1,0:T(8,128)S(1)}) custom-call(s32[8,2]{1,0:T(8,128)S(1)} %copy.15.offsets.own.own_offsets, s32[8,2]{1,0:T(8,128)S(1)} %collective-permute-done.far, f32[4,64,2048]{2,1,0:T(8,128)S(1)} %bitcast.10), custom_call_target="tpu_custom_call" | custom-call | bytes 4194304 | tf_op jit(solution)/shard_map/pallas_call | solution.py:311
  15.3 0.0 collective-permute-done.1.refs_1_
  15.3 17.2 %collective-permute-done.2.refs_2_ = f32[16,64,128]{2,1,0:T(8,128)S(1)} collective-permute-done((f32[16,64,128]{2,1,0:T(8,128)S(1)}, f32[16,64,128]{2,1,0:T(8,128)S(1)}, u32[]{:S(2)}, u32[]{:S(2)}) %collective-permute-start.2) | collective-permute-done | bytes 524320 | tf_op jit(solution)/shard_map/ppermute | solution.py:322
  32.6 0.0 collective-permute-start.6
  32.6 0.5 collective-permute-start.4
  33.1 0.0 collective-permute-start.5
  33.1 0.0 collective-permute-done.3.refs_3_
  33.1 0.0 copy-done.2
  33.1 0.0 copy-done.3
  33.1 14.4 %shard_map.89 = (f32[16,64,128]{2,1,0:T(8,128)S(1)}, f32[16,64,128]{2,1,0:T(8,128)S(1)}, f32[16,64,128]{2,1,0:T(8,128)S(1)}, f32[9,128,128]{2,1,0:T(8,128)S(1)}, s32[8,2]{1,0:T(8,128)S(1)}) custom-call(s32[8,2]{1,0:T(8,128)S(1)} %copy.15.offsets.own.own_offsets, f32[4,64,2048]{2,1,0:T(8,128)} %bitcast.7, f32[16,64,128]{2,1,0:T(8,128)S(1)} %collective-permute-done.1.refs_1_, ...), custom_call_target="tpu_custom_call" | custom-call | flops 9663676416 | bytes 8388608 | tf_op jit(solution)/shard_map/pallas_call | solution.py:345
  47.5 1.3 %collective-permute-start.7 = (f32[16,64,128]{2,1,0:T(8,128)S(1)}, f32[16,64,128]{2,1,0:T(8,128)S(1)}, u32[]{:S(2)}, u32[]{:S(2)}) collective-permute-start(f32[16,64,128]{2,1,0:T(8,128)S(1)} %get-tuple-element.62), channel_id=1, source_target_pairs={{0,1},{1,0},{2,3},{3,2},{4,5},{5,4},{6,7},{7,6},{8,9},{9,8},{10,11... | collective-permute-start | bytes 1572872 | tf_op jit(solution)/shard_map/ppermute | solution.py:322
  48.8 0.6 collective-permute-start.8
  49.4 0.0 collective-permute-done.6.refs_4_
  49.4 0.0 collective-permute-done.4.refs_2_
  49.4 0.0 collective-permute-done.5.refs_3_
  49.5 14.7 %shard_map.90 = (f32[16,64,128]{2,1,0:T(8,128)S(1)}, f32[16,64,128]{2,1,0:T(8,128)S(1)}, f32[16,64,128]{2,1,0:T(8,128)S(1)}, f32[9,128,128]{2,1,0:T(8,128)}, f32...) custom-call(s32[8,2]{1,0:T(8,128)S(1)} %copy.15.offsets.own.own_offsets, ...), custom_call_target="tpu_custom_call" | custom-call | flops 9663676416 | bytes 8388608 | tf_op jit(solution)/shard_map/pallas_call | solution.py:345
  64.1 0.0 collective-permute-done.7.refs_2_
  64.1 0.0 collective-permute-done.8.refs_3_
  64.1 0.1 collective-permute-start.9
  64.2 0.5 collective-permute-start.10
  64.7 1.1 %collective-permute-start.11 = (f32[16,64,128]{2,1,0:T(8,128)S(1)}, f32[16,64,128]{2,1,0:T(8,128)S(1)}, u32[]{:S(2)}, u32[]{:S(2)}) collective-permute-start(f32[16,64,128]{2,1,0:T(8,128)S(1)} %get-tuple-element.71), channel_id=1, source_target_pairs={{0,15},{1,2},{2,1},{3,4},{4,3},{5,6},{6,5},{7,8},{8,7},{9,10},{10,... | collective-permute-start | bytes 1572872 | tf_op jit(solution)/shard_map/ppermute | solution.py:322
  65.8 0.0 collective-permute-done.9
  65.9 15.6 %all_to_all.10.parts = f32[8,9,8,128]{3,2,1,0:T(8,128)S(1)} all-to-all(f32[8,9,8,128]{3,2,1,0:T(8,128)S(1)} %add.3), channel_id=1, replica_groups={{0,2,4,6,8,10,12,14},{1,3,5,7,9,11,13,15},{16,18,20,22,24,26,28,30},{17..., dimensions={0} | all-to-all | bytes 589824 | tf_op jit(solution)/shard_map/all_to_all | solution.py:383
  81.5 0.0 collective-permute-done.10.refs_4_
  81.5 0.4 collective-permute-done.11.refs_5_
  81.9 10.9 %all_to_all.11.own = f32[8,8,8,128]{3,2,1,0:T(8,128)S(1)} all-to-all(f32[8,8,8,128]{3,2,1,0:T(8,128)S(1)} %shard_map.91), channel_id=1, replica_groups={{0,2,4,6,8,10,12,14},{1,3,5,7,9,11,13,15},{16,18,20,22,24,26,28,30},{17..., dimensions={0} | all-to-all | bytes 524288 | tf_op jit(solution)/shard_map/all_to_all | solution.py:394
  92.8 2.8 %collective-permute-start.12 = (f32[8,8,8,128]{3,2,1,0:T(8,128)S(1)}, f32[8,8,8,128]{3,2,1,0:T(8,128)S(1)}, u32[]{:S(2)}, u32[]{:S(2)}) collective-permute-start(f32[8,8,8,128]{3,2,1,0:T(8,128)S(1)} %all_to_all.11.own), channel_id=1, source_target_pairs={{0,1},{1,0},{2,3},{3,2},{4,5},{5,4},{6,7},{7,6},{8,9},{9,8},{10,11... | collective-permute-start | bytes 786440 | tf_op jit(solution)/shard_map/ppermute | solution.py:406
  95.6 3.8 %shard_map.92 = f32[4,64,2048]{2,1,0:T(8,128)} custom-call(s32[8,2]{1,0:T(8,128)S(1)} %copy.15.offsets.own.own_offsets, s32[8,2]{1,0:T(8,128)S(1)} %get-tuple-element.55.refs_0_.middle, s32[8,2]{1,0:T(8,128)S(1)} %collective-permute-done.far, f32[16,64,128]{2,1,0:T(8,128)S(1)} %get-tuple-element.79.refs_0_, f32[16,64,128]{2,1,0:T(8,128)S(1)} %get-tuple-element.80.refs_1_, ...), custom_call_target="tpu_custom_call" | custom-call | bytes 5242880 | tf_op jit(solution)/shard_map/pallas_call | solution.py:370
  99.4 0.0 collective-permute-done.12.other
  99.4 1.5 %shard_map.93 = f32[8,128,128]{2,1,0:T(8,128)} custom-call(s32[8,2]{1,0:T(8,128)S(1)} %copy.15.offsets.own.own_offsets, f32[8,8,8,128]{3,2,1,0:T(8,128)S(1)} %all_to_all.11.own, f32[8,8,8,128]{3,2,1,0:T(8,128)S(1)} %collective-permute-done.12.other), custom_call_target="tpu_custom_call" | custom-call | tf_op jit(solution)/shard_map/pallas_call | solution.py:400
  (4 shorter events, 0.1 us)
Async XLA Ops:
  1.4 6.1 %collective-permute-start = (s32[8,2]{1,0:T(8,128)S(1)}, s32[8,2]{1,0:T(8,128)S(1)}, u32[]{:S(2)}, u32[]{:S(2)}) collective-permute-start(s32[8,2]{1,0:T(8,128)S(1)} %copy.15.offsets.own.own_offsets), channel_id=1, source_target_pairs={{0,2},{1,3},{2,4},{3,5},{4,6},{5,7},{6,8},{7,9},{8,10},{9,11},{10,... | collective-permute-start | bytes 200 | tf_op jit(solution)/shard_map/ppermute | solution.py:20
  4.1 1.0 %copy-start.1 = (f32[8,128,128]{2,1,0:T(8,128)S(1)}, f32[8,128,128]{2,1,0:T(8,128)}, u32[]{:S(2)}) copy-start(f32[8,128,128]{2,1,0:T(8,128)} %measured.1) | copy-start | bytes 1572868
  5.1 8.6 %copy-start.4 = (f32[128,128]{1,0:T(8,128)S(1)}, f32[128,128]{1,0:T(8,128)}, u32[]{:S(2)}) copy-start(f32[128,128]{1,0:T(8,128)} %param.9) | copy-start | bytes 196612
  7.5 1.6 %copy-start = (f32[2,2,64,2048]{3,2,1,0:T(8,128)S(1)}, f32[2,2,64,2048]{3,2,1,0:T(8,128)}, u32[]{:S(2)}) copy-start(f32[2,2,64,2048]{3,2,1,0:T(8,128)} %param.7) | copy-start | bytes 6291460
  10.4 22.7 %copy-start.2 = (f32[4,2,128,128]{3,2,1,0:T(8,128)S(1)}, f32[4,2,128,128]{3,2,1,0:T(8,128)}, u32[]{:S(2)}) copy-start(f32[4,2,128,128]{3,2,1,0:T(8,128)} %refs_5_.1) | copy-start | bytes 1572868
  10.4 22.7 %copy-start.3 = (bf16[4,256,256]{2,1,0:T(8,128)(2,1)S(1)}, bf16[4,256,256]{2,1,0:T(8,128)(2,1)}, u32[]{:S(2)}) copy-start(bf16[4,256,256]{2,1,0:T(8,128)(2,1)} %constant.4.clone.refs_6_.refs_7_) | copy-start | bytes 1572868
  10.4 4.9 %collective-permute-start.1 = (f32[16,64,128]{2,1,0:T(8,128)S(1)}, f32[16,64,128]{2,1,0:T(8,128)S(1)}, u32[]{:S(2)}, u32[]{:S(2)}) collective-permute-start(f32[16,64,128]{2,1,0:T(8,128)S(1)} %get-tuple-element.47), channel_id=1, source_target_pairs={{0,1},{1,0},{2,3},{3,2},{4,5},{5,4},{6,7},{7,6},{8,9},{9,8},{10,11... | collective-permute-start | bytes 1572872 | tf_op jit(solution)/shard_map/ppermute | solution.py:322
  12.0 20.5 %collective-permute-start.2 = (f32[16,64,128]{2,1,0:T(8,128)S(1)}, f32[16,64,128]{2,1,0:T(8,128)S(1)}, u32[]{:S(2)}, u32[]{:S(2)}) collective-permute-start(f32[16,64,128]{2,1,0:T(8,128)S(1)} %get-tuple-element.48), channel_id=1, source_target_pairs={{0,15},{1,2},{2,1},{3,4},{4,3},{5,6},{6,5},{7,8},{8,7},{9,10},{10,... | collective-permute-start | bytes 1572872 | tf_op jit(solution)/shard_map/ppermute | solution.py:322
  12.0 21.1 %collective-permute-start.3 = (f32[5,128,128]{2,1,0:T(8,128)S(1)}, f32[5,128,128]{2,1,0:T(8,128)S(1)}, u32[]{:S(2)}, u32[]{:S(2)}) collective-permute-start(f32[5,128,128]{2,1,0:T(8,128)S(1)} %get-tuple-element.51), channel_id=1, source_target_pairs={{0,1},{1,2},{2,3},{3,4},{4,5},{5,6},{6,7},{7,8},{8,9},{9,10},{10,1... | collective-permute-start | bytes 983048 | tf_op jit(solution)/shard_map/ppermute | solution.py:20
  32.6 16.9 %collective-permute-start.6 = (f32[4,128,128]{2,1,0:T(8,128)S(1)}, f32[4,128,128]{2,1,0:T(8,128)S(1)}, u32[]{:S(2)}, u32[]{:S(2)}) collective-permute-start(f32[4,128,128]{2,1,0:T(8,128)S(1)} %get-tuple-element.58), channel_id=1, source_target_pairs={{0,1},{1,2},{2,3},{3,4},{4,5},{5,6},{6,7},{7,8},{8,9},{9,10},{10,1... | collective-permute-start | bytes 786440 | tf_op jit(solution)/shard_map/ppermute | solution.py:20
  32.6 16.9 %collective-permute-start.4 = (f32[16,64,128]{2,1,0:T(8,128)S(1)}, f32[16,64,128]{2,1,0:T(8,128)S(1)}, u32[]{:S(2)}, u32[]{:S(2)}) collective-permute-start(f32[16,64,128]{2,1,0:T(8,128)S(1)} %get-tuple-element.56), channel_id=1, source_target_pairs={{0,1},{1,0},{2,3},{3,2},{4,5},{5,4},{6,7},{7,6},{8,9},{9,8},{10,11... | collective-permute-start | bytes 1572872 | tf_op jit(solution)/shard_map/ppermute | solution.py:322
  33.1 16.4 %collective-permute-start.5 = (f32[16,64,128]{2,1,0:T(8,128)S(1)}, f32[16,64,128]{2,1,0:T(8,128)S(1)}, u32[]{:S(2)}, u32[]{:S(2)}) collective-permute-start(f32[16,64,128]{2,1,0:T(8,128)S(1)} %get-tuple-element.57), channel_id=1, source_target_pairs={{0,15},{1,2},{2,1},{3,4},{4,3},{5,6},{6,5},{7,8},{8,7},{9,10},{10,... | collective-permute-start | bytes 1572872 | tf_op jit(solution)/shard_map/ppermute | solution.py:322
  47.5 16.6 %collective-permute-start.7 = (f32[16,64,128]{2,1,0:T(8,128)S(1)}, f32[16,64,128]{2,1,0:T(8,128)S(1)}, u32[]{:S(2)}, u32[]{:S(2)}) collective-permute-start(f32[16,64,128]{2,1,0:T(8,128)S(1)} %get-tuple-element.62), channel_id=1, source_target_pairs={{0,1},{1,0},{2,3},{3,2},{4,5},{5,4},{6,7},{7,6},{8,9},{9,8},{10,11... | collective-permute-start | bytes 1572872 | tf_op jit(solution)/shard_map/ppermute | solution.py:322
  48.8 15.3 %collective-permute-start.8 = (f32[16,64,128]{2,1,0:T(8,128)S(1)}, f32[16,64,128]{2,1,0:T(8,128)S(1)}, u32[]{:S(2)}, u32[]{:S(2)}) collective-permute-start(f32[16,64,128]{2,1,0:T(8,128)S(1)} %get-tuple-element.63), channel_id=1, source_target_pairs={{0,15},{1,2},{2,1},{3,4},{4,3},{5,6},{6,5},{7,8},{8,7},{9,10},{10,... | collective-permute-start | bytes 1572872 | tf_op jit(solution)/shard_map/ppermute | solution.py:322
  64.1 1.7 %collective-permute-start.9 = (f32[8,9,8,128]{3,2,1,0:T(8,128)S(1)}, f32[8,9,8,128]{3,2,1,0:T(8,128)S(1)}, u32[]{:S(2)}, u32[]{:S(2)}) collective-permute-start(f32[8,9,8,128]{3,2,1,0:T(8,128)S(1)} %get-tuple-element.65), channel_id=1, source_target_pairs={{0,1},{1,0},{2,3},{3,2},{4,5},{5,4},{6,7},{7,6},{8,9},{9,8},{10,11... | collective-permute-start | bytes 884744 | tf_op jit(solution)/shard_map/ppermute | solution.py:382
  64.2 17.3 %collective-permute-start.10 = (f32[16,64,128]{2,1,0:T(8,128)S(1)}, f32[16,64,128]{2,1,0:T(8,128)S(1)}, u32[]{:S(2)}, u32[]{:S(2)}) collective-permute-start(f32[16,64,128]{2,1,0:T(8,128)S(1)} %get-tuple-element.70), channel_id=1, source_target_pairs={{0,1},{1,0},{2,3},{3,2},{4,5},{5,4},{6,7},{7,6},{8,9},{9,8},{10,11... | collective-permute-start | bytes 1572872 | tf_op jit(solution)/shard_map/ppermute | solution.py:322
  64.7 17.2 %collective-permute-start.11 = (f32[16,64,128]{2,1,0:T(8,128)S(1)}, f32[16,64,128]{2,1,0:T(8,128)S(1)}, u32[]{:S(2)}, u32[]{:S(2)}) collective-permute-start(f32[16,64,128]{2,1,0:T(8,128)S(1)} %get-tuple-element.71), channel_id=1, source_target_pairs={{0,15},{1,2},{2,1},{3,4},{4,3},{5,6},{6,5},{7,8},{8,7},{9,10},{10,... | collective-permute-start | bytes 1572872 | tf_op jit(solution)/shard_map/ppermute | solution.py:322
  92.8 6.6 %collective-permute-start.12 = (f32[8,8,8,128]{3,2,1,0:T(8,128)S(1)}, f32[8,8,8,128]{3,2,1,0:T(8,128)S(1)}, u32[]{:S(2)}, u32[]{:S(2)}) collective-permute-start(f32[8,8,8,128]{3,2,1,0:T(8,128)S(1)} %all_to_all.11.own), channel_id=1, source_target_pairs={{0,1},{1,0},{2,3},{3,2},{4,5},{5,4},{6,7},{7,6},{8,9},{9,8},{10,11... | collective-permute-start | bytes 786440 | tf_op jit(solution)/shard_map/ppermute | solution.py:406

commit v3 on v2

--- a/solution.py
+++ b/solution.py
@@ -11,6 +11,7 @@
 CHUNKS = (4, 4)
 BATCH = 4
 VMEM_LIMIT = 48 * 1024 * 1024
+ROW = ("chip", "core")
 F32 = jnp.float32
 BF16 = jnp.bfloat16
 
@@ -92,17 +93,29 @@
     return lax.rem(offsets[0, 0] // rows, 2) == 0
 
 
-def pack_kernel(chunks, offsets, counts, measured, *outs):
+def pack_kernel(offsets, counts, measured, out):
     slots, _, pixels = measured.shape
-    for (first, size), out in zip(chunks, outs):
-        for at in range(size):
-            live = jnp.where(first + at < counts[0], 1.0, 0.0).astype(F32)
-            out[at] = measured[first + at] * live
-    first_out = outs[0]
     for slot in range(slots):
+        live = jnp.where(slot < counts[0], 1.0, 0.0).astype(F32)
+        out[slot] = measured[slot] * live
         for entry in range(2):
             line = jnp.full((1, pixels), offsets[slot, entry], jnp.int32).astype(F32)
-            first_out[chunks[0][1], 2 * slot + entry : 2 * slot + entry + 1] = line
+            out[slots, 2 * slot + entry : 2 * slot + entry + 1] = line
+
+
+def middle_kernel(pixels, target, tile, *outs):
+    *parts, offsets = outs
+    planes = tile.shape[0]
+    for slot in range(offsets.shape[0]):
+        for entry in range(2):
+            line = 2 * slot + entry
+            value = target[target.shape[0] - 1, line : line + 1]
+            offsets[slot, entry] = jnp.max(value).astype(jnp.int32)
+    slot = 0
+    for part in parts:
+        for at in range(part.shape[0] // planes):
+            part[at * planes : (at + 1) * planes] = cut(tile, offsets[slot, 1], pixels)
+            slot += 1
 
 
 def cut_kernel(pixels, chunks, own, far, tile, *outs):
@@ -143,34 +156,23 @@
             out[:, :, beside] += jnp.where(lane < shift, part, 0.0)
 
 
-def slot_kernel(
-    first, size, ahead, own_offsets, *refs
-):
-    if first == 0:
-        offsets, refs = refs[-6], refs[:-6] + refs[-5:]
-    else:
-        offsets, *refs = refs
-    tile, near, cross, target, probe, prop, tables, so_far, *refs = refs
+def slot_kernel(first, size, ahead, own_offsets, *refs):
+    offsets, mid, near, cross, target, probe, prop, tables, *refs = refs
+    so_far, refs = (refs[0], refs[1:]) if first else (None, refs)
     given, refs = refs[:ahead], refs[ahead:]
     out_near, out_mid, out_cross, total, *shares = refs[:-5]
     window, patch, grads, exit_wave, far = refs[-5:]
     modes, _, pixels, _ = probe.shape
-    planes, rows, _ = tile.shape
+    planes, rows = mid.shape[0] // size, mid.shape[1]
     behind = given[0].shape[0] if given else 0
     for message, out in zip(given, (out_near, out_cross)):
         out[:behind] = message[...]
     even = is_even(own_offsets, rows)
-    if first == 0:
-        for slot in range(offsets.shape[0]):
-            for entry in range(2):
-                line = 2 * slot + entry
-                value = target[target.shape[0] - 1, line : line + 1]
-                offsets[slot, entry] = jnp.max(value).astype(jnp.int32)
-    total[...] = so_far[...]
+    total[...] = so_far[...] if first else jnp.zeros_like(total)
     held = range(BATCH)
 
     def is_live(at):
-        return jnp.max(target[at, :8]) > 0.0
+        return jnp.max(target[first + at, :8]) > 0.0
 
     def leave(slots):
         for at in slots:
@@ -183,7 +185,7 @@
         for s, at in enumerate(slots):
             strip = pl.ds(at * planes, planes)
             window[:, :rows] = jnp.where(even, cross[strip], near[strip])
-            window[:, rows : 2 * rows] = cut(tile, offsets[first + at, 1], pixels)
+            window[:, rows : 2 * rows] = mid[strip]
             window[:, 2 * rows :] = jnp.where(even, near[strip], cross[strip])
             patch[s] = window[:, pl.ds(starts[s], pixels), :]
             total[2 * modes] += live[s] * (patch[s, 0] * patch[s, 0] + patch[s, 1] * patch[s, 1])
@@ -205,7 +207,7 @@
                 wave = groups[s][m]
                 far[s, m, 0], far[s, m, 1] = wave
                 intensity = intensity + wave[0] * wave[0] + wave[1] * wave[1]
-            misfit = 2.0 * live[s] * (intensity - target[at])
+            misfit = 2.0 * live[s] * (intensity - target[first + at])
             groups[s] = [(misfit * far[s, m, 0], misfit * far[s, m, 1]) for m in all_modes]
         groups = transform(tables, True, groups)
         for s in held:
@@ -283,25 +285,26 @@
     slices, _, tile_rows, columns = object_slices.shape
     modes, _, pixels, _ = probe_modes.shape
     planes = 2 * slices
-    peers = lax.axis_size("row")
+    peers = lax.axis_size(ROW)
     params = pltpu.CompilerParams(vmem_limit_bytes=VMEM_LIMIT)
     tile = object_slices.reshape(planes, tile_rows, columns)
     starts = [sum(CHUNKS[:i]) for i in range(len(CHUNKS))]
 
     pair = [(i, i ^ 1) for i in range(peers)]
     other_pair = [(i, (i - 1) % peers if i % 2 == 0 else (i + 1) % peers) for i in range(peers)]
-    far = shifted(offsets, "row", 2)
+    far = shifted(offsets, ROW, 2)
 
     chunks = list(zip(starts, CHUNKS))
-    packed = pl.pallas_call(
-        functools.partial(pack_kernel, chunks),
-        out_shape=[jax.ShapeDtypeStruct((size + (first == 0), pixels, pixels), F32) for first, size in chunks],
+    target = pl.pallas_call(
+        pack_kernel,
+        out_shape=jax.ShapeDtypeStruct((measured.shape[0] + 1, pixels, pixels), F32),
         in_specs=[in_smem()] * 2 + [in_vmem()],
-        out_specs=[in_vmem()] * len(chunks),
+        out_specs=in_vmem(),
         compiler_params=params,
         cost_estimate=pl.CostEstimate(flops=0, bytes_accessed=1 << 20, transcendentals=0),
     )(offsets, counts, measured)
-    far, packed = lax.optimization_barrier((far, packed))
+    far, target = lax.optimization_barrier((far, target))
+    target = shifted(target, ROW, 1)
 
     def units(count):
         return jax.ShapeDtypeStruct((count, tile_rows, pixels), F32)
@@ -319,45 +322,49 @@
         return list(zip(outs[::2], outs[1::2]))
 
     def swapped(to_near, to_cross):
-        return lax.ppermute(to_near, "row", pair), lax.ppermute(to_cross, "row", other_pair)
-
-    waiting = strips(chunks[:1], far) + strips(chunks[1:], far)
+        return lax.ppermute(to_near, ROW, pair), lax.ppermute(to_cross, ROW, other_pair)
+
+    far_later, target = lax.optimization_barrier((far, target))
+    waiting = strips(chunks[:1], far) + strips(chunks[1:], far_later)
+    *middles, middle = pl.pallas_call(
+        functools.partial(middle_kernel, pixels),
+        out_shape=[units(size * planes) for size in CHUNKS] + [jax.ShapeDtypeStruct(offsets.shape, jnp.int32)],
+        in_specs=[in_vmem()] * 2,
+        out_specs=[in_vmem()] * len(CHUNKS) + [in_smem()],
+        compiler_params=params,
+        cost_estimate=pl.CostEstimate(flops=0, bytes_accessed=4 << 20, transcendentals=0),
+    )(target, tile)
     arrived = [swapped(*waiting[0])]
-    targets = [shifted(packed[0], "row", 1)]
     if len(waiting) > 1:
-        arrived[0], following, packed = lax.optimization_barrier((arrived[0], waiting[1], packed))
+        arrived[0], following, middles = lax.optimization_barrier((arrived[0], waiting[1], middles))
         arrived.append(swapped(*following))
-        targets += [shifted(part, "row", 1) for part in packed[1:]]
     prop = jnp.stack([jnp.cos(propagator_phase), jnp.sin(propagator_phase)])
     tables = jnp.asarray(fourier_tables(pixels))
 
     share = pixels // peers
-    total = jnp.zeros((2 * modes + 1, pixels, pixels), F32)
-    mid, back, mid_groups, back_groups, places = [], [], [], [], [offsets]
+    total = ()
+    mid, back, mid_groups, back_groups = [], [], [], []
     for index, (first, size) in enumerate(chunks):
         given = waiting[index + 2] if index + 2 < len(chunks) else ()
         ahead = CHUNKS[index + 2] * planes if given else 0
+        sums = jax.ShapeDtypeStruct((2 * modes + 1, pixels, pixels), F32)
         part = jax.ShapeDtypeStruct((peers // 2, 2 * modes + 1, share, pixels), F32)
         shares = [part, part] if index == len(CHUNKS) - 1 else []
         message = units(ahead + size * planes)
         field = pltpu.VMEM((BATCH, planes, pixels, pixels), F32)
         kept = pltpu.VMEM((BATCH, modes, 2, pixels, pixels), F32)
-        to_near, to_mid, to_cross, total, *shares = pl.pallas_call(
+        to_near, to_mid, to_cross, *total = pl.pallas_call(
             functools.partial(slot_kernel, first, size, len(given)),
-            out_shape=[message, units(size * planes), message, jax.ShapeDtypeStruct(total.shape, F32)]
-            + shares
-            + ([] if index else [jax.ShapeDtypeStruct(offsets.shape, jnp.int32)]),
-            in_specs=[in_smem()] * len(places) + [in_vmem()] * (8 + len(given)),
-            out_specs=[in_vmem()] * (4 + len(shares)) + ([] if index else [in_smem()]),
+            out_shape=[message, units(size * planes), message, sums] + shares,
+            in_specs=[in_smem()] * 2 + [in_vmem()] * (7 + len(total) + len(given)),
+            out_specs=[in_vmem()] * (4 + len(shares)),
             scratch_shapes=[pltpu.VMEM((planes, 3 * tile_rows, pixels), F32), field, field, kept, kept],
             compiler_params=params,
             cost_estimate=pl.CostEstimate(
                 flops=size * 6 * modes * 3 * 16 * pixels**3, bytes_accessed=8 << 20, transcendentals=0
             ),
-        )(*places, tile, *arrived[index], targets[index], probe_modes, prop, tables, total, *given)
-        if index == 0:
-            middle = shares.pop()
-            places.append(middle)
+        )(offsets, middle, middles[index], *arrived[index], target, probe_modes, prop, tables, *total, *given)
+        total, shares = total[:1], total[1:]
         mid_groups.append(("mid", first, size, 0))
         mid.append(to_mid)
         message = swapped(to_near, to_cross)
@@ -376,11 +383,10 @@
             cost_estimate=pl.CostEstimate(flops=0, bytes_accessed=5 << 20, transcendentals=0),
         )(offsets, middle, far, *strips)
 
-    cores = [list(range(core, peers, 2)) for core in range(2)]
     own, other = shares
     own, other, back[:-1] = lax.optimization_barrier((own, other, back[:-1]))
-    both = own + lax.ppermute(other, "row", pair)
-    parts = lax.all_to_all(both, "row", 0, 0, axis_index_groups=cores)
+    both = own + lax.ppermute(other, ROW, pair)
+    parts = lax.all_to_all(both, "chip", 0, 0)
     spread = pl.pallas_call(
         step_kernel,
         out_shape=jax.ShapeDtypeStruct((peers // 2, 2 * modes, share, pixels), F32),
@@ -391,7 +397,7 @@
     groups = mid_groups + back_groups
     strips = mid + [part for message in back for part in message]
     spread, strips = lax.optimization_barrier((spread, strips))
-    gathered = lax.all_to_all(spread, "row", 0, 0, axis_index_groups=cores)
+    gathered = lax.all_to_all(spread, "chip", 0, 0)
     gathered, strips = lax.optimization_barrier((gathered, strips))
 
     object_grad = added(groups, strips)
@@ -403,18 +409,21 @@
         in_specs=[in_smem()] + [in_vmem()] * 2,
         out_specs=in_vmem(),
         compiler_params=params,
-    )(offsets, gathered, lax.ppermute(gathered, "row", pair)).reshape(probe_modes.shape)
+    )(offsets, gathered, lax.ppermute(gathered, ROW, pair)).reshape(probe_modes.shape)
     return (object_grad, probe_step)
 
 
 def solution(mesh):
+    groups, peers = mesh.shape["grp"], mesh.shape["row"]
+    split = jax.sharding.Mesh(mesh.devices.reshape(groups, peers // 2, 2), ("grp",) + ROW)
+    everywhere = ("grp",) + ROW
     in_specs = (
-        P(None, None, ("grp", "row"), None),
+        P(None, None, everywhere, None),
         P("grp", None, None, None),
         P(),
-        P(("grp", "row"), None, None),
-        P(("grp", "row"), None),
-        P(("grp", "row")),
+        P(everywhere, None, None),
+        P(everywhere, None),
+        P(everywhere),
     )
-    out_specs = (P(None, None, ("grp", "row"), None), P("grp", None, None, None))
-    return jax.shard_map(local, mesh=mesh, in_specs=in_specs, out_specs=out_specs, check_vma=False)
+    out_specs = (P(None, None, everywhere, None), P("grp", None, None, None))
+    return jax.shard_map(local, mesh=split, in_specs=in_specs, out_specs=out_specs, check_vma=False)

time: 102 us -> 100 us (0.980)
  Pallas kernels: 37.5 us -> 25.5 us
  waiting for transfers between devices: 19.4 us -> 28.3 us
    pallas_call x2, Pallas kernels: 29 us -> 15.7 us  [local(): pl.pallas_call(functools.partial(slot_kernel, first, size, len(given)), o...]
    ppermute x10, waiting for transfers between devices: 17.7 us -> 25.3 us  [the longest x4 25.3 us: swapped(): lax.ppermute(to_cross, ROW, other_pair)]
    ppermute x3 -> x2, waiting for transfers between devices: 1.69 us -> 3.06 us  [shifted(): lax.ppermute(array, axis, [(i, (i + by) % peers) for i in range(peers)])]
    pallas_call x1 -> x2, Pallas kernels: 0.64 us -> 1.95 us  [the longest x1 1.31 us: local(): pl.pallas_call(functools.partial(middle_kernel, pixels), out_shape=[units...]
    ppermute x3 -> x2, starting transfers between devices: 3.81 us -> 2.53 us  [shifted(): lax.ppermute(array, axis, [(i, (i + by) % peers) for i in range(peers)])]
    unnamed x11 -> x15, local copies, waits for them, and re-layouts: 3.4 us -> 4.21 us
  transfers between devices with their start and end apart: 13 -> 12, of which waited for: 3 -> 5; matrix products, arithmetic and copies ran while one was open for 0% -> 0% of each run, Pallas kernels for 35% -> 24%
where the time goes in v3:
time: 100 us; the launch traced here: 99 us
  waiting for transfers between devices  28.3 us (28%)
  blocking collectives  27.4 us (27%)
  Pallas kernels  25.5 us (26%)
  starting transfers between devices  11.9 us (12%)
  local copies, waits for them, and re-layouts  4.45 us (4%)
  between operations  1.42 us (1%)
    ppermute x4, waiting for transfers between devices, swapped(): lax.ppermute(to_cross, ROW, other_pair)  25.3 us
    pallas_call x2, Pallas kernels, local(): pl.pallas_call(functools.partial(slot_kernel, first, size, len(given)), o...  15.7 us
    all_to_all x1, blocking collectives, local(): parts = lax.all_to_all(both, 'chip', 0, 0)  14.9 us
    all_to_all x1, blocking collectives, local(): gathered = lax.all_to_all(spread, 'chip', 0, 0)  12.5 us
    ppermute x4, starting transfers between devices, swapped(): lax.ppermute(to_cross, ROW, other_pair)  4.53 us
    unnamed x15, local copies, waits for them, and re-layouts  4.21 us
    pallas_call x1, Pallas kernels, added(): pl.pallas_call(functools.partial(add_kernel, pixels, groups), out_shape=j...  3.78 us
    ppermute x2, waiting for transfers between devices, shifted(): lax.ppermute(array, axis, [(i, (i + by) % peers) for i in range(peers)])  3.06 us
  transfers between devices with their start and end apart: 12, of which 5 were waited for; matrix products, arithmetic and copies ran while one was open for 0% of the time, Pallas kernels for 24%

profile of v3, /device:TPU:1, one launch (start us, length us, event | category | flops | bytes accessed | tf_op | source)
XLA Modules:
  0.0 99.0 jit_solution(3753082177424296933)
XLA Ops:
  0.6 0.8 copy.15.offsets.own.own_offsets
  1.4 2.1 %collective-permute-start = (s32[8,2]{1,0:T(8,128)S(1)}, s32[8,2]{1,0:T(8,128)S(1)}, u32[]{:S(2)}, u32[]{:S(2)}) collective-permute-start(s32[8,2]{1,0:T(8,128)S(1)} %copy.15.offsets.own.own_offsets), channel_id=1, source_target_pairs={{0,2},{1,3},{2,4},{3,5},{4,6},{5,7},{6,8},{7,9},{8,10},{9,11},{10,... | collective-permute-start | bytes 200 | tf_op jit(solution)/shard_map/ppermute | solution.py:21
  4.1 0.0 copy-start.2
  4.1 1.0 %copy-done.2 = f32[8,128,128]{2,1,0:T(8,128)S(1)} copy-done((f32[8,128,128]{2,1,0:T(8,128)S(1)}, f32[8,128,128]{2,1,0:T(8,128)}, u32[]{:S(2)}) %copy-start.2) | copy-done | bytes 524312
  5.1 0.0 copy-start.6
  5.2 0.6 shard_map.86
  5.8 1.7 %collective-permute-done.far = s32[8,2]{1,0:T(8,128)S(1)} collective-permute-done((s32[8,2]{1,0:T(8,128)S(1)}, s32[8,2]{1,0:T(8,128)S(1)}, u32[]{:S(2)}, u32[]{:S(2)}) %collective-permute-start) | collective-permute-done | bytes 96 | tf_op jit(solution)/shard_map/ppermute | solution.py:21
  7.5 0.5 collective-permute-start.1
  7.9 1.6 %copy-done = f32[2,2,64,2048]{3,2,1,0:T(8,128)S(1)} copy-done((f32[2,2,64,2048]{3,2,1,0:T(8,128)S(1)}, f32[2,2,64,2048]{3,2,1,0:T(8,128)}, u32[]{:S(2)}) %copy-start) | copy-done | bytes 2097176
  9.5 1.3 %shard_map.88 = (f32[16,64,128]{2,1,0:T(8,128)S(1)}, f32[16,64,128]{2,1,0:T(8,128)S(1)}) custom-call(s32[8,2]{1,0:T(8,128)S(1)} %copy.15.offsets.own.own_offsets, s32[8,2]{1,0:T(8,128)S(1)} %collective-permute-done.far, f32[4,64,2048]{2,1,0:T(8,128)S(1)} %bitcast.7), custom_call_target="tpu_custom_call" | custom-call | bytes 4194304 | tf_op jit(solution)/shard_map/pallas_call | solution.py:314
  10.8 1.2 %collective-permute-start.2 = (f32[16,64,128]{2,1,0:T(8,128)S(1)}, f32[16,64,128]{2,1,0:T(8,128)S(1)}, u32[]{:S(2)}, u32[]{:S(2)}) collective-permute-start(f32[16,64,128]{2,1,0:T(8,128)S(1)} %get-tuple-element.50), channel_id=1, source_target_pairs={{0,1},{1,0},{2,3},{3,2},{4,5},{5,4},{6,7},{7,6},{8,9},{9,8},{10,11... | collective-permute-start | bytes 1572872 | tf_op jit(solution)/shard_map/ppermute | solution.py:325
  12.0 1.1 %collective-permute-start.3 = (f32[16,64,128]{2,1,0:T(8,128)S(1)}, f32[16,64,128]{2,1,0:T(8,128)S(1)}, u32[]{:S(2)}, u32[]{:S(2)}) collective-permute-start(f32[16,64,128]{2,1,0:T(8,128)S(1)} %get-tuple-element.51), channel_id=1, source_target_pairs={{0,15},{1,2},{2,1},{3,4},{4,3},{5,6},{6,5},{7,8},{8,7},{9,10},{10,... | collective-permute-start | bytes 1572872 | tf_op jit(solution)/shard_map/ppermute | solution.py:325
  13.1 0.0 copy-done.6
  13.1 0.2 cosine_bitcast_fusion
  13.4 0.0 copy-start.3
  13.4 0.0 copy-start.4
  13.4 1.4 %collective-permute-done.1.target.refs_4_ = f32[9,128,128]{2,1,0:T(8,128)S(1)} collective-permute-done((f32[9,128,128]{2,1,0:T(8,128)S(1)}, f32[9,128,128]{2,1,0:T(8,128)S(1)}, u32[]{:S(2)}, u32[]{:S(2)}) %collective-permute-start.1) | collective-permute-done | bytes 589856 | tf_op jit(solution)/shard_map/ppermute | solution.py:21
  14.8 1.3 %shard_map.89 = (f32[16,64,128]{2,1,0:T(8,128)S(1)}, f32[16,64,128]{2,1,0:T(8,128)S(1)}) custom-call(s32[8,2]{1,0:T(8,128)S(1)} %copy.15.offsets.own.own_offsets, s32[8,2]{1,0:T(8,128)S(1)} %collective-permute-done.far, f32[4,64,2048]{2,1,0:T(8,128)S(1)} %bitcast.8), custom_call_target="tpu_custom_call" | custom-call | bytes 4194304 | tf_op jit(solution)/shard_map/pallas_call | solution.py:314
  16.1 0.0 copy-done.1
  16.1 1.3 %shard_map.87 = (f32[16,64,128]{2,1,0:T(8,128)S(1)}, f32[16,64,128]{2,1,0:T(8,128)S(1)}, s32[8,2]{1,0:T(8,128)S(1)}) custom-call(f32[9,128,128]{2,1,0:T(8,128)S(1)} %collective-permute-done.1.target.refs_4_, f32[4,64,2048]{2,1,0:T(8,128)S(1)} %bitcast.9), custom_call_target="tpu_custom_call" | custom-call | bytes 4194304 | tf_op jit(solution)/shard_map/pallas_call | solution.py:329
  17.4 0.0 collective-permute-done.2.refs_2_
  17.4 14.2 %collective-permute-done.3.refs_3_ = f32[16,64,128]{2,1,0:T(8,128)S(1)} collective-permute-done((f32[16,64,128]{2,1,0:T(8,128)S(1)}, f32[16,64,128]{2,1,0:T(8,128)S(1)}, u32[]{:S(2)}, u32[]{:S(2)}) %collective-permute-start.3) | collective-permute-done | bytes 524320 | tf_op jit(solution)/shard_map/ppermute | solution.py:325
  31.6 0.0 collective-permute-start.4
  31.6 0.0 collective-permute-start.5
  31.6 0.0 copy-done.3
  31.6 0.0 copy-done.4
  31.6 13.2 %shard_map.90 = (f32[16,64,128]{2,1,0:T(8,128)S(1)}, f32[16,64,128]{2,1,0:T(8,128)S(1)}, f32[16,64,128]{2,1,0:T(8,128)S(1)}, f32[9,128,128]{2,1,0:T(8,128)S(1)}) custom-call(s32[8,2]{1,0:T(8,128)S(1)} %copy.15.offsets.own.own_offsets, s32[8,2]{1,0:T(8,128)S(1)} %get-tuple-element.49.refs_0_.middle, f32[16,64,128]{2,1,0:T(8,128)S(1)} %get-tuple-element.60.refs_1_, ...), custom_call_target="tpu_custom_call" | custom-call | flops 9663676416 | bytes 8388608 | tf_op jit(solution)/shard_map/pallas_call | solution.py:356
  44.8 0.0 copy-start.5
  44.8 0.8 copy-done.5
  45.6 0.5 collective-permute-start.6
  46.1 1.2 %collective-permute-start.7 = (f32[16,64,128]{2,1,0:T(8,128)S(1)}, f32[16,64,128]{2,1,0:T(8,128)S(1)}, u32[]{:S(2)}, u32[]{:S(2)}) collective-permute-start(f32[16,64,128]{2,1,0:T(8,128)S(1)} %get-tuple-element.67), channel_id=1, source_target_pairs={{0,15},{1,2},{2,1},{3,4},{4,3},{5,6},{6,5},{7,8},{8,7},{9,10},{10,... | collective-permute-start | bytes 1572872 | tf_op jit(solution)/shard_map/ppermute | solution.py:325
  47.4 0.0 collective-permute-done.4.refs_2_
  47.4 0.0 collective-permute-done.5.refs_3_
  47.4 2.4 %shard_map.91 = (f32[16,64,128]{2,1,0:T(8,128)S(1)}, f32[16,64,128]{2,1,0:T(8,128)S(1)}, f32[16,64,128]{2,1,0:T(8,128)S(1)}, f32[9,128,128]{2,1,0:T(8,128)}, f32...) custom-call(s32[8,2]{1,0:T(8,128)S(1)} %copy.15.offsets.own.own_offsets, ...), custom_call_target="tpu_custom_call" | custom-call | flops 9663676416 | bytes 8388608 | tf_op jit(solution)/shard_map/pallas_call | solution.py:356
  49.8 0.0 collective-permute-done.6.refs_2_
  49.8 10.5 %collective-permute-done.7.refs_3_ = f32[16,64,128]{2,1,0:T(8,128)S(1)} collective-permute-done((f32[16,64,128]{2,1,0:T(8,128)S(1)}, f32[16,64,128]{2,1,0:T(8,128)S(1)}, u32[]{:S(2)}, u32[]{:S(2)}) %collective-permute-start.7) | collective-permute-done | bytes 524320 | tf_op jit(solution)/shard_map/ppermute | solution.py:325
  60.4 0.0 collective-permute-start.8
  60.4 0.5 collective-permute-start.9
  60.9 2.2 %collective-permute-start.10 = (f32[16,64,128]{2,1,0:T(8,128)S(1)}, f32[16,64,128]{2,1,0:T(8,128)S(1)}, u32[]{:S(2)}, u32[]{:S(2)}) collective-permute-start(f32[16,64,128]{2,1,0:T(8,128)S(1)} %get-tuple-element.75), channel_id=1, source_target_pairs={{0,15},{1,2},{2,1},{3,4},{4,3},{5,6},{6,5},{7,8},{8,7},{9,10},{10,... | collective-permute-start | bytes 1572872 | tf_op jit(solution)/shard_map/ppermute | solution.py:325
  63.1 0.0 collective-permute-done.8
  63.1 14.9 %all_to_all.10.parts = f32[8,9,8,128]{3,2,1,0:T(8,128)S(1)} all-to-all(f32[8,9,8,128]{3,2,1,0:T(8,128)S(1)} %add.3), channel_id=1, replica_groups=mesh['grp'=2,'chip'=8,'core'=2] {'chip'}, dimensions={0} | all-to-all | bytes 589824 | tf_op jit(solution)/shard_map/all_to_all | solution.py:389
  78.0 0.0 collective-permute-done.9.refs_4_
  78.0 0.6 collective-permute-done.10.refs_5_
  78.6 12.5 %all_to_all.11.own = f32[8,8,8,128]{3,2,1,0:T(8,128)S(1)} all-to-all(f32[8,8,8,128]{3,2,1,0:T(8,128)S(1)} %shard_map.92), channel_id=1, replica_groups=mesh['grp'=2,'chip'=8,'core'=2] {'chip'}, dimensions={0} | all-to-all | bytes 524288 | tf_op jit(solution)/shard_map/all_to_all | solution.py:400
  91.1 2.7 %collective-permute-start.11 = (f32[8,8,8,128]{3,2,1,0:T(8,128)S(1)}, f32[8,8,8,128]{3,2,1,0:T(8,128)S(1)}, u32[]{:S(2)}, u32[]{:S(2)}) collective-permute-start(f32[8,8,8,128]{3,2,1,0:T(8,128)S(1)} %all_to_all.11.own), channel_id=1, source_target_pairs={{0,1},{1,0},{2,3},{3,2},{4,5},{5,4},{6,7},{7,6},{8,9},{9,8},{10,11... | collective-permute-start | bytes 786440 | tf_op jit(solution)/shard_map/ppermute | solution.py:412
  93.8 3.8 %shard_map.93 = f32[4,64,2048]{2,1,0:T(8,128)} custom-call(s32[8,2]{1,0:T(8,128)S(1)} %copy.15.offsets.own.own_offsets, s32[8,2]{1,0:T(8,128)S(1)} %get-tuple-element.49.refs_0_.middle, s32[8,2]{1,0:T(8,128)S(1)} %collective-permute-done.far, f32[16,64,128]{2,1,0:T(8,128)S(1)} %get-tuple-element.83.refs_0_, f32[16,64,128]{2,1,0:T(8,128)S(1)} %get-tuple-element.84.refs_1_, ...), custom_call_target="tpu_custom_call" | custom-call | bytes 5242880 | tf_op jit(solution)/shard_map/pallas_call | solution.py:377
  97.6 0.0 collective-permute-done.11.other
  97.6 1.5 %shard_map.94 = f32[8,128,128]{2,1,0:T(8,128)} custom-call(s32[8,2]{1,0:T(8,128)S(1)} %copy.15.offsets.own.own_offsets, f32[8,8,8,128]{3,2,1,0:T(8,128)S(1)} %all_to_all.11.own, f32[8,8,8,128]{3,2,1,0:T(8,128)S(1)} %collective-permute-done.11.other), custom_call_target="tpu_custom_call" | custom-call | tf_op jit(solution)/shard_map/pallas_call | solution.py:406
  (5 shorter events, 0.1 us)
Async XLA Ops:
  1.4 6.1 %collective-permute-start = (s32[8,2]{1,0:T(8,128)S(1)}, s32[8,2]{1,0:T(8,128)S(1)}, u32[]{:S(2)}, u32[]{:S(2)}) collective-permute-start(s32[8,2]{1,0:T(8,128)S(1)} %copy.15.offsets.own.own_offsets), channel_id=1, source_target_pairs={{0,2},{1,3},{2,4},{3,5},{4,6},{5,7},{6,8},{7,9},{8,10},{9,11},{10,... | collective-permute-start | bytes 200 | tf_op jit(solution)/shard_map/ppermute | solution.py:21
  4.1 1.0 %copy-start.2 = (f32[8,128,128]{2,1,0:T(8,128)S(1)}, f32[8,128,128]{2,1,0:T(8,128)}, u32[]{:S(2)}) copy-start(f32[8,128,128]{2,1,0:T(8,128)} %measured.1) | copy-start | bytes 1572868
  5.1 8.0 %copy-start.6 = (f32[128,128]{1,0:T(8,128)S(1)}, f32[128,128]{1,0:T(8,128)}, u32[]{:S(2)}) copy-start(f32[128,128]{1,0:T(8,128)} %param.9) | copy-start | bytes 196612
  7.5 7.3 %collective-permute-start.1 = (f32[9,128,128]{2,1,0:T(8,128)S(1)}, f32[9,128,128]{2,1,0:T(8,128)S(1)}, u32[]{:S(2)}, u32[]{:S(2)}) collective-permute-start(f32[9,128,128]{2,1,0:T(8,128)S(1)} %shard_map.86), channel_id=1, source_target_pairs={{0,1},{1,2},{2,3},{3,4},{4,5},{5,6},{6,7},{7,8},{8,9},{9,10},{10,1... | collective-permute-start | bytes 1769480 | tf_op jit(solution)/shard_map/ppermute | solution.py:21
  7.9 1.6 %copy-start = (f32[2,2,64,2048]{3,2,1,0:T(8,128)S(1)}, f32[2,2,64,2048]{3,2,1,0:T(8,128)}, u32[]{:S(2)}) copy-start(f32[2,2,64,2048]{3,2,1,0:T(8,128)} %param.7) | copy-start | bytes 6291460
  9.5 6.5 %copy-start.1 = (f32[2,2,64,2048]{3,2,1,0:T(8,128)S(1)}, f32[2,2,64,2048]{3,2,1,0:T(8,128)}, u32[]{:S(2)}) copy-start(f32[2,2,64,2048]{3,2,1,0:T(8,128)} %param.7) | copy-start | bytes 6291460
  10.8 6.6 %collective-permute-start.2 = (f32[16,64,128]{2,1,0:T(8,128)S(1)}, f32[16,64,128]{2,1,0:T(8,128)S(1)}, u32[]{:S(2)}, u32[]{:S(2)}) collective-permute-start(f32[16,64,128]{2,1,0:T(8,128)S(1)} %get-tuple-element.50), channel_id=1, source_target_pairs={{0,1},{1,0},{2,3},{3,2},{4,5},{5,4},{6,7},{7,6},{8,9},{9,8},{10,11... | collective-permute-start | bytes 1572872 | tf_op jit(solution)/shard_map/ppermute | solution.py:325
  12.0 19.6 %collective-permute-start.3 = (f32[16,64,128]{2,1,0:T(8,128)S(1)}, f32[16,64,128]{2,1,0:T(8,128)S(1)}, u32[]{:S(2)}, u32[]{:S(2)}) collective-permute-start(f32[16,64,128]{2,1,0:T(8,128)S(1)} %get-tuple-element.51), channel_id=1, source_target_pairs={{0,15},{1,2},{2,1},{3,4},{4,3},{5,6},{6,5},{7,8},{8,7},{9,10},{10,... | collective-permute-start | bytes 1572872 | tf_op jit(solution)/shard_map/ppermute | solution.py:325
  13.4 18.2 %copy-start.3 = (f32[4,2,128,128]{3,2,1,0:T(8,128)S(1)}, f32[4,2,128,128]{3,2,1,0:T(8,128)}, u32[]{:S(2)}) copy-start(f32[4,2,128,128]{3,2,1,0:T(8,128)} %refs_5_.3) | copy-start | bytes 1572868
  13.4 18.2 %copy-start.4 = (bf16[4,256,256]{2,1,0:T(8,128)(2,1)S(1)}, bf16[4,256,256]{2,1,0:T(8,128)(2,1)}, u32[]{:S(2)}) copy-start(bf16[4,256,256]{2,1,0:T(8,128)(2,1)} %constant.2.clone.refs_7_) | copy-start | bytes 1572868
  31.6 15.8 %collective-permute-start.4 = (f32[16,64,128]{2,1,0:T(8,128)S(1)}, f32[16,64,128]{2,1,0:T(8,128)S(1)}, u32[]{:S(2)}, u32[]{:S(2)}) collective-permute-start(f32[16,64,128]{2,1,0:T(8,128)S(1)} %get-tuple-element.58), channel_id=1, source_target_pairs={{0,1},{1,0},{2,3},{3,2},{4,5},{5,4},{6,7},{7,6},{8,9},{9,8},{10,11... | collective-permute-start | bytes 1572872 | tf_op jit(solution)/shard_map/ppermute | solution.py:325
  31.6 15.8 %collective-permute-start.5 = (f32[16,64,128]{2,1,0:T(8,128)S(1)}, f32[16,64,128]{2,1,0:T(8,128)S(1)}, u32[]{:S(2)}, u32[]{:S(2)}) collective-permute-start(f32[16,64,128]{2,1,0:T(8,128)S(1)} %get-tuple-element.59), channel_id=1, source_target_pairs={{0,15},{1,2},{2,1},{3,4},{4,3},{5,6},{6,5},{7,8},{8,7},{9,10},{10,... | collective-permute-start | bytes 1572872 | tf_op jit(solution)/shard_map/ppermute | solution.py:325
  44.8 0.8 copy-start.5
  45.6 4.2 %collective-permute-start.6 = (f32[16,64,128]{2,1,0:T(8,128)S(1)}, f32[16,64,128]{2,1,0:T(8,128)S(1)}, u32[]{:S(2)}, u32[]{:S(2)}) collective-permute-start(f32[16,64,128]{2,1,0:T(8,128)S(1)} %get-tuple-element.66), channel_id=1, source_target_pairs={{0,1},{1,0},{2,3},{3,2},{4,5},{5,4},{6,7},{7,6},{8,9},{9,8},{10,11... | collective-permute-start | bytes 1572872 | tf_op jit(solution)/shard_map/ppermute | solution.py:325
  46.1 14.2 %collective-permute-start.7 = (f32[16,64,128]{2,1,0:T(8,128)S(1)}, f32[16,64,128]{2,1,0:T(8,128)S(1)}, u32[]{:S(2)}, u32[]{:S(2)}) collective-permute-start(f32[16,64,128]{2,1,0:T(8,128)S(1)} %get-tuple-element.67), channel_id=1, source_target_pairs={{0,15},{1,2},{2,1},{3,4},{4,3},{5,6},{6,5},{7,8},{8,7},{9,10},{10,... | collective-permute-start | bytes 1572872 | tf_op jit(solution)/shard_map/ppermute | solution.py:325
  60.4 2.7 %collective-permute-start.8 = (f32[8,9,8,128]{3,2,1,0:T(8,128)S(1)}, f32[8,9,8,128]{3,2,1,0:T(8,128)S(1)}, u32[]{:S(2)}, u32[]{:S(2)}) collective-permute-start(f32[8,9,8,128]{3,2,1,0:T(8,128)S(1)} %get-tuple-element.69), channel_id=1, source_target_pairs={{0,1},{1,0},{2,3},{3,2},{4,5},{5,4},{6,7},{7,6},{8,9},{9,8},{10,11... | collective-permute-start | bytes 884744 | tf_op jit(solution)/shard_map/ppermute | solution.py:388
  60.4 17.6 %collective-permute-start.9 = (f32[16,64,128]{2,1,0:T(8,128)S(1)}, f32[16,64,128]{2,1,0:T(8,128)S(1)}, u32[]{:S(2)}, u32[]{:S(2)}) collective-permute-start(f32[16,64,128]{2,1,0:T(8,128)S(1)} %get-tuple-element.74), channel_id=1, source_target_pairs={{0,1},{1,0},{2,3},{3,2},{4,5},{5,4},{6,7},{7,6},{8,9},{9,8},{10,11... | collective-permute-start | bytes 1572872 | tf_op jit(solution)/shard_map/ppermute | solution.py:325
  60.9 17.7 %collective-permute-start.10 = (f32[16,64,128]{2,1,0:T(8,128)S(1)}, f32[16,64,128]{2,1,0:T(8,128)S(1)}, u32[]{:S(2)}, u32[]{:S(2)}) collective-permute-start(f32[16,64,128]{2,1,0:T(8,128)S(1)} %get-tuple-element.75), channel_id=1, source_target_pairs={{0,15},{1,2},{2,1},{3,4},{4,3},{5,6},{6,5},{7,8},{8,7},{9,10},{10,... | collective-permute-start | bytes 1572872 | tf_op jit(solution)/shard_map/ppermute | solution.py:325
  91.1 6.5 %collective-permute-start.11 = (f32[8,8,8,128]{3,2,1,0:T(8,128)S(1)}, f32[8,8,8,128]{3,2,1,0:T(8,128)S(1)}, u32[]{:S(2)}, u32[]{:S(2)}) collective-permute-start(f32[8,8,8,128]{3,2,1,0:T(8,128)S(1)} %all_to_all.11.own), channel_id=1, source_target_pairs={{0,1},{1,0},{2,3},{3,2},{4,5},{5,4},{6,7},{7,6},{8,9},{9,8},{10,11... | collective-permute-start | bytes 786440 | tf_op jit(solution)/shard_map/ppermute | solution.py:412

commit v4 on v3

--- a/solution.py
+++ b/solution.py
@@ -10,7 +10,7 @@
 
 CHUNKS = (4, 4)
 BATCH = 4
-VMEM_LIMIT = 48 * 1024 * 1024
+VMEM_LIMIT = 32 * 1024 * 1024
 ROW = ("chip", "core")
 F32 = jnp.float32
 BF16 = jnp.bfloat16
@@ -21,15 +21,31 @@
     return lax.ppermute(array, axis, [(i, (i + by) % peers) for i in range(peers)])
 
 
+def real_form(matrix):
+    return np.block([[matrix.real, -matrix.imag], [matrix.imag, matrix.real]]).astype(np.float32)
+
+
+def two_pieces(matrix):
+    high = matrix.astype(BF16)
+    return high, (matrix - high.astype(np.float32)).astype(BF16)
+
+
 def fourier_tables(pixels):
+    half = pixels // 2
+    kept, rows = np.arange(half)[:, None], np.arange(half)[None, :]
+    lefts = []
+    for odd in range(2):
+        turns = (2 * kept + odd) * rows % pixels / pixels
+        part = real_form(np.exp(-2j * np.pi * turns) / np.sqrt(pixels))
+        for table in (part, part.T):
+            high, low = two_pieces(table)
+            lefts.append(np.block([[high, high], [low, np.zeros_like(low)]]))
     indices = np.arange(pixels)
-    angles = 2.0 * np.pi * (indices[:, None] * indices[None, :] % pixels) / pixels
-    re = np.cos(angles) / np.sqrt(pixels)
-    im = -np.sin(angles) / np.sqrt(pixels)
-    left = np.block([[re, -im], [im, re]]).astype(np.float32)
-    high = left.astype(BF16)
-    low = (left - high.astype(np.float32)).astype(BF16)
-    return np.stack([high, low, high.T, low.T])
+    whole = np.exp(-2j * np.pi * (indices[:, None] * indices[None, :] % pixels) / pixels) / np.sqrt(pixels)
+    rights = []
+    for table in (real_form(whole).T, real_form(whole)):
+        rights += two_pieces(table)
+    return np.stack(lefts + rights)
 
 
 def pieces(array):
@@ -37,21 +53,37 @@
     return high, (array - high.astype(F32)).astype(BF16)
 
 
+def from_left(tables, conj, waves):
+    half = waves[0][0].shape[0] // 2
+    pixels = 2 * half
+    sides = []
+    for odd in range(2):
+        parts = []
+        for wave in waves:
+            if conj:
+                parts.append(jnp.concatenate([part[odd * half : (odd + 1) * half] for part in wave], axis=0))
+            elif odd:
+                parts.append(jnp.concatenate([part[:half] - part[half:] for part in wave], axis=0))
+            else:
+                parts.append(jnp.concatenate([part[:half] + part[half:] for part in wave], axis=0))
+        stacked = jnp.concatenate(pieces(jnp.concatenate(parts, axis=1)), axis=0)
+        product = jnp.dot(tables[2 * odd + conj], stacked, preferred_element_type=F32)
+        sides.append(product[:pixels] + product[pixels:])
+    if conj:
+        sides = [sides[0] + sides[1], sides[0] - sides[1]]
+    turned = []
+    for at in range(0, len(waves) * pixels, pixels):
+        re = jnp.concatenate([side[:half, at : at + pixels] for side in sides], axis=0)
+        im = jnp.concatenate([side[half:, at : at + pixels] for side in sides], axis=0)
+        turned.append(jnp.concatenate([re, im], axis=1))
+    return jnp.concatenate(turned, axis=0)
+
+
 def transform(tables, conj, groups):
-    at_left, at_right = (2, 0) if conj else (0, 2)
-    left = jnp.concatenate([tables[at_left], tables[at_left + 1], tables[at_left]], axis=1)
-    right = jnp.concatenate([tables[at_right], tables[at_right], tables[at_right + 1]], axis=0)
-    pixels = left.shape[0] // 2
-    halves = []
-    for waves in groups:
-        stacked = jnp.concatenate([jnp.concatenate(wave, axis=0) for wave in waves], axis=1)
-        high, low = pieces(stacked)
-        half = jnp.dot(left, jnp.concatenate([high, high, low], axis=0), preferred_element_type=F32)
-        turned = [
-            jnp.concatenate([half[:pixels, at : at + pixels], half[pixels:, at : at + pixels]], axis=1)
-            for at in range(0, half.shape[1], pixels)
-        ]
-        halves.append(pieces(jnp.concatenate(turned, axis=0)))
+    right_high, right_low = tables[4 + 2 * conj], tables[5 + 2 * conj]
+    right = jnp.concatenate([right_high, right_high, right_low], axis=0)
+    halves = [pieces(from_left(tables, conj, waves)) for waves in groups]
+    pixels = right.shape[1] // 2
     wholes = []
     for high, low in halves:
         whole = jnp.dot(jnp.concatenate([high, low, high], axis=1), right, preferred_element_type=F32)
@@ -97,7 +129,9 @@
     slots, _, pixels = measured.shape
     for slot in range(slots):
         live = jnp.where(slot < counts[0], 1.0, 0.0).astype(F32)
-        out[slot] = measured[slot] * live
+        for odd in range(2):
+            rows = pl.ds(odd, pixels // 2, stride=2)
+            out[slot, odd * pixels // 2 : (odd + 1) * pixels // 2] = measured[slot, rows] * live
         for entry in range(2):
             line = jnp.full((1, pixels), offsets[slot, entry], jnp.int32).astype(F32)
             out[slots, 2 * slot + entry : 2 * slot + entry + 1] = line
@@ -160,8 +194,9 @@
     offsets, mid, near, cross, target, probe, prop, tables, *refs = refs
     so_far, refs = (refs[0], refs[1:]) if first else (None, refs)
     given, refs = refs[:ahead], refs[ahead:]
-    out_near, out_mid, out_cross, total, *shares = refs[:-5]
+    out_near, out_mid, out_cross, *shares = refs[:-5]
     window, patch, grads, exit_wave, far = refs[-5:]
+    total = shares.pop()
     modes, _, pixels, _ = probe.shape
     planes, rows = mid.shape[0] // size, mid.shape[1]
     behind = given[0].shape[0] if given else 0
@@ -338,7 +373,8 @@
     if len(waiting) > 1:
         arrived[0], following, middles = lax.optimization_barrier((arrived[0], waiting[1], middles))
         arrived.append(swapped(*following))
-    prop = jnp.stack([jnp.cos(propagator_phase), jnp.sin(propagator_phase)])
+    phase = jnp.concatenate([propagator_phase[0::2], propagator_phase[1::2]], axis=0)
+    prop = jnp.stack([jnp.cos(phase), jnp.sin(phase)])
     tables = jnp.asarray(fourier_tables(pixels))
 
     share = pixels // peers
@@ -355,16 +391,16 @@
         kept = pltpu.VMEM((BATCH, modes, 2, pixels, pixels), F32)
         to_near, to_mid, to_cross, *total = pl.pallas_call(
             functools.partial(slot_kernel, first, size, len(given)),
-            out_shape=[message, units(size * planes), message, sums] + shares,
+            out_shape=[message, units(size * planes), message] + (shares or [sums]),
             in_specs=[in_smem()] * 2 + [in_vmem()] * (7 + len(total) + len(given)),
-            out_specs=[in_vmem()] * (4 + len(shares)),
-            scratch_shapes=[pltpu.VMEM((planes, 3 * tile_rows, pixels), F32), field, field, kept, kept],
+            out_specs=[in_vmem()] * (3 + (len(shares) or 1)),
+            scratch_shapes=([pltpu.VMEM(sums.shape, F32)] if shares else [])
+            + [pltpu.VMEM((planes, 3 * tile_rows, pixels), F32), field, field, kept, kept],
             compiler_params=params,
             cost_estimate=pl.CostEstimate(
                 flops=size * 6 * modes * 3 * 16 * pixels**3, bytes_accessed=8 << 20, transcendentals=0
             ),
         )(offsets, middle, middles[index], *arrived[index], target, probe_modes, prop, tables, *total, *given)
-        total, shares = total[:1], total[1:]
         mid_groups.append(("mid", first, size, 0))
         mid.append(to_mid)
         message = swapped(to_near, to_cross)
@@ -383,7 +419,7 @@
             cost_estimate=pl.CostEstimate(flops=0, bytes_accessed=5 << 20, transcendentals=0),
         )(offsets, middle, far, *strips)
 
-    own, other = shares
+    own, other = total
     own, other, back[:-1] = lax.optimization_barrier((own, other, back[:-1]))
     both = own + lax.ppermute(other, ROW, pair)
     parts = lax.all_to_all(both, "chip", 0, 0)

time: 100 us -> 97.8 us (0.978)
  local copies, waits for them, and re-layouts: 4.45 us -> 3.43 us
  Pallas kernels: 25.5 us -> 24.5 us
  waiting for transfers between devices: 28.3 us -> 29.3 us
    pallas_call x2, Pallas kernels: 15.7 us -> 13.8 us  [local(): pl.pallas_call(functools.partial(slot_kernel, first, size, len(given)), o...]
    ppermute x4, waiting for transfers between devices: 25.3 us -> 27.1 us  [swapped(): lax.ppermute(to_cross, ROW, other_pair)]
    ppermute x4, starting transfers between devices: 4.53 us -> 3.53 us  [swapped(): lax.ppermute(to_cross, ROW, other_pair)]
    unnamed x15 -> x13, local copies, waits for them, and re-layouts: 4.21 us -> 3.4 us
where the time goes in v4:
time: 97.8 us; the launch traced here: 97.3 us
  waiting for transfers between devices  29.3 us (30%)
  blocking collectives  27.3 us (28%)
  Pallas kernels  24.5 us (25%)
  starting transfers between devices  11 us (11%)
  local copies, waits for them, and re-layouts  3.43 us (4%)
  between operations  1.42 us (1%)
    ppermute x4, waiting for transfers between devices, swapped(): lax.ppermute(to_cross, ROW, other_pair)  27.1 us
    all_to_all x1, blocking collectives, local(): parts = lax.all_to_all(both, 'chip', 0, 0)  14.9 us
    pallas_call x2, Pallas kernels, local(): pl.pallas_call(functools.partial(slot_kernel, first, size, len(given)), o...  13.8 us
    all_to_all x1, blocking collectives, local(): gathered = lax.all_to_all(spread, 'chip', 0, 0)  12.5 us
    pallas_call x1, Pallas kernels, added(): pl.pallas_call(functools.partial(add_kernel, pixels, groups), out_shape=j...  3.77 us
    ppermute x4, starting transfers between devices, swapped(): lax.ppermute(to_cross, ROW, other_pair)  3.53 us
    pallas_call x2, Pallas kernels, strips(): pl.pallas_call(functools.partial(cut_kernel, pixels, chunks), out_shape=s...  3.48 us
    unnamed x13, local copies, waits for them, and re-layouts  3.4 us
  transfers between devices with their start and end apart: 12, of which 5 were waited for; matrix products, arithmetic and copies ran while one was open for 0% of the time, Pallas kernels for 24%

profile of v4, /device:TPU:1, one launch (start us, length us, event | category | flops | bytes accessed | tf_op | source)
XLA Modules:
  0.0 97.3 jit_solution(9106440899732773109)
XLA Ops:
  0.6 0.8 copy.15.offsets.own.own_offsets
  1.4 2.1 %collective-permute-start = (s32[8,2]{1,0:T(8,128)S(1)}, s32[8,2]{1,0:T(8,128)S(1)}, u32[]{:S(2)}, u32[]{:S(2)}) collective-permute-start(s32[8,2]{1,0:T(8,128)S(1)} %copy.15.offsets.own.own_offsets), channel_id=1, source_target_pairs={{0,2},{1,3},{2,4},{3,5},{4,6},{5,7},{6,8},{7,9},{8,10},{9,11},{10,... | collective-permute-start | bytes 200 | tf_op jit(solution)/shard_map/ppermute | solution.py:21
  4.1 0.0 copy-start.2
  4.1 1.0 %copy-done.2 = f32[8,128,128]{2,1,0:T(8,128)S(1)} copy-done((f32[8,128,128]{2,1,0:T(8,128)S(1)}, f32[8,128,128]{2,1,0:T(8,128)}, u32[]{:S(2)}) %copy-start.2) | copy-done | bytes 524312
  5.1 0.0 copy-start.5
  5.2 0.6 shard_map.86
  5.8 1.7 %collective-permute-done.far = s32[8,2]{1,0:T(8,128)S(1)} collective-permute-done((s32[8,2]{1,0:T(8,128)S(1)}, s32[8,2]{1,0:T(8,128)S(1)}, u32[]{:S(2)}, u32[]{:S(2)}) %collective-permute-start) | collective-permute-done | bytes 96 | tf_op jit(solution)/shard_map/ppermute | solution.py:21
  7.5 0.5 collective-permute-start.1
  7.9 0.0 copy-start
  7.9 1.6 %copy-done = f32[2,2,64,2048]{3,2,1,0:T(8,128)S(1)} copy-done((f32[2,2,64,2048]{3,2,1,0:T(8,128)S(1)}, f32[2,2,64,2048]{3,2,1,0:T(8,128)}, u32[]{:S(2)}) %copy-start) | copy-done | bytes 2097176
  9.5 0.0 copy-start.1
  9.5 2.2 %shard_map.88 = (f32[16,64,128]{2,1,0:T(8,128)}, f32[16,64,128]{2,1,0:T(8,128)}) custom-call(s32[8,2]{1,0:T(8,128)S(1)} %copy.15.offsets.own.own_offsets, s32[8,2]{1,0:T(8,128)S(1)} %collective-permute-done.far, f32[4,64,2048]{2,1,0:T(8,128)S(1)} %bitcast.5), custom_call_target="tpu_custom_call" | custom-call | bytes 4194304 | tf_op jit(solution)/shard_map/pallas_call | solution.py:349
  11.7 1.1 %collective-permute-start.2 = (f32[16,64,128]{2,1,0:T(8,128)}, f32[16,64,128]{2,1,0:T(8,128)}, u32[]{:S(2)}, u32[]{:S(2)}) collective-permute-start(f32[16,64,128]{2,1,0:T(8,128)} %get-tuple-element.50), channel_id=1, source_target_pairs={{0,1},{1,0},{2,3},{3,2},{4,5},{5,4},{6,7},{7,6},{8,9},{9,8},{10,11... | collective-permute-start | bytes 1572872 | tf_op jit(solution)/shard_map/ppermute | solution.py:360
  12.8 1.1 %collective-permute-start.3 = (f32[16,64,128]{2,1,0:T(8,128)}, f32[16,64,128]{2,1,0:T(8,128)}, u32[]{:S(2)}, u32[]{:S(2)}) collective-permute-start(f32[16,64,128]{2,1,0:T(8,128)} %get-tuple-element.51), channel_id=1, source_target_pairs={{0,15},{1,2},{2,1},{3,4},{4,3},{5,6},{6,5},{7,8},{8,7},{9,10},{10,... | collective-permute-start | bytes 1572872 | tf_op jit(solution)/shard_map/ppermute | solution.py:360
  13.9 0.0 copy-done.5
  14.0 0.2 fusion.1
  14.2 0.0 copy-start.3
  14.3 0.0 copy-start.4
  14.3 0.5 collective-permute-done.1.target.refs_4_
  14.8 0.0 copy-done.1
  14.8 1.3 %shard_map.89 = (f32[16,64,128]{2,1,0:T(8,128)S(1)}, f32[16,64,128]{2,1,0:T(8,128)S(1)}) custom-call(s32[8,2]{1,0:T(8,128)S(1)} %copy.15.offsets.own.own_offsets, s32[8,2]{1,0:T(8,128)S(1)} %collective-permute-done.far, f32[4,64,2048]{2,1,0:T(8,128)S(1)} %bitcast.6), custom_call_target="tpu_custom_call" | custom-call | bytes 4194304 | tf_op jit(solution)/shard_map/pallas_call | solution.py:349
  16.1 1.3 %shard_map.87 = (f32[16,64,128]{2,1,0:T(8,128)S(1)}, f32[16,64,128]{2,1,0:T(8,128)S(1)}, s32[8,2]{1,0:T(8,128)S(1)}) custom-call(f32[9,128,128]{2,1,0:T(8,128)S(1)} %collective-permute-done.1.target.refs_4_, f32[4,64,2048]{2,1,0:T(8,128)S(1)} %bitcast.7), custom_call_target="tpu_custom_call" | custom-call | bytes 4194304 | tf_op jit(solution)/shard_map/pallas_call | solution.py:364
  17.4 0.0 collective-permute-done.2.refs_2_
  17.4 14.3 %collective-permute-done.3.refs_3_ = f32[16,64,128]{2,1,0:T(8,128)} collective-permute-done((f32[16,64,128]{2,1,0:T(8,128)}, f32[16,64,128]{2,1,0:T(8,128)}, u32[]{:S(2)}, u32[]{:S(2)}) %collective-permute-start.3) | collective-permute-done | bytes 524320 | tf_op jit(solution)/shard_map/ppermute | solution.py:360
  31.7 0.0 collective-permute-start.4
  31.7 0.0 collective-permute-start.5
  31.7 0.0 copy-done.3
  31.7 0.0 copy-done.4
  31.7 12.6 %shard_map.90 = (f32[16,64,128]{2,1,0:T(8,128)S(1)}, f32[16,64,128]{2,1,0:T(8,128)S(1)}, f32[16,64,128]{2,1,0:T(8,128)S(1)}, f32[9,128,128]{2,1,0:T(8,128)S(1)}) custom-call(s32[8,2]{1,0:T(8,128)S(1)} %copy.15.offsets.own.own_offsets, s32[8,2]{1,0:T(8,128)S(1)} %get-tuple-element.49.refs_0_.middle, f32[16,64,128]{2,1,0:T(8,128)S(1)} %get-tuple-element.60.refs_1_, ...), custom_call_target="tpu_custom_call" | custom-call | flops 9663676416 | bytes 8388608 | tf_op jit(solution)/shard_map/pallas_call | solution.py:392
  44.3 0.7 collective-permute-start.6
  45.0 1.2 %collective-permute-start.7 = (f32[16,64,128]{2,1,0:T(8,128)S(1)}, f32[16,64,128]{2,1,0:T(8,128)S(1)}, u32[]{:S(2)}, u32[]{:S(2)}) collective-permute-start(f32[16,64,128]{2,1,0:T(8,128)S(1)} %get-tuple-element.67), channel_id=1, source_target_pairs={{0,15},{1,2},{2,1},{3,4},{4,3},{5,6},{6,5},{7,8},{8,7},{9,10},{10,... | collective-permute-start | bytes 1572872 | tf_op jit(solution)/shard_map/ppermute | solution.py:360
  46.2 0.0 collective-permute-done.4.refs_2_
  46.2 0.0 collective-permute-done.5.refs_3_
  46.2 1.2 %shard_map.91 = (f32[16,64,128]{2,1,0:T(8,128)S(1)}, f32[16,64,128]{2,1,0:T(8,128)S(1)}, f32[16,64,128]{2,1,0:T(8,128)S(1)}, f32[8,9,8,128]{3,2,1,0:T(8,128)S(1)}, f32[8,9,8,128]{3,2,1,0:T(8,128)S(1)}) custom-call(s32[8,2]{1,0:T(8,128)S(1)} %copy.15.offsets.own.own_offsets, s32[8,2]{1,0:T(8,128)S(1)} %get-tuple-element.49.refs_0_.middle, ...), custom_call_target="tpu_custom_call" | custom-call | flops 9663676416 | bytes 8388608 | tf_op jit(solution)/shard_map/pallas_call | solution.py:392
  47.4 0.0 collective-permute-done.6.refs_2_
  47.4 11.8 %collective-permute-done.7.refs_3_ = f32[16,64,128]{2,1,0:T(8,128)S(1)} collective-permute-done((f32[16,64,128]{2,1,0:T(8,128)S(1)}, f32[16,64,128]{2,1,0:T(8,128)S(1)}, u32[]{:S(2)}, u32[]{:S(2)}) %collective-permute-start.7) | collective-permute-done | bytes 524320 | tf_op jit(solution)/shard_map/ppermute | solution.py:360
  59.2 0.0 collective-permute-start.8
  59.2 0.5 collective-permute-start.9
  59.7 1.2 %collective-permute-start.10 = (f32[16,64,128]{2,1,0:T(8,128)S(1)}, f32[16,64,128]{2,1,0:T(8,128)S(1)}, u32[]{:S(2)}, u32[]{:S(2)}) collective-permute-start(f32[16,64,128]{2,1,0:T(8,128)S(1)} %get-tuple-element.75), channel_id=1, source_target_pairs={{0,15},{1,2},{2,1},{3,4},{4,3},{5,6},{6,5},{7,8},{8,7},{9,10},{10,... | collective-permute-start | bytes 1572872 | tf_op jit(solution)/shard_map/ppermute | solution.py:360
  60.9 0.0 collective-permute-done.8
  61.0 14.9 %all_to_all.10.parts = f32[8,9,8,128]{3,2,1,0:T(8,128)S(1)} all-to-all(f32[8,9,8,128]{3,2,1,0:T(8,128)S(1)} %add.3), channel_id=1, replica_groups=mesh['grp'=2,'chip'=8,'core'=2] {'chip'}, dimensions={0} | all-to-all | bytes 589824 | tf_op jit(solution)/shard_map/all_to_all | solution.py:425
  75.9 0.0 collective-permute-done.9.refs_4_
  75.9 1.0 %collective-permute-done.10.refs_5_ = f32[16,64,128]{2,1,0:T(8,128)S(1)} collective-permute-done((f32[16,64,128]{2,1,0:T(8,128)S(1)}, f32[16,64,128]{2,1,0:T(8,128)S(1)}, u32[]{:S(2)}, u32[]{:S(2)}) %collective-permute-start.10) | collective-permute-done | bytes 524320 | tf_op jit(solution)/shard_map/ppermute | solution.py:360
  76.9 12.5 %all_to_all.11.own = f32[8,8,8,128]{3,2,1,0:T(8,128)S(1)} all-to-all(f32[8,8,8,128]{3,2,1,0:T(8,128)S(1)} %shard_map.92), channel_id=1, replica_groups=mesh['grp'=2,'chip'=8,'core'=2] {'chip'}, dimensions={0} | all-to-all | bytes 524288 | tf_op jit(solution)/shard_map/all_to_all | solution.py:436
  89.4 2.7 %collective-permute-start.11 = (f32[8,8,8,128]{3,2,1,0:T(8,128)S(1)}, f32[8,8,8,128]{3,2,1,0:T(8,128)S(1)}, u32[]{:S(2)}, u32[]{:S(2)}) collective-permute-start(f32[8,8,8,128]{3,2,1,0:T(8,128)S(1)} %all_to_all.11.own), channel_id=1, source_target_pairs={{0,1},{1,0},{2,3},{3,2},{4,5},{5,4},{6,7},{7,6},{8,9},{9,8},{10,11... | collective-permute-start | bytes 786440 | tf_op jit(solution)/shard_map/ppermute | solution.py:448
  92.1 3.8 %shard_map.93 = f32[4,64,2048]{2,1,0:T(8,128)} custom-call(s32[8,2]{1,0:T(8,128)S(1)} %copy.15.offsets.own.own_offsets, s32[8,2]{1,0:T(8,128)S(1)} %get-tuple-element.49.refs_0_.middle, s32[8,2]{1,0:T(8,128)S(1)} %collective-permute-done.far, f32[16,64,128]{2,1,0:T(8,128)S(1)} %get-tuple-element.83.refs_0_, f32[16,64,128]{2,1,0:T(8,128)S(1)} %get-tuple-element.84.refs_1_, ...), custom_call_target="tpu_custom_call" | custom-call | bytes 5242880 | tf_op jit(solution)/shard_map/pallas_call | solution.py:413
  95.8 0.0 collective-permute-done.11.other
  95.9 1.5 %shard_map.94 = f32[8,128,128]{2,1,0:T(8,128)} custom-call(s32[8,2]{1,0:T(8,128)S(1)} %copy.15.offsets.own.own_offsets, f32[8,8,8,128]{3,2,1,0:T(8,128)S(1)} %all_to_all.11.own, f32[8,8,8,128]{3,2,1,0:T(8,128)S(1)} %collective-permute-done.11.other), custom_call_target="tpu_custom_call" | custom-call | tf_op jit(solution)/shard_map/pallas_call | solution.py:442
  (5 shorter events, 0.1 us)
Async XLA Ops:
  1.4 6.1 %collective-permute-start = (s32[8,2]{1,0:T(8,128)S(1)}, s32[8,2]{1,0:T(8,128)S(1)}, u32[]{:S(2)}, u32[]{:S(2)}) collective-permute-start(s32[8,2]{1,0:T(8,128)S(1)} %copy.15.offsets.own.own_offsets), channel_id=1, source_target_pairs={{0,2},{1,3},{2,4},{3,5},{4,6},{5,7},{6,8},{7,9},{8,10},{9,11},{10,... | collective-permute-start | bytes 200 | tf_op jit(solution)/shard_map/ppermute | solution.py:21
  4.1 1.0 %copy-start.2 = (f32[8,128,128]{2,1,0:T(8,128)S(1)}, f32[8,128,128]{2,1,0:T(8,128)}, u32[]{:S(2)}) copy-start(f32[8,128,128]{2,1,0:T(8,128)} %measured.1) | copy-start | bytes 1572868
  5.1 8.8 %copy-start.5 = (f32[128,128]{1,0:T(8,128)S(1)}, f32[128,128]{1,0:T(8,128)}, u32[]{:S(2)}) copy-start(f32[128,128]{1,0:T(8,128)} %param.9) | copy-start | bytes 196612
  7.5 7.3 %collective-permute-start.1 = (f32[9,128,128]{2,1,0:T(8,128)S(1)}, f32[9,128,128]{2,1,0:T(8,128)S(1)}, u32[]{:S(2)}, u32[]{:S(2)}) collective-permute-start(f32[9,128,128]{2,1,0:T(8,128)S(1)} %shard_map.86), channel_id=1, source_target_pairs={{0,1},{1,2},{2,3},{3,4},{4,5},{5,6},{6,7},{7,8},{8,9},{9,10},{10,1... | collective-permute-start | bytes 1769480 | tf_op jit(solution)/shard_map/ppermute | solution.py:21
  7.9 1.6 %copy-start = (f32[2,2,64,2048]{3,2,1,0:T(8,128)S(1)}, f32[2,2,64,2048]{3,2,1,0:T(8,128)}, u32[]{:S(2)}) copy-start(f32[2,2,64,2048]{3,2,1,0:T(8,128)} %param.7) | copy-start | bytes 6291460
  9.5 5.2 %copy-start.1 = (f32[2,2,64,2048]{3,2,1,0:T(8,128)S(1)}, f32[2,2,64,2048]{3,2,1,0:T(8,128)}, u32[]{:S(2)}) copy-start(f32[2,2,64,2048]{3,2,1,0:T(8,128)} %param.7) | copy-start | bytes 6291460
  11.7 5.7 %collective-permute-start.2 = (f32[16,64,128]{2,1,0:T(8,128)}, f32[16,64,128]{2,1,0:T(8,128)}, u32[]{:S(2)}, u32[]{:S(2)}) collective-permute-start(f32[16,64,128]{2,1,0:T(8,128)} %get-tuple-element.50), channel_id=1, source_target_pairs={{0,1},{1,0},{2,3},{3,2},{4,5},{5,4},{6,7},{7,6},{8,9},{9,8},{10,11... | collective-permute-start | bytes 1572872 | tf_op jit(solution)/shard_map/ppermute | solution.py:360
  12.8 18.9 %collective-permute-start.3 = (f32[16,64,128]{2,1,0:T(8,128)}, f32[16,64,128]{2,1,0:T(8,128)}, u32[]{:S(2)}, u32[]{:S(2)}) collective-permute-start(f32[16,64,128]{2,1,0:T(8,128)} %get-tuple-element.51), channel_id=1, source_target_pairs={{0,15},{1,2},{2,1},{3,4},{4,3},{5,6},{6,5},{7,8},{8,7},{9,10},{10,... | collective-permute-start | bytes 1572872 | tf_op jit(solution)/shard_map/ppermute | solution.py:360
  14.2 17.5 %copy-start.3 = (f32[4,2,128,128]{3,2,1,0:T(8,128)S(1)}, f32[4,2,128,128]{3,2,1,0:T(8,128)}, u32[]{:S(2)}) copy-start(f32[4,2,128,128]{3,2,1,0:T(8,128)} %refs_5_.3) | copy-start | bytes 1572868
  14.3 17.4 %copy-start.4 = (bf16[8,256,256]{2,1,0:T(8,128)(2,1)S(1)}, bf16[8,256,256]{2,1,0:T(8,128)(2,1)}, u32[]{:S(2)}) copy-start(bf16[8,256,256]{2,1,0:T(8,128)(2,1)} %constant.2.clone.refs_7_) | copy-start | bytes 3145732
  31.7 14.5 %collective-permute-start.4 = (f32[16,64,128]{2,1,0:T(8,128)S(1)}, f32[16,64,128]{2,1,0:T(8,128)S(1)}, u32[]{:S(2)}, u32[]{:S(2)}) collective-permute-start(f32[16,64,128]{2,1,0:T(8,128)S(1)} %get-tuple-element.58), channel_id=1, source_target_pairs={{0,1},{1,0},{2,3},{3,2},{4,5},{5,4},{6,7},{7,6},{8,9},{9,8},{10,11... | collective-permute-start | bytes 1572872 | tf_op jit(solution)/shard_map/ppermute | solution.py:360
  31.7 14.5 %collective-permute-start.5 = (f32[16,64,128]{2,1,0:T(8,128)S(1)}, f32[16,64,128]{2,1,0:T(8,128)S(1)}, u32[]{:S(2)}, u32[]{:S(2)}) collective-permute-start(f32[16,64,128]{2,1,0:T(8,128)S(1)} %get-tuple-element.59), channel_id=1, source_target_pairs={{0,15},{1,2},{2,1},{3,4},{4,3},{5,6},{6,5},{7,8},{8,7},{9,10},{10,... | collective-permute-start | bytes 1572872 | tf_op jit(solution)/shard_map/ppermute | solution.py:360
  44.3 3.1 %collective-permute-start.6 = (f32[16,64,128]{2,1,0:T(8,128)S(1)}, f32[16,64,128]{2,1,0:T(8,128)S(1)}, u32[]{:S(2)}, u32[]{:S(2)}) collective-permute-start(f32[16,64,128]{2,1,0:T(8,128)S(1)} %get-tuple-element.66), channel_id=1, source_target_pairs={{0,1},{1,0},{2,3},{3,2},{4,5},{5,4},{6,7},{7,6},{8,9},{9,8},{10,11... | collective-permute-start | bytes 1572872 | tf_op jit(solution)/shard_map/ppermute | solution.py:360
  45.0 14.2 %collective-permute-start.7 = (f32[16,64,128]{2,1,0:T(8,128)S(1)}, f32[16,64,128]{2,1,0:T(8,128)S(1)}, u32[]{:S(2)}, u32[]{:S(2)}) collective-permute-start(f32[16,64,128]{2,1,0:T(8,128)S(1)} %get-tuple-element.67), channel_id=1, source_target_pairs={{0,15},{1,2},{2,1},{3,4},{4,3},{5,6},{6,5},{7,8},{8,7},{9,10},{10,... | collective-permute-start | bytes 1572872 | tf_op jit(solution)/shard_map/ppermute | solution.py:360
  59.2 1.7 %collective-permute-start.8 = (f32[8,9,8,128]{3,2,1,0:T(8,128)S(1)}, f32[8,9,8,128]{3,2,1,0:T(8,128)S(1)}, u32[]{:S(2)}, u32[]{:S(2)}) collective-permute-start(f32[8,9,8,128]{3,2,1,0:T(8,128)S(1)} %get-tuple-element.69), channel_id=1, source_target_pairs={{0,1},{1,0},{2,3},{3,2},{4,5},{5,4},{6,7},{7,6},{8,9},{9,8},{10,11... | collective-permute-start | bytes 884744 | tf_op jit(solution)/shard_map/ppermute | solution.py:424
  59.2 16.7 %collective-permute-start.9 = (f32[16,64,128]{2,1,0:T(8,128)S(1)}, f32[16,64,128]{2,1,0:T(8,128)S(1)}, u32[]{:S(2)}, u32[]{:S(2)}) collective-permute-start(f32[16,64,128]{2,1,0:T(8,128)S(1)} %get-tuple-element.74), channel_id=1, source_target_pairs={{0,1},{1,0},{2,3},{3,2},{4,5},{5,4},{6,7},{7,6},{8,9},{9,8},{10,11... | collective-permute-start | bytes 1572872 | tf_op jit(solution)/shard_map/ppermute | solution.py:360
  59.7 17.2 %collective-permute-start.10 = (f32[16,64,128]{2,1,0:T(8,128)S(1)}, f32[16,64,128]{2,1,0:T(8,128)S(1)}, u32[]{:S(2)}, u32[]{:S(2)}) collective-permute-start(f32[16,64,128]{2,1,0:T(8,128)S(1)} %get-tuple-element.75), channel_id=1, source_target_pairs={{0,15},{1,2},{2,1},{3,4},{4,3},{5,6},{6,5},{7,8},{8,7},{9,10},{10,... | collective-permute-start | bytes 1572872 | tf_op jit(solution)/shard_map/ppermute | solution.py:360
  89.4 6.5 %collective-permute-start.11 = (f32[8,8,8,128]{3,2,1,0:T(8,128)S(1)}, f32[8,8,8,128]{3,2,1,0:T(8,128)S(1)}, u32[]{:S(2)}, u32[]{:S(2)}) collective-permute-start(f32[8,8,8,128]{3,2,1,0:T(8,128)S(1)} %all_to_all.11.own), channel_id=1, source_target_pairs={{0,1},{1,0},{2,3},{3,2},{4,5},{5,4},{6,7},{7,6},{8,9},{9,8},{10,11... | collective-permute-start | bytes 786440 | tf_op jit(solution)/shard_map/ppermute | solution.py:448

commit v5 on v4

--- a/solution.py
+++ b/solution.py
@@ -10,7 +10,7 @@
 
 CHUNKS = (4, 4)
 BATCH = 4
-VMEM_LIMIT = 32 * 1024 * 1024
+VMEM_LIMIT = 20 * 1024 * 1024
 ROW = ("chip", "core")
 F32 = jnp.float32
 BF16 = jnp.bfloat16
@@ -163,6 +163,21 @@
             cross[strip : strip + planes] = cut(tile, jnp.where(even, far[slot, 1], own[slot, 1]), pixels)
 
 
+def own_kernel(pixels, own, tile, out):
+    planes = tile.shape[0]
+    for at in range(out.shape[0] // planes):
+        out[at * planes : (at + 1) * planes] = cut(tile, own[at, 1], pixels)
+
+
+def far_kernel(pixels, own, far, tile, up, near, down):
+    planes, rows, _ = tile.shape
+    even = is_even(own, rows)
+    for at in range(up.shape[0] // planes):
+        strip = slice(at * planes, (at + 1) * planes)
+        down[strip] = cut(tile, far[at, 1], pixels)
+        near[strip] = jnp.where(even, up[strip], down[strip])
+
+
 def add_kernel(pixels, groups, own, middle, far, *refs):
     *parts, out = refs
     planes, rows, _ = out.shape
@@ -191,7 +206,7 @@
 
 
 def slot_kernel(first, size, ahead, own_offsets, *refs):
-    offsets, mid, near, cross, target, probe, prop, tables, *refs = refs
+    offsets, mid, near, even_cross, odd_cross, target, probe, prop, tables, *refs = refs
     so_far, refs = (refs[0], refs[1:]) if first else (None, refs)
     given, refs = refs[:ahead], refs[ahead:]
     out_near, out_mid, out_cross, *shares = refs[:-5]
@@ -219,9 +234,9 @@
         live = [jnp.where(is_live(at), 1.0, 0.0).astype(F32) for at in slots]
         for s, at in enumerate(slots):
             strip = pl.ds(at * planes, planes)
-            window[:, :rows] = jnp.where(even, cross[strip], near[strip])
+            window[:, :rows] = jnp.where(even, even_cross[strip], near[strip])
             window[:, rows : 2 * rows] = mid[strip]
-            window[:, 2 * rows :] = jnp.where(even, near[strip], cross[strip])
+            window[:, 2 * rows :] = jnp.where(even, near[strip], odd_cross[strip])
             patch[s] = window[:, pl.ds(starts[s], pixels), :]
             total[2 * modes] += live[s] * (patch[s, 0] * patch[s, 0] + patch[s, 1] * patch[s, 1])
         all_modes = range(modes)
@@ -338,11 +353,25 @@
         compiler_params=params,
         cost_estimate=pl.CostEstimate(flops=0, bytes_accessed=1 << 20, transcendentals=0),
     )(offsets, counts, measured)
-    far, target = lax.optimization_barrier((far, target))
-    target = shifted(target, ROW, 1)
-
     def units(count):
         return jax.ShapeDtypeStruct((count, tile_rows, pixels), F32)
+
+    first_units = units(CHUNKS[0] * planes)
+
+    def cut_first(kernel, inputs, outputs):
+        return pl.pallas_call(
+            functools.partial(kernel, pixels),
+            out_shape=[first_units] * outputs,
+            in_specs=[in_smem() if part.dtype == jnp.int32 else in_vmem() for part in inputs],
+            out_specs=[in_vmem()] * outputs,
+            compiler_params=params,
+            cost_estimate=pl.CostEstimate(flops=0, bytes_accessed=3 << 20, transcendentals=0),
+        )(*inputs)
+
+    (up,) = cut_first(own_kernel, (offsets, tile), 1)
+    from_odd = lax.ppermute(up, ROW, other_pair[1::2])
+    far, target, up = lax.optimization_barrier((far, target, up))
+    target = shifted(target, ROW, 1)
 
     def strips(chunks, far):
         shapes = [units(size * planes) for _, size in chunks for _ in range(2)]
@@ -359,8 +388,11 @@
     def swapped(to_near, to_cross):
         return lax.ppermute(to_near, ROW, pair), lax.ppermute(to_cross, ROW, other_pair)
 
+    to_near, down = cut_first(far_kernel, (offsets, far, tile, up), 2)
+    from_even = lax.ppermute(down, ROW, other_pair[0::2])
+    arrived = [(lax.ppermute(to_near, ROW, pair), from_odd, from_even)]
     far_later, target = lax.optimization_barrier((far, target))
-    waiting = strips(chunks[:1], far) + strips(chunks[1:], far_later)
+    waiting = strips(chunks[1:], far_later)
     *middles, middle = pl.pallas_call(
         functools.partial(middle_kernel, pixels),
         out_shape=[units(size * planes) for size in CHUNKS] + [jax.ShapeDtypeStruct(offsets.shape, jnp.int32)],
@@ -369,10 +401,10 @@
         compiler_params=params,
         cost_estimate=pl.CostEstimate(flops=0, bytes_accessed=4 << 20, transcendentals=0),
     )(target, tile)
-    arrived = [swapped(*waiting[0])]
-    if len(waiting) > 1:
-        arrived[0], following, middles = lax.optimization_barrier((arrived[0], waiting[1], middles))
-        arrived.append(swapped(*following))
+    for message in waiting:
+        arrived[-1], message, middles = lax.optimization_barrier((arrived[-1], message, middles))
+        to_near, to_cross = swapped(*message)
+        arrived.append((to_near, to_cross, to_cross))
     phase = jnp.concatenate([propagator_phase[0::2], propagator_phase[1::2]], axis=0)
     prop = jnp.stack([jnp.cos(phase), jnp.sin(phase)])
     tables = jnp.asarray(fourier_tables(pixels))
@@ -381,8 +413,7 @@
     total = ()
     mid, back, mid_groups, back_groups = [], [], [], []
     for index, (first, size) in enumerate(chunks):
-        given = waiting[index + 2] if index + 2 < len(chunks) else ()
-        ahead = CHUNKS[index + 2] * planes if given else 0
+        given, ahead = (), 0
         sums = jax.ShapeDtypeStruct((2 * modes + 1, pixels, pixels), F32)
         part = jax.ShapeDtypeStruct((peers // 2, 2 * modes + 1, share, pixels), F32)
         shares = [part, part] if index == len(CHUNKS) - 1 else []
@@ -392,7 +423,7 @@
         to_near, to_mid, to_cross, *total = pl.pallas_call(
             functools.partial(slot_kernel, first, size, len(given)),
             out_shape=[message, units(size * planes), message] + (shares or [sums]),
-            in_specs=[in_smem()] * 2 + [in_vmem()] * (7 + len(total) + len(given)),
+            in_specs=[in_smem()] * 2 + [in_vmem()] * (8 + len(total) + len(given)),
             out_specs=[in_vmem()] * (3 + (len(shares) or 1)),
             scratch_shapes=([pltpu.VMEM(sums.shape, F32)] if shares else [])
             + [pltpu.VMEM((planes, 3 * tile_rows, pixels), F32), field, field, kept, kept],
@@ -404,8 +435,6 @@
         mid_groups.append(("mid", first, size, 0))
         mid.append(to_mid)
         message = swapped(to_near, to_cross)
-        if given:
-            arrived.append(message)
         back_groups += [(kind, first, size, ahead) for kind in ("near", "cross")]
         back.append(message)
 

time: 97.8 us -> 98 us (level)
  waiting for transfers between devices: 29.3 us -> 25.1 us
  starting transfers between devices: 11 us -> 14.1 us
  Pallas kernels: 24.5 us -> 27 us
    ppermute x4 -> x3, waiting for transfers between devices: 27.1 us -> 12.6 us  [swapped(): lax.ppermute(to_cross, ROW, other_pair)]
    ppermute x0 -> x3, waiting for transfers between devices: none -> 11.6 us  [the longest x1 7.55 us: local(): from_odd = lax.ppermute(up, ROW, other_pair[1::2])]
    ppermute x0 -> x3, starting transfers between devices: none -> 4 us  [the longest x1 2.72 us: local(): from_odd = lax.ppermute(up, ROW, other_pair[1::2])]
    pallas_call x0 -> x2, Pallas kernels: none -> 2.93 us  [cut_first(): pl.pallas_call(functools.partial(kernel, pixels), out_shape=[first_units]...]
    pallas_call x2 -> x1, Pallas kernels: 3.48 us -> 1.29 us  [strips(): pl.pallas_call(functools.partial(cut_kernel, pixels, chunks), out_shape=s...]
    ppermute x4 -> x3, starting transfers between devices: 3.53 us -> 1.72 us  [swapped(): lax.ppermute(to_cross, ROW, other_pair)]
    ppermute x2, waiting for transfers between devices: 2.19 us -> 0.59 us  [shifted(): lax.ppermute(array, axis, [(i, (i + by) % peers) for i in range(peers)])]
    ppermute x2, starting transfers between devices: 2.53 us -> 4.12 us  [shifted(): lax.ppermute(array, axis, [(i, (i + by) % peers) for i in range(peers)])]
  transfers between devices with their start and end apart: 12 -> 13, of which waited for: 5 -> 7; matrix products, arithmetic and copies ran while one was open for 0% -> 0% of each run, Pallas kernels for 24% -> 26%
where the time goes in v5:
time: 98 us; the launch traced here: 97.6 us
  blocking collectives  27.2 us (28%)
  Pallas kernels  27 us (28%)
  waiting for transfers between devices  25.1 us (26%)
  starting transfers between devices  14.1 us (14%)
  local copies, waits for them, and re-layouts  2.47 us (3%)
  between operations  1.44 us (1%)
    all_to_all x1, blocking collectives, local(): parts = lax.all_to_all(both, 'chip', 0, 0)  15.1 us
    pallas_call x2, Pallas kernels, local(): pl.pallas_call(functools.partial(slot_kernel, first, size, len(given)), o...  14.5 us
    ppermute x3, waiting for transfers between devices, swapped(): lax.ppermute(to_cross, ROW, other_pair)  12.6 us
    all_to_all x1, blocking collectives, local(): gathered = lax.all_to_all(spread, 'chip', 0, 0)  12.1 us
    ppermute x1, waiting for transfers between devices, local(): from_odd = lax.ppermute(up, ROW, other_pair[1::2])  7.55 us
    ppermute x2, starting transfers between devices, shifted(): lax.ppermute(array, axis, [(i, (i + by) % peers) for i in range(peers)])  4.12 us
    ppermute x1, waiting for transfers between devices, local(): from_even = lax.ppermute(down, ROW, other_pair[0::2])  4.08 us
    pallas_call x1, Pallas kernels, added(): pl.pallas_call(functools.partial(add_kernel, pixels, groups), out_shape=j...  3.78 us
  transfers between devices with their start and end apart: 13, of which 7 were waited for; matrix products, arithmetic and copies ran while one was open for 0% of the time, Pallas kernels for 26%

profile of v5, /device:TPU:1, one launch (start us, length us, event | category | flops | bytes accessed | tf_op | source)
XLA Modules:
  0.0 97.6 jit_solution(10115575538986042962)
XLA Ops:
  0.6 0.8 copy.16.offsets.own.own_offsets
  1.4 2.1 %collective-permute-start = (s32[8,2]{1,0:T(8,128)S(1)}, s32[8,2]{1,0:T(8,128)S(1)}, u32[]{:S(2)}, u32[]{:S(2)}) collective-permute-start(s32[8,2]{1,0:T(8,128)S(1)} %copy.16.offsets.own.own_offsets), channel_id=1, source_target_pairs={{0,2},{1,3},{2,4},{3,5},{4,6},{5,7},{6,8},{7,9},{8,10},{9,11},{10,... | collective-permute-start | bytes 200 | tf_op jit(solution)/shard_map/ppermute | solution.py:21
  4.1 0.0 copy-start
  4.1 1.6 %copy-done = f32[2,2,64,2048]{3,2,1,0:T(8,128)S(1)} copy-done((f32[2,2,64,2048]{3,2,1,0:T(8,128)S(1)}, f32[2,2,64,2048]{3,2,1,0:T(8,128)}, u32[]{:S(2)}) %copy-start) | copy-done | bytes 2097176
  5.7 0.9 shard_map.87.up
  6.7 0.1 copy-done.2
  6.7 0.6 shard_map.86
  7.4 0.1 collective-permute-done.far
  7.5 2.1 %collective-permute-start.1 = (f32[9,128,128]{2,1,0:T(8,128)S(1)}, f32[9,128,128]{2,1,0:T(8,128)}, u32[]{:S(2)}, u32[]{:S(2)}) collective-permute-start(f32[9,128,128]{2,1,0:T(8,128)S(1)} %shard_map.86), channel_id=1, source_target_pairs={{0,1},{1,2},{2,3},{3,4},{4,5},{5,6},{6,7},{7,8},{8,9},{9,10},{10,1... | collective-permute-start | bytes 1769480 | tf_op jit(solution)/shard_map/ppermute | solution.py:21
  9.5 2.7 %collective-permute-start.3 = (f32[16,64,128]{2,1,0:T(8,128)S(1)}, f32[16,64,128]{2,1,0:T(8,128)}, u32[]{:S(2)}, u32[]{:S(2)}) collective-permute-start(f32[16,64,128]{2,1,0:T(8,128)S(1)} %shard_map.87.up), channel_id=1, source_target_pairs={{1,2},{3,4},{5,6},{7,8},{9,10},{11,12},{13,14},{15,0},{17,18},{19,... | collective-permute-start | bytes 1572872 | tf_op jit(solution)/shard_map/ppermute | solution.py:372
  12.3 0.0 copy-done.1
  12.3 2.0 %shard_map.89 = (f32[16,64,128]{2,1,0:T(8,128)}, f32[16,64,128]{2,1,0:T(8,128)}) custom-call(s32[8,2]{1,0:T(8,128)S(1)} %copy.16.offsets.own.own_offsets, s32[8,2]{1,0:T(8,128)S(1)} %collective-permute-done.far, f32[4,64,2048]{2,1,0:T(8,128)S(1)} %bitcast.6, f32[16,64,128]{2,1,0:T(8,128)S(1)} %shard_map.87.up), custom_call_target="tpu_custom_call" | custom-call | bytes 3145728 | tf_op jit(solution)/shard_map/pallas_call | solution.py:362
  14.2 0.0 collective-permute-start.2
  14.2 1.3 %collective-permute-start.4 = (f32[16,64,128]{2,1,0:T(8,128)}, f32[16,64,128]{2,1,0:T(8,128)}, u32[]{:S(2)}, u32[]{:S(2)}) collective-permute-start(f32[16,64,128]{2,1,0:T(8,128)} %get-tuple-element.54), channel_id=1, source_target_pairs={{0,15},{2,1},{4,3},{6,5},{8,7},{10,9},{12,11},{14,13},{16,31},{18,... | collective-permute-start | bytes 1572872 | tf_op jit(solution)/shard_map/ppermute | solution.py:392
  15.5 0.0 copy-done.5
  15.6 0.2 fusion.1
  15.8 0.0 copy-start.3
  15.9 0.0 copy-start.4
  15.9 0.5 collective-permute-done.1.target.refs_5_
  16.4 1.3 %shard_map.90 = (f32[16,64,128]{2,1,0:T(8,128)S(1)}, f32[16,64,128]{2,1,0:T(8,128)S(1)}) custom-call(s32[8,2]{1,0:T(8,128)S(1)} %copy.16.offsets.own.own_offsets, s32[8,2]{1,0:T(8,128)S(1)} %collective-permute-done.far, f32[4,64,2048]{2,1,0:T(8,128)S(1)} %bitcast.7), custom_call_target="tpu_custom_call" | custom-call | bytes 4194304 | tf_op jit(solution)/shard_map/pallas_call | solution.py:378
  17.7 2.4 %shard_map.88 = (f32[16,64,128]{2,1,0:T(8,128)S(1)}, f32[16,64,128]{2,1,0:T(8,128)S(1)}, s32[8,2]{1,0:T(8,128)S(1)}) custom-call(f32[9,128,128]{2,1,0:T(8,128)} %collective-permute-done.1.target.refs_5_, f32[4,64,2048]{2,1,0:T(8,128)S(1)} %bitcast.8), custom_call_target="tpu_custom_call" | custom-call | bytes 4194304 | tf_op jit(solution)/shard_map/pallas_call | solution.py:396
  20.0 7.6 %collective-permute-done.3.refs_3_ = f32[16,64,128]{2,1,0:T(8,128)} collective-permute-done((f32[16,64,128]{2,1,0:T(8,128)S(1)}, f32[16,64,128]{2,1,0:T(8,128)}, u32[]{:S(2)}, u32[]{:S(2)}) %collective-permute-start.3) | collective-permute-done | bytes 524320 | tf_op jit(solution)/shard_map/ppermute | solution.py:372
  27.6 0.0 collective-permute-done.2.refs_2_
  27.6 4.1 %collective-permute-done.4.refs_4_ = f32[16,64,128]{2,1,0:T(8,128)} collective-permute-done((f32[16,64,128]{2,1,0:T(8,128)}, f32[16,64,128]{2,1,0:T(8,128)}, u32[]{:S(2)}, u32[]{:S(2)}) %collective-permute-start.4) | collective-permute-done | bytes 524320 | tf_op jit(solution)/shard_map/ppermute | solution.py:392
  31.7 0.0 collective-permute-start.5
  31.7 0.0 collective-permute-start.6
  31.7 0.0 copy-done.3
  31.7 0.0 copy-done.4
  31.7 12.9 %shard_map.91 = (f32[16,64,128]{2,1,0:T(8,128)S(1)}, f32[16,64,128]{2,1,0:T(8,128)S(1)}, f32[16,64,128]{2,1,0:T(8,128)S(1)}, f32[9,128,128]{2,1,0:T(8,128)S(1)}) custom-call(s32[8,2]{1,0:T(8,128)S(1)} %copy.16.offsets.own.own_offsets, s32[8,2]{1,0:T(8,128)S(1)} %get-tuple-element.51.refs_0_.middle, f32[16,64,128]{2,1,0:T(8,128)S(1)} %get-tuple-element.63.refs_1_, ...), custom_call_target="tpu_custom_call" | custom-call | flops 9663676416 | bytes 8388608 | tf_op jit(solution)/shard_map/pallas_call | solution.py:423
  44.6 1.0 %collective-permute-start.7 = (f32[16,64,128]{2,1,0:T(8,128)S(1)}, f32[16,64,128]{2,1,0:T(8,128)S(1)}, u32[]{:S(2)}, u32[]{:S(2)}) collective-permute-start(f32[16,64,128]{2,1,0:T(8,128)S(1)} %get-tuple-element.70), channel_id=1, source_target_pairs={{0,1},{1,0},{2,3},{3,2},{4,5},{5,4},{6,7},{7,6},{8,9},{9,8},{10,11... | collective-permute-start | bytes 1572872 | tf_op jit(solution)/shard_map/ppermute | solution.py:389
  45.7 0.9 collective-permute-start.8
  46.5 0.0 collective-permute-done.5.refs_2_
  46.5 0.0 collective-permute-done.6.refs_3_.refs_4_
  46.5 1.6 %shard_map.92 = (f32[16,64,128]{2,1,0:T(8,128)S(1)}, f32[16,64,128]{2,1,0:T(8,128)S(1)}, f32[16,64,128]{2,1,0:T(8,128)S(1)}, f32[8,9,8,128]{3,2,1,0:T(8,128)S(1)}, f32[8,9,8,128]{3,2,1,0:T(8,128)S(1)}) custom-call(s32[8,2]{1,0:T(8,128)S(1)} %copy.16.offsets.own.own_offsets, s32[8,2]{1,0:T(8,128)S(1)} %get-tuple-element.51.refs_0_.middle, ...), custom_call_target="tpu_custom_call" | custom-call | flops 9663676416 | bytes 8388608 | tf_op jit(solution)/shard_map/pallas_call | solution.py:423
  48.1 0.0 collective-permute-done.7.refs_2_
  48.2 11.7 %collective-permute-done.8.refs_3_ = f32[16,64,128]{2,1,0:T(8,128)S(1)} collective-permute-done((f32[16,64,128]{2,1,0:T(8,128)S(1)}, f32[16,64,128]{2,1,0:T(8,128)S(1)}, u32[]{:S(2)}, u32[]{:S(2)}) %collective-permute-start.8) | collective-permute-done | bytes 524320 | tf_op jit(solution)/shard_map/ppermute | solution.py:389
  59.9 0.0 collective-permute-start.9
  59.9 0.5 collective-permute-start.10
  60.4 0.9 collective-permute-start.11
  61.3 0.2 collective-permute-done.9
  61.5 15.1 %all_to_all.10.parts = f32[8,9,8,128]{3,2,1,0:T(8,128)S(1)} all-to-all(f32[8,9,8,128]{3,2,1,0:T(8,128)S(1)} %add.3), channel_id=1, replica_groups=mesh['grp'=2,'chip'=8,'core'=2] {'chip'}, dimensions={0} | all-to-all | bytes 589824 | tf_op jit(solution)/shard_map/all_to_all | solution.py:454
  76.6 0.0 collective-permute-done.10.refs_4_
  76.7 0.9 collective-permute-done.11.refs_5_
  77.6 12.1 %all_to_all.11.own = f32[8,8,8,128]{3,2,1,0:T(8,128)S(1)} all-to-all(f32[8,8,8,128]{3,2,1,0:T(8,128)S(1)} %shard_map.93), channel_id=1, replica_groups=mesh['grp'=2,'chip'=8,'core'=2] {'chip'}, dimensions={0} | all-to-all | bytes 524288 | tf_op jit(solution)/shard_map/all_to_all | solution.py:465
  89.7 2.7 %collective-permute-start.12 = (f32[8,8,8,128]{3,2,1,0:T(8,128)S(1)}, f32[8,8,8,128]{3,2,1,0:T(8,128)S(1)}, u32[]{:S(2)}, u32[]{:S(2)}) collective-permute-start(f32[8,8,8,128]{3,2,1,0:T(8,128)S(1)} %all_to_all.11.own), channel_id=1, source_target_pairs={{0,1},{1,0},{2,3},{3,2},{4,5},{5,4},{6,7},{7,6},{8,9},{9,8},{10,11... | collective-permute-start | bytes 786440 | tf_op jit(solution)/shard_map/ppermute | solution.py:477
  92.4 3.8 %shard_map.94 = f32[4,64,2048]{2,1,0:T(8,128)} custom-call(s32[8,2]{1,0:T(8,128)S(1)} %copy.16.offsets.own.own_offsets, s32[8,2]{1,0:T(8,128)S(1)} %get-tuple-element.51.refs_0_.middle, s32[8,2]{1,0:T(8,128)S(1)} %collective-permute-done.far, f32[16,64,128]{2,1,0:T(8,128)S(1)} %get-tuple-element.87.refs_0_, f32[16,64,128]{2,1,0:T(8,128)S(1)} %get-tuple-element.88.refs_1_, ...), custom_call_target="tpu_custom_call" | custom-call | bytes 5242880 | tf_op jit(solution)/shard_map/pallas_call | solution.py:442
  96.2 0.0 collective-permute-done.12.other
  96.2 1.5 %shard_map.95 = f32[8,128,128]{2,1,0:T(8,128)} custom-call(s32[8,2]{1,0:T(8,128)S(1)} %copy.16.offsets.own.own_offsets, f32[8,8,8,128]{3,2,1,0:T(8,128)S(1)} %all_to_all.11.own, f32[8,8,8,128]{3,2,1,0:T(8,128)S(1)} %collective-permute-done.12.other), custom_call_target="tpu_custom_call" | custom-call | tf_op jit(solution)/shard_map/pallas_call | solution.py:471
  (8 shorter events, 0.1 us)
Async XLA Ops:
  1.4 6.1 %collective-permute-start = (s32[8,2]{1,0:T(8,128)S(1)}, s32[8,2]{1,0:T(8,128)S(1)}, u32[]{:S(2)}, u32[]{:S(2)}) collective-permute-start(s32[8,2]{1,0:T(8,128)S(1)} %copy.16.offsets.own.own_offsets), channel_id=1, source_target_pairs={{0,2},{1,3},{2,4},{3,5},{4,6},{5,7},{6,8},{7,9},{8,10},{9,11},{10,... | collective-permute-start | bytes 200 | tf_op jit(solution)/shard_map/ppermute | solution.py:21
  4.1 1.6 %copy-start = (f32[2,2,64,2048]{3,2,1,0:T(8,128)S(1)}, f32[2,2,64,2048]{3,2,1,0:T(8,128)}, u32[]{:S(2)}) copy-start(f32[2,2,64,2048]{3,2,1,0:T(8,128)} %param.7) | copy-start | bytes 6291460
  5.7 1.0 %copy-start.2 = (f32[8,128,128]{2,1,0:T(8,128)S(1)}, f32[8,128,128]{2,1,0:T(8,128)}, u32[]{:S(2)}) copy-start(f32[8,128,128]{2,1,0:T(8,128)} %measured.1) | copy-start | bytes 1572868
  5.7 6.6 %copy-start.1 = (f32[2,2,64,2048]{3,2,1,0:T(8,128)S(1)}, f32[2,2,64,2048]{3,2,1,0:T(8,128)}, u32[]{:S(2)}) copy-start(f32[2,2,64,2048]{3,2,1,0:T(8,128)} %param.7) | copy-start | bytes 6291460
  6.7 8.8 %copy-start.5 = (f32[128,128]{1,0:T(8,128)S(1)}, f32[128,128]{1,0:T(8,128)}, u32[]{:S(2)}) copy-start(f32[128,128]{1,0:T(8,128)} %param.9) | copy-start | bytes 196612
  7.5 8.9 %collective-permute-start.1 = (f32[9,128,128]{2,1,0:T(8,128)S(1)}, f32[9,128,128]{2,1,0:T(8,128)}, u32[]{:S(2)}, u32[]{:S(2)}) collective-permute-start(f32[9,128,128]{2,1,0:T(8,128)S(1)} %shard_map.86), channel_id=1, source_target_pairs={{0,1},{1,2},{2,3},{3,4},{4,5},{5,6},{6,7},{7,8},{8,9},{9,10},{10,1... | collective-permute-start | bytes 1769480 | tf_op jit(solution)/shard_map/ppermute | solution.py:21
  9.5 18.1 %collective-permute-start.3 = (f32[16,64,128]{2,1,0:T(8,128)S(1)}, f32[16,64,128]{2,1,0:T(8,128)}, u32[]{:S(2)}, u32[]{:S(2)}) collective-permute-start(f32[16,64,128]{2,1,0:T(8,128)S(1)} %shard_map.87.up), channel_id=1, source_target_pairs={{1,2},{3,4},{5,6},{7,8},{9,10},{11,12},{13,14},{15,0},{17,18},{19,... | collective-permute-start | bytes 1572872 | tf_op jit(solution)/shard_map/ppermute | solution.py:372
  14.2 13.4 %collective-permute-start.2 = (f32[16,64,128]{2,1,0:T(8,128)}, f32[16,64,128]{2,1,0:T(8,128)}, u32[]{:S(2)}, u32[]{:S(2)}) collective-permute-start(f32[16,64,128]{2,1,0:T(8,128)} %get-tuple-element.53), channel_id=1, source_target_pairs={{0,1},{1,0},{2,3},{3,2},{4,5},{5,4},{6,7},{7,6},{8,9},{9,8},{10,11... | collective-permute-start | bytes 1572872 | tf_op jit(solution)/shard_map/ppermute | solution.py:393
  14.2 17.4 %collective-permute-start.4 = (f32[16,64,128]{2,1,0:T(8,128)}, f32[16,64,128]{2,1,0:T(8,128)}, u32[]{:S(2)}, u32[]{:S(2)}) collective-permute-start(f32[16,64,128]{2,1,0:T(8,128)} %get-tuple-element.54), channel_id=1, source_target_pairs={{0,15},{2,1},{4,3},{6,5},{8,7},{10,9},{12,11},{14,13},{16,31},{18,... | collective-permute-start | bytes 1572872 | tf_op jit(solution)/shard_map/ppermute | solution.py:392
  15.8 15.9 %copy-start.3 = (f32[4,2,128,128]{3,2,1,0:T(8,128)S(1)}, f32[4,2,128,128]{3,2,1,0:T(8,128)}, u32[]{:S(2)}) copy-start(f32[4,2,128,128]{3,2,1,0:T(8,128)} %refs_6_.3) | copy-start | bytes 1572868
  15.9 15.8 %copy-start.4 = (bf16[8,256,256]{2,1,0:T(8,128)(2,1)S(1)}, bf16[8,256,256]{2,1,0:T(8,128)(2,1)}, u32[]{:S(2)}) copy-start(bf16[8,256,256]{2,1,0:T(8,128)(2,1)} %constant.2.clone.refs_8_) | copy-start | bytes 3145732
  31.7 14.8 %collective-permute-start.5 = (f32[16,64,128]{2,1,0:T(8,128)S(1)}, f32[16,64,128]{2,1,0:T(8,128)S(1)}, u32[]{:S(2)}, u32[]{:S(2)}) collective-permute-start(f32[16,64,128]{2,1,0:T(8,128)S(1)} %get-tuple-element.61), channel_id=1, source_target_pairs={{0,1},{1,0},{2,3},{3,2},{4,5},{5,4},{6,7},{7,6},{8,9},{9,8},{10,11... | collective-permute-start | bytes 1572872 | tf_op jit(solution)/shard_map/ppermute | solution.py:389
  31.7 14.8 %collective-permute-start.6 = (f32[16,64,128]{2,1,0:T(8,128)S(1)}, f32[16,64,128]{2,1,0:T(8,128)S(1)}, u32[]{:S(2)}, u32[]{:S(2)}) collective-permute-start(f32[16,64,128]{2,1,0:T(8,128)S(1)} %get-tuple-element.62), channel_id=1, source_target_pairs={{0,15},{1,2},{2,1},{3,4},{4,3},{5,6},{6,5},{7,8},{8,7},{9,10},{10,... | collective-permute-start | bytes 1572872 | tf_op jit(solution)/shard_map/ppermute | solution.py:389
  44.6 3.5 %collective-permute-start.7 = (f32[16,64,128]{2,1,0:T(8,128)S(1)}, f32[16,64,128]{2,1,0:T(8,128)S(1)}, u32[]{:S(2)}, u32[]{:S(2)}) collective-permute-start(f32[16,64,128]{2,1,0:T(8,128)S(1)} %get-tuple-element.70), channel_id=1, source_target_pairs={{0,1},{1,0},{2,3},{3,2},{4,5},{5,4},{6,7},{7,6},{8,9},{9,8},{10,11... | collective-permute-start | bytes 1572872 | tf_op jit(solution)/shard_map/ppermute | solution.py:389
  45.7 14.2 %collective-permute-start.8 = (f32[16,64,128]{2,1,0:T(8,128)S(1)}, f32[16,64,128]{2,1,0:T(8,128)S(1)}, u32[]{:S(2)}, u32[]{:S(2)}) collective-permute-start(f32[16,64,128]{2,1,0:T(8,128)S(1)} %get-tuple-element.71), channel_id=1, source_target_pairs={{0,15},{1,2},{2,1},{3,4},{4,3},{5,6},{6,5},{7,8},{8,7},{9,10},{10,... | collective-permute-start | bytes 1572872 | tf_op jit(solution)/shard_map/ppermute | solution.py:389
  59.9 1.6 %collective-permute-start.9 = (f32[8,9,8,128]{3,2,1,0:T(8,128)S(1)}, f32[8,9,8,128]{3,2,1,0:T(8,128)S(1)}, u32[]{:S(2)}, u32[]{:S(2)}) collective-permute-start(f32[8,9,8,128]{3,2,1,0:T(8,128)S(1)} %get-tuple-element.73), channel_id=1, source_target_pairs={{0,1},{1,0},{2,3},{3,2},{4,5},{5,4},{6,7},{7,6},{8,9},{9,8},{10,11... | collective-permute-start | bytes 884744 | tf_op jit(solution)/shard_map/ppermute | solution.py:453
  59.9 16.8 %collective-permute-start.10 = (f32[16,64,128]{2,1,0:T(8,128)S(1)}, f32[16,64,128]{2,1,0:T(8,128)S(1)}, u32[]{:S(2)}, u32[]{:S(2)}) collective-permute-start(f32[16,64,128]{2,1,0:T(8,128)S(1)} %get-tuple-element.78), channel_id=1, source_target_pairs={{0,1},{1,0},{2,3},{3,2},{4,5},{5,4},{6,7},{7,6},{8,9},{9,8},{10,11... | collective-permute-start | bytes 1572872 | tf_op jit(solution)/shard_map/ppermute | solution.py:389
  60.4 17.2 %collective-permute-start.11 = (f32[16,64,128]{2,1,0:T(8,128)S(1)}, f32[16,64,128]{2,1,0:T(8,128)S(1)}, u32[]{:S(2)}, u32[]{:S(2)}) collective-permute-start(f32[16,64,128]{2,1,0:T(8,128)S(1)} %get-tuple-element.79), channel_id=1, source_target_pairs={{0,15},{1,2},{2,1},{3,4},{4,3},{5,6},{6,5},{7,8},{8,7},{9,10},{10,... | collective-permute-start | bytes 1572872 | tf_op jit(solution)/shard_map/ppermute | solution.py:389
  89.7 6.5 %collective-permute-start.12 = (f32[8,8,8,128]{3,2,1,0:T(8,128)S(1)}, f32[8,8,8,128]{3,2,1,0:T(8,128)S(1)}, u32[]{:S(2)}, u32[]{:S(2)}) collective-permute-start(f32[8,8,8,128]{3,2,1,0:T(8,128)S(1)} %all_to_all.11.own), channel_id=1, source_target_pairs={{0,1},{1,0},{2,3},{3,2},{4,5},{5,4},{6,7},{7,6},{8,9},{9,8},{10,11... | collective-permute-start | bytes 786440 | tf_op jit(solution)/shard_map/ppermute | solution.py:477

commit v6 on v4

--- a/solution.py
+++ b/solution.py
@@ -10,7 +10,7 @@
 
 CHUNKS = (4, 4)
 BATCH = 4
-VMEM_LIMIT = 32 * 1024 * 1024
+VMEM_LIMIT = 40 * 1024 * 1024
 ROW = ("chip", "core")
 F32 = jnp.float32
 BF16 = jnp.bfloat16
@@ -434,9 +434,8 @@
     strips = mid + [part for message in back for part in message]
     spread, strips = lax.optimization_barrier((spread, strips))
     gathered = lax.all_to_all(spread, "chip", 0, 0)
-    gathered, strips = lax.optimization_barrier((gathered, strips))
-
     object_grad = added(groups, strips)
+    gathered, object_grad = lax.optimization_barrier((gathered, object_grad))
     object_grad = object_grad.reshape(object_slices.shape)
 
     probe_step = pl.pallas_call(

time: 97.8 us -> 96.4 us (0.986)
  blocking collectives: 27.3 us -> 14.9 us
  starting transfers between devices: 11 us -> 17.3 us
  waiting for transfers between devices: 29.3 us -> 33.1 us
    all_to_all x1 -> x0, blocking collectives: 12.5 us -> none  [local(): gathered = lax.all_to_all(spread, 'chip', 0, 0)]
    all_to_all x0 -> x1, starting transfers between devices: none -> 6.22 us  [local(): gathered = lax.all_to_all(spread, 'chip', 0, 0)]
    all_to_all x0 -> x1, waiting for transfers between devices: none -> 3.38 us  [local(): gathered = lax.all_to_all(spread, 'chip', 0, 0)]
    ppermute x1, waiting for transfers between devices: 0.01 us -> 1.16 us  [local(): lax.ppermute(gathered, ROW, pair)]
  transfers between devices with their start and end apart: 12 -> 13, of which waited for: 5 -> 7; matrix products, arithmetic and copies ran while one was open for 0% -> 0% of each run, Pallas kernels for 24% -> 25%
where the time goes in v6:
time: 96.4 us; the launch traced here: 95.5 us
  waiting for transfers between devices  33.1 us (34%)
  Pallas kernels  25.1 us (26%)
  starting transfers between devices  17.3 us (18%)
  blocking collectives  14.9 us (15%)
  local copies, waits for them, and re-layouts  3.43 us (4%)
  between operations  1.41 us (1%)
    ppermute x4, waiting for transfers between devices, swapped(): lax.ppermute(to_cross, ROW, other_pair)  26.4 us
    all_to_all x1, blocking collectives, local(): parts = lax.all_to_all(both, 'chip', 0, 0)  14.9 us
    pallas_call x2, Pallas kernels, local(): pl.pallas_call(functools.partial(slot_kernel, first, size, len(given)), o...  13.7 us
    all_to_all x1, starting transfers between devices, local(): gathered = lax.all_to_all(spread, 'chip', 0, 0)  6.22 us
    pallas_call x1, Pallas kernels, added(): pl.pallas_call(functools.partial(add_kernel, pixels, groups), out_shape=j...  3.78 us
    ppermute x4, starting transfers between devices, swapped(): lax.ppermute(to_cross, ROW, other_pair)  3.57 us
    pallas_call x2, Pallas kernels, strips(): pl.pallas_call(functools.partial(cut_kernel, pixels, chunks), out_shape=s...  3.48 us
    unnamed x13, local copies, waits for them, and re-layouts  3.4 us
  transfers between devices with their start and end apart: 13, of which 7 were waited for; matrix products, arithmetic and copies ran while one was open for 0% of the time, Pallas kernels for 25%

profile of v6, /device:TPU:1, one launch (start us, length us, event | category | flops | bytes accessed | tf_op | source)
XLA Modules:
  0.0 95.5 jit_solution(16176199787257313091)
XLA Ops:
  0.6 0.8 copy.14.offsets.own.own_offsets
  1.4 2.1 %collective-permute-start = (s32[8,2]{1,0:T(8,128)S(1)}, s32[8,2]{1,0:T(8,128)S(1)}, u32[]{:S(2)}, u32[]{:S(2)}) collective-permute-start(s32[8,2]{1,0:T(8,128)S(1)} %copy.14.offsets.own.own_offsets), channel_id=1, source_target_pairs={{0,2},{1,3},{2,4},{3,5},{4,6},{5,7},{6,8},{7,9},{8,10},{9,11},{10,... | collective-permute-start | bytes 200 | tf_op jit(solution)/shard_map/ppermute | solution.py:21
  4.1 0.0 copy-start.2
  4.1 1.0 %copy-done.2 = f32[8,128,128]{2,1,0:T(8,128)S(1)} copy-done((f32[8,128,128]{2,1,0:T(8,128)S(1)}, f32[8,128,128]{2,1,0:T(8,128)}, u32[]{:S(2)}) %copy-start.2) | copy-done | bytes 524312
  5.1 0.0 copy-start.5
  5.2 0.6 shard_map.86
  5.8 1.7 %collective-permute-done.far = s32[8,2]{1,0:T(8,128)S(1)} collective-permute-done((s32[8,2]{1,0:T(8,128)S(1)}, s32[8,2]{1,0:T(8,128)S(1)}, u32[]{:S(2)}, u32[]{:S(2)}) %collective-permute-start) | collective-permute-done | bytes 96 | tf_op jit(solution)/shard_map/ppermute | solution.py:21
  7.5 0.5 collective-permute-start.1
  7.9 1.6 %copy-done = f32[2,2,64,2048]{3,2,1,0:T(8,128)S(1)} copy-done((f32[2,2,64,2048]{3,2,1,0:T(8,128)S(1)}, f32[2,2,64,2048]{3,2,1,0:T(8,128)}, u32[]{:S(2)}) %copy-start) | copy-done | bytes 2097176
  9.5 2.2 %shard_map.88 = (f32[16,64,128]{2,1,0:T(8,128)}, f32[16,64,128]{2,1,0:T(8,128)}) custom-call(s32[8,2]{1,0:T(8,128)S(1)} %copy.14.offsets.own.own_offsets, s32[8,2]{1,0:T(8,128)S(1)} %collective-permute-done.far, f32[4,64,2048]{2,1,0:T(8,128)S(1)} %bitcast.5), custom_call_target="tpu_custom_call" | custom-call | bytes 4194304 | tf_op jit(solution)/shard_map/pallas_call | solution.py:349
  11.7 1.1 %collective-permute-start.2 = (f32[16,64,128]{2,1,0:T(8,128)}, f32[16,64,128]{2,1,0:T(8,128)}, u32[]{:S(2)}, u32[]{:S(2)}) collective-permute-start(f32[16,64,128]{2,1,0:T(8,128)} %get-tuple-element.45), channel_id=1, source_target_pairs={{0,1},{1,0},{2,3},{3,2},{4,5},{5,4},{6,7},{7,6},{8,9},{9,8},{10,11... | collective-permute-start | bytes 1572872 | tf_op jit(solution)/shard_map/ppermute | solution.py:360
  12.8 1.1 %collective-permute-start.3 = (f32[16,64,128]{2,1,0:T(8,128)}, f32[16,64,128]{2,1,0:T(8,128)}, u32[]{:S(2)}, u32[]{:S(2)}) collective-permute-start(f32[16,64,128]{2,1,0:T(8,128)} %get-tuple-element.46), channel_id=1, source_target_pairs={{0,15},{1,2},{2,1},{3,4},{4,3},{5,6},{6,5},{7,8},{8,7},{9,10},{10,... | collective-permute-start | bytes 1572872 | tf_op jit(solution)/shard_map/ppermute | solution.py:360
  13.9 0.0 copy-done.5
  14.0 0.2 fusion.1
  14.2 0.0 copy-start.3
  14.3 0.0 copy-start.4
  14.3 0.5 collective-permute-done.1.target.refs_4_
  14.8 0.0 copy-done.1
  14.8 1.3 %shard_map.89 = (f32[16,64,128]{2,1,0:T(8,128)S(1)}, f32[16,64,128]{2,1,0:T(8,128)S(1)}) custom-call(s32[8,2]{1,0:T(8,128)S(1)} %copy.14.offsets.own.own_offsets, s32[8,2]{1,0:T(8,128)S(1)} %collective-permute-done.far, f32[4,64,2048]{2,1,0:T(8,128)S(1)} %bitcast.6), custom_call_target="tpu_custom_call" | custom-call | bytes 4194304 | tf_op jit(solution)/shard_map/pallas_call | solution.py:349
  16.1 1.3 %shard_map.87 = (f32[16,64,128]{2,1,0:T(8,128)S(1)}, f32[16,64,128]{2,1,0:T(8,128)S(1)}, s32[8,2]{1,0:T(8,128)S(1)}) custom-call(f32[9,128,128]{2,1,0:T(8,128)S(1)} %collective-permute-done.1.target.refs_4_, f32[4,64,2048]{2,1,0:T(8,128)S(1)} %bitcast.7), custom_call_target="tpu_custom_call" | custom-call | bytes 4194304 | tf_op jit(solution)/shard_map/pallas_call | solution.py:364
  17.4 0.0 collective-permute-done.2.refs_2_
  17.4 14.3 %collective-permute-done.3.refs_3_ = f32[16,64,128]{2,1,0:T(8,128)} collective-permute-done((f32[16,64,128]{2,1,0:T(8,128)}, f32[16,64,128]{2,1,0:T(8,128)}, u32[]{:S(2)}, u32[]{:S(2)}) %collective-permute-start.3) | collective-permute-done | bytes 524320 | tf_op jit(solution)/shard_map/ppermute | solution.py:360
  31.7 0.0 collective-permute-start.4
  31.7 0.0 collective-permute-start.5
  31.7 0.0 copy-done.3
  31.7 0.0 copy-done.4
  31.7 12.5 %shard_map.90 = (f32[16,64,128]{2,1,0:T(8,128)S(1)}, f32[16,64,128]{2,1,0:T(8,128)S(1)}, f32[16,64,128]{2,1,0:T(8,128)S(1)}, f32[9,128,128]{2,1,0:T(8,128)S(1)}) custom-call(s32[8,2]{1,0:T(8,128)S(1)} %copy.14.offsets.own.own_offsets, s32[8,2]{1,0:T(8,128)S(1)} %get-tuple-element.44.refs_0_.middle, f32[16,64,128]{2,1,0:T(8,128)S(1)} %get-tuple-element.55.refs_1_, ...), custom_call_target="tpu_custom_call" | custom-call | flops 9663676416 | bytes 8388608 | tf_op jit(solution)/shard_map/pallas_call | solution.py:392
  44.2 0.6 collective-permute-start.6
  44.9 1.2 %collective-permute-start.7 = (f32[16,64,128]{2,1,0:T(8,128)S(1)}, f32[16,64,128]{2,1,0:T(8,128)S(1)}, u32[]{:S(2)}, u32[]{:S(2)}) collective-permute-start(f32[16,64,128]{2,1,0:T(8,128)S(1)} %get-tuple-element.62), channel_id=1, source_target_pairs={{0,15},{1,2},{2,1},{3,4},{4,3},{5,6},{6,5},{7,8},{8,7},{9,10},{10,... | collective-permute-start | bytes 1572872 | tf_op jit(solution)/shard_map/ppermute | solution.py:360
  46.1 0.0 collective-permute-done.4.refs_2_
  46.1 0.0 collective-permute-done.5.refs_3_
  46.1 1.2 %shard_map.91 = (f32[16,64,128]{2,1,0:T(8,128)S(1)}, f32[16,64,128]{2,1,0:T(8,128)S(1)}, f32[16,64,128]{2,1,0:T(8,128)S(1)}, f32[8,9,8,128]{3,2,1,0:T(8,128)S(1)}, f32[8,9,8,128]{3,2,1,0:T(8,128)S(1)}) custom-call(s32[8,2]{1,0:T(8,128)S(1)} %copy.14.offsets.own.own_offsets, s32[8,2]{1,0:T(8,128)S(1)} %get-tuple-element.44.refs_0_.middle, ...), custom_call_target="tpu_custom_call" | custom-call | flops 9663676416 | bytes 8388608 | tf_op jit(solution)/shard_map/pallas_call | solution.py:392
  47.3 0.0 collective-permute-done.6.refs_2_
  47.3 11.8 %collective-permute-done.7.refs_3_ = f32[16,64,128]{2,1,0:T(8,128)S(1)} collective-permute-done((f32[16,64,128]{2,1,0:T(8,128)S(1)}, f32[16,64,128]{2,1,0:T(8,128)S(1)}, u32[]{:S(2)}, u32[]{:S(2)}) %collective-permute-start.7) | collective-permute-done | bytes 524320 | tf_op jit(solution)/shard_map/ppermute | solution.py:360
  59.1 0.0 collective-permute-start.8
  59.1 0.5 collective-permute-start.9
  59.6 1.2 %collective-permute-start.10 = (f32[16,64,128]{2,1,0:T(8,128)S(1)}, f32[16,64,128]{2,1,0:T(8,128)S(1)}, u32[]{:S(2)}, u32[]{:S(2)}) collective-permute-start(f32[16,64,128]{2,1,0:T(8,128)S(1)} %get-tuple-element.70), channel_id=1, source_target_pairs={{0,15},{1,2},{2,1},{3,4},{4,3},{5,6},{6,5},{7,8},{8,7},{9,10},{10,... | collective-permute-start | bytes 1572872 | tf_op jit(solution)/shard_map/ppermute | solution.py:360
  60.8 0.0 collective-permute-done.8
  60.9 14.9 %all_to_all.10.parts = f32[8,9,8,128]{3,2,1,0:T(8,128)S(1)} all-to-all(f32[8,9,8,128]{3,2,1,0:T(8,128)S(1)} %add.3), channel_id=1, replica_groups=mesh['grp'=2,'chip'=8,'core'=2] {'chip'}, dimensions={0} | all-to-all | bytes 589824 | tf_op jit(solution)/shard_map/all_to_all | solution.py:425
  75.8 0.7 shard_map.92
  76.5 0.0 collective-permute-done.9.refs_4_
  76.5 0.3 collective-permute-done.10.refs_5_
  76.8 6.2 %all-to-all-start.1 = ((f32[8,8,8,128]{3,2,1,0:T(8,128)}), f32[8,8,8,128]{3,2,1,0:T(8,128)S(1)}, u32[]{:S(2)}, u32[]{:S(2)}) async-start(f32[8,8,8,128]{3,2,1,0:T(8,128)} %shard_map.92), calls=%async_computation.1 | async-start | bytes 524288 | tf_op jit(solution)/shard_map/all_to_all | solution.py:436
  83.0 3.8 %shard_map.93 = f32[4,64,2048]{2,1,0:T(8,128)} custom-call(s32[8,2]{1,0:T(8,128)S(1)} %copy.14.offsets.own.own_offsets, s32[8,2]{1,0:T(8,128)S(1)} %get-tuple-element.44.refs_0_.middle, s32[8,2]{1,0:T(8,128)S(1)} %collective-permute-done.far, f32[16,64,128]{2,1,0:T(8,128)S(1)} %get-tuple-element.72.refs_0_, f32[16,64,128]{2,1,0:T(8,128)S(1)} %get-tuple-element.73.refs_1_, ...), custom_call_target="tpu_custom_call" | custom-call | bytes 5242880 | tf_op jit(solution)/shard_map/pallas_call | solution.py:413
  86.8 3.4 %all-to-all-done.1.own = f32[8,8,8,128]{3,2,1,0:T(8,128)S(1)} async-done(((f32[8,8,8,128]{3,2,1,0:T(8,128)}), f32[8,8,8,128]{3,2,1,0:T(8,128)S(1)}, u32[]{:S(2)}, u32[]{:S(2)}) %all-to-all-start.1) | async-done | bytes 262176 | tf_op jit(solution)/shard_map/all_to_all | solution.py:436
  90.2 2.7 %collective-permute-start.11 = (f32[8,8,8,128]{3,2,1,0:T(8,128)S(1)}, f32[8,8,8,128]{3,2,1,0:T(8,128)S(1)}, u32[]{:S(2)}, u32[]{:S(2)}) collective-permute-start(f32[8,8,8,128]{3,2,1,0:T(8,128)S(1)} %all-to-all-done.1.own), channel_id=1, source_target_pairs={{0,1},{1,0},{2,3},{3,2},{4,5},{5,4},{6,7},{7,6},{8,9},{9,8},{10,11... | collective-permute-start | bytes 786440 | tf_op jit(solution)/shard_map/ppermute | solution.py:447
  92.9 1.2 %collective-permute-done.11.other = f32[8,8,8,128]{3,2,1,0:T(8,128)S(1)} collective-permute-done((f32[8,8,8,128]{3,2,1,0:T(8,128)S(1)}, f32[8,8,8,128]{3,2,1,0:T(8,128)S(1)}, u32[]{:S(2)}, u32[]{:S(2)}) %collective-permute-start.11) | collective-permute-done | bytes 262176 | tf_op jit(solution)/shard_map/ppermute | solution.py:447
  94.0 1.5 %shard_map.94 = f32[8,128,128]{2,1,0:T(8,128)} custom-call(s32[8,2]{1,0:T(8,128)S(1)} %copy.14.offsets.own.own_offsets, f32[8,8,8,128]{3,2,1,0:T(8,128)S(1)} %all-to-all-done.1.own, f32[8,8,8,128]{3,2,1,0:T(8,128)S(1)} %collective-permute-done.11.other), custom_call_target="tpu_custom_call" | custom-call | tf_op jit(solution)/shard_map/pallas_call | solution.py:441
  (6 shorter events, 0.1 us)
Async XLA Ops:
  1.4 6.1 %collective-permute-start = (s32[8,2]{1,0:T(8,128)S(1)}, s32[8,2]{1,0:T(8,128)S(1)}, u32[]{:S(2)}, u32[]{:S(2)}) collective-permute-start(s32[8,2]{1,0:T(8,128)S(1)} %copy.14.offsets.own.own_offsets), channel_id=1, source_target_pairs={{0,2},{1,3},{2,4},{3,5},{4,6},{5,7},{6,8},{7,9},{8,10},{9,11},{10,... | collective-permute-start | bytes 200 | tf_op jit(solution)/shard_map/ppermute | solution.py:21
  4.1 1.0 %copy-start.2 = (f32[8,128,128]{2,1,0:T(8,128)S(1)}, f32[8,128,128]{2,1,0:T(8,128)}, u32[]{:S(2)}) copy-start(f32[8,128,128]{2,1,0:T(8,128)} %measured.1) | copy-start | bytes 1572868
  5.1 8.8 %copy-start.5 = (f32[128,128]{1,0:T(8,128)S(1)}, f32[128,128]{1,0:T(8,128)}, u32[]{:S(2)}) copy-start(f32[128,128]{1,0:T(8,128)} %param.9) | copy-start | bytes 196612
  7.5 7.3 %collective-permute-start.1 = (f32[9,128,128]{2,1,0:T(8,128)S(1)}, f32[9,128,128]{2,1,0:T(8,128)S(1)}, u32[]{:S(2)}, u32[]{:S(2)}) collective-permute-start(f32[9,128,128]{2,1,0:T(8,128)S(1)} %shard_map.86), channel_id=1, source_target_pairs={{0,1},{1,2},{2,3},{3,4},{4,5},{5,6},{6,7},{7,8},{8,9},{9,10},{10,1... | collective-permute-start | bytes 1769480 | tf_op jit(solution)/shard_map/ppermute | solution.py:21
  7.9 1.6 %copy-start = (f32[2,2,64,2048]{3,2,1,0:T(8,128)S(1)}, f32[2,2,64,2048]{3,2,1,0:T(8,128)}, u32[]{:S(2)}) copy-start(f32[2,2,64,2048]{3,2,1,0:T(8,128)} %param.7) | copy-start | bytes 6291460
  9.5 5.2 %copy-start.1 = (f32[2,2,64,2048]{3,2,1,0:T(8,128)S(1)}, f32[2,2,64,2048]{3,2,1,0:T(8,128)}, u32[]{:S(2)}) copy-start(f32[2,2,64,2048]{3,2,1,0:T(8,128)} %param.7) | copy-start | bytes 6291460
  11.7 5.7 %collective-permute-start.2 = (f32[16,64,128]{2,1,0:T(8,128)}, f32[16,64,128]{2,1,0:T(8,128)}, u32[]{:S(2)}, u32[]{:S(2)}) collective-permute-start(f32[16,64,128]{2,1,0:T(8,128)} %get-tuple-element.45), channel_id=1, source_target_pairs={{0,1},{1,0},{2,3},{3,2},{4,5},{5,4},{6,7},{7,6},{8,9},{9,8},{10,11... | collective-permute-start | bytes 1572872 | tf_op jit(solution)/shard_map/ppermute | solution.py:360
  12.8 18.9 %collective-permute-start.3 = (f32[16,64,128]{2,1,0:T(8,128)}, f32[16,64,128]{2,1,0:T(8,128)}, u32[]{:S(2)}, u32[]{:S(2)}) collective-permute-start(f32[16,64,128]{2,1,0:T(8,128)} %get-tuple-element.46), channel_id=1, source_target_pairs={{0,15},{1,2},{2,1},{3,4},{4,3},{5,6},{6,5},{7,8},{8,7},{9,10},{10,... | collective-permute-start | bytes 1572872 | tf_op jit(solution)/shard_map/ppermute | solution.py:360
  14.2 17.5 %copy-start.3 = (f32[4,2,128,128]{3,2,1,0:T(8,128)S(1)}, f32[4,2,128,128]{3,2,1,0:T(8,128)}, u32[]{:S(2)}) copy-start(f32[4,2,128,128]{3,2,1,0:T(8,128)} %refs_5_.3) | copy-start | bytes 1572868
  14.3 17.4 %copy-start.4 = (bf16[8,256,256]{2,1,0:T(8,128)(2,1)S(1)}, bf16[8,256,256]{2,1,0:T(8,128)(2,1)}, u32[]{:S(2)}) copy-start(bf16[8,256,256]{2,1,0:T(8,128)(2,1)} %constant.2.clone.refs_7_) | copy-start | bytes 3145732
  31.7 14.4 %collective-permute-start.4 = (f32[16,64,128]{2,1,0:T(8,128)S(1)}, f32[16,64,128]{2,1,0:T(8,128)S(1)}, u32[]{:S(2)}, u32[]{:S(2)}) collective-permute-start(f32[16,64,128]{2,1,0:T(8,128)S(1)} %get-tuple-element.53), channel_id=1, source_target_pairs={{0,1},{1,0},{2,3},{3,2},{4,5},{5,4},{6,7},{7,6},{8,9},{9,8},{10,11... | collective-permute-start | bytes 1572872 | tf_op jit(solution)/shard_map/ppermute | solution.py:360
  31.7 14.4 %collective-permute-start.5 = (f32[16,64,128]{2,1,0:T(8,128)S(1)}, f32[16,64,128]{2,1,0:T(8,128)S(1)}, u32[]{:S(2)}, u32[]{:S(2)}) collective-permute-start(f32[16,64,128]{2,1,0:T(8,128)S(1)} %get-tuple-element.54), channel_id=1, source_target_pairs={{0,15},{1,2},{2,1},{3,4},{4,3},{5,6},{6,5},{7,8},{8,7},{9,10},{10,... | collective-permute-start | bytes 1572872 | tf_op jit(solution)/shard_map/ppermute | solution.py:360
  44.2 3.1 %collective-permute-start.6 = (f32[16,64,128]{2,1,0:T(8,128)S(1)}, f32[16,64,128]{2,1,0:T(8,128)S(1)}, u32[]{:S(2)}, u32[]{:S(2)}) collective-permute-start(f32[16,64,128]{2,1,0:T(8,128)S(1)} %get-tuple-element.61), channel_id=1, source_target_pairs={{0,1},{1,0},{2,3},{3,2},{4,5},{5,4},{6,7},{7,6},{8,9},{9,8},{10,11... | collective-permute-start | bytes 1572872 | tf_op jit(solution)/shard_map/ppermute | solution.py:360
  44.9 14.2 %collective-permute-start.7 = (f32[16,64,128]{2,1,0:T(8,128)S(1)}, f32[16,64,128]{2,1,0:T(8,128)S(1)}, u32[]{:S(2)}, u32[]{:S(2)}) collective-permute-start(f32[16,64,128]{2,1,0:T(8,128)S(1)} %get-tuple-element.62), channel_id=1, source_target_pairs={{0,15},{1,2},{2,1},{3,4},{4,3},{5,6},{6,5},{7,8},{8,7},{9,10},{10,... | collective-permute-start | bytes 1572872 | tf_op jit(solution)/shard_map/ppermute | solution.py:360
  59.1 1.7 %collective-permute-start.8 = (f32[8,9,8,128]{3,2,1,0:T(8,128)S(1)}, f32[8,9,8,128]{3,2,1,0:T(8,128)S(1)}, u32[]{:S(2)}, u32[]{:S(2)}) collective-permute-start(f32[8,9,8,128]{3,2,1,0:T(8,128)S(1)} %get-tuple-element.64), channel_id=1, source_target_pairs={{0,1},{1,0},{2,3},{3,2},{4,5},{5,4},{6,7},{7,6},{8,9},{9,8},{10,11... | collective-permute-start | bytes 884744 | tf_op jit(solution)/shard_map/ppermute | solution.py:424
  59.1 17.4 %collective-permute-start.9 = (f32[16,64,128]{2,1,0:T(8,128)S(1)}, f32[16,64,128]{2,1,0:T(8,128)S(1)}, u32[]{:S(2)}, u32[]{:S(2)}) collective-permute-start(f32[16,64,128]{2,1,0:T(8,128)S(1)} %get-tuple-element.69), channel_id=1, source_target_pairs={{0,1},{1,0},{2,3},{3,2},{4,5},{5,4},{6,7},{7,6},{8,9},{9,8},{10,11... | collective-permute-start | bytes 1572872 | tf_op jit(solution)/shard_map/ppermute | solution.py:360
  59.6 17.2 %collective-permute-start.10 = (f32[16,64,128]{2,1,0:T(8,128)S(1)}, f32[16,64,128]{2,1,0:T(8,128)S(1)}, u32[]{:S(2)}, u32[]{:S(2)}) collective-permute-start(f32[16,64,128]{2,1,0:T(8,128)S(1)} %get-tuple-element.70), channel_id=1, source_target_pairs={{0,15},{1,2},{2,1},{3,4},{4,3},{5,6},{6,5},{7,8},{8,7},{9,10},{10,... | collective-permute-start | bytes 1572872 | tf_op jit(solution)/shard_map/ppermute | solution.py:360
  76.8 13.4 %all-to-all-start.1 = ((f32[8,8,8,128]{3,2,1,0:T(8,128)}), f32[8,8,8,128]{3,2,1,0:T(8,128)S(1)}, u32[]{:S(2)}, u32[]{:S(2)}) async-start(f32[8,8,8,128]{3,2,1,0:T(8,128)} %shard_map.92), calls=%async_computation.1 | async-start | bytes 524288 | tf_op jit(solution)/shard_map/all_to_all | solution.py:436
  90.2 3.9 %collective-permute-start.11 = (f32[8,8,8,128]{3,2,1,0:T(8,128)S(1)}, f32[8,8,8,128]{3,2,1,0:T(8,128)S(1)}, u32[]{:S(2)}, u32[]{:S(2)}) collective-permute-start(f32[8,8,8,128]{3,2,1,0:T(8,128)S(1)} %all-to-all-done.1.own), channel_id=1, source_target_pairs={{0,1},{1,0},{2,3},{3,2},{4,5},{5,4},{6,7},{7,6},{8,9},{9,8},{10,11... | collective-permute-start | bytes 786440 | tf_op jit(solution)/shard_map/ppermute | solution.py:447

commit v7 on v6

--- a/solution.py
+++ b/solution.py
@@ -11,6 +11,7 @@
 CHUNKS = (4, 4)
 BATCH = 4
 VMEM_LIMIT = 40 * 1024 * 1024
+SMALL_LIMIT = 16 * 1024 * 1024
 ROW = ("chip", "core")
 F32 = jnp.float32
 BF16 = jnp.bfloat16
@@ -321,7 +322,7 @@
     modes, _, pixels, _ = probe_modes.shape
     planes = 2 * slices
     peers = lax.axis_size(ROW)
-    params = pltpu.CompilerParams(vmem_limit_bytes=VMEM_LIMIT)
+    params = pltpu.CompilerParams(vmem_limit_bytes=SMALL_LIMIT)
     tile = object_slices.reshape(planes, tile_rows, columns)
     starts = [sum(CHUNKS[:i]) for i in range(len(CHUNKS))]
 
@@ -396,7 +397,7 @@
             out_specs=[in_vmem()] * (3 + (len(shares) or 1)),
             scratch_shapes=([pltpu.VMEM(sums.shape, F32)] if shares else [])
             + [pltpu.VMEM((planes, 3 * tile_rows, pixels), F32), field, field, kept, kept],
-            compiler_params=params,
+            compiler_params=pltpu.CompilerParams(vmem_limit_bytes=VMEM_LIMIT),
             cost_estimate=pl.CostEstimate(
                 flops=size * 6 * modes * 3 * 16 * pixels**3, bytes_accessed=8 << 20, transcendentals=0
             ),

time: 96.4 us -> 96.6 us (level)
  starting transfers between devices: 17.3 us -> 14.9 us
  blocking collectives: 14.9 us -> 16.3 us
  waiting for transfers between devices: 33.1 us -> 34.5 us
    all_to_all x1, starting transfers between devices: 6.22 us -> 3.63 us  [local(): gathered = lax.all_to_all(spread, 'chip', 0, 0)]
    ppermute x1, starting transfers between devices: 0.01 us -> 2.36 us  [local(): both = own + lax.ppermute(other, ROW, pair)]
    all_to_all x1, blocking collectives: 14.9 us -> 16.3 us  [local(): parts = lax.all_to_all(both, 'chip', 0, 0)]
    ppermute x4, starting transfers between devices: 3.57 us -> 2.35 us  [swapped(): lax.ppermute(to_cross, ROW, other_pair)]
    ppermute x1, waiting for transfers between devices: 0.01 us -> 1.13 us  [local(): both = own + lax.ppermute(other, ROW, pair)]
where the time goes in v7:
time: 96.6 us; the launch traced here: 95.9 us
  waiting for transfers between devices  34.5 us (36%)
  Pallas kernels  25.1 us (26%)
  blocking collectives  16.3 us (17%)
  starting transfers between devices  14.9 us (15%)
  local copies, waits for them, and re-layouts  3.43 us (4%)
  between operations  1.41 us (1%)
    ppermute x4, waiting for transfers between devices, swapped(): lax.ppermute(to_cross, ROW, other_pair)  26.1 us
    all_to_all x1, blocking collectives, local(): parts = lax.all_to_all(both, 'chip', 0, 0)  16.3 us
    pallas_call x2, Pallas kernels, local(): pl.pallas_call(functools.partial(slot_kernel, first, size, len(given)), o...  13.7 us
    all_to_all x1, waiting for transfers between devices, local(): gathered = lax.all_to_all(spread, 'chip', 0, 0)  3.91 us
    pallas_call x1, Pallas kernels, added(): pl.pallas_call(functools.partial(add_kernel, pixels, groups), out_shape=j...  3.77 us
    all_to_all x1, starting transfers between devices, local(): gathered = lax.all_to_all(spread, 'chip', 0, 0)  3.63 us
    pallas_call x2, Pallas kernels, strips(): pl.pallas_call(functools.partial(cut_kernel, pixels, chunks), out_shape=s...  3.48 us
    unnamed x13, local copies, waits for them, and re-layouts  3.4 us
  transfers between devices with their start and end apart: 13, of which 7 were waited for; matrix products, arithmetic and copies ran while one was open for 0% of the time, Pallas kernels for 25%

profile of v7, /device:TPU:1, one launch (start us, length us, event | category | flops | bytes accessed | tf_op | source)
XLA Modules:
  0.0 95.9 jit_solution(6351213678237008999)
XLA Ops:
  0.6 0.8 copy.14.offsets.own.own_offsets
  1.4 2.1 %collective-permute-start = (s32[8,2]{1,0:T(8,128)S(1)}, s32[8,2]{1,0:T(8,128)S(1)}, u32[]{:S(2)}, u32[]{:S(2)}) collective-permute-start(s32[8,2]{1,0:T(8,128)S(1)} %copy.14.offsets.own.own_offsets), channel_id=1, source_target_pairs={{0,2},{1,3},{2,4},{3,5},{4,6},{5,7},{6,8},{7,9},{8,10},{9,11},{10,... | collective-permute-start | bytes 200 | tf_op jit(solution)/shard_map/ppermute | solution.py:22
  4.1 0.0 copy-start.2
  4.1 1.0 %copy-done.2 = f32[8,128,128]{2,1,0:T(8,128)S(1)} copy-done((f32[8,128,128]{2,1,0:T(8,128)S(1)}, f32[8,128,128]{2,1,0:T(8,128)}, u32[]{:S(2)}) %copy-start.2) | copy-done | bytes 524312
  5.1 0.0 copy-start.5
  5.2 0.6 shard_map.86
  5.8 1.7 %collective-permute-done.far = s32[8,2]{1,0:T(8,128)S(1)} collective-permute-done((s32[8,2]{1,0:T(8,128)S(1)}, s32[8,2]{1,0:T(8,128)S(1)}, u32[]{:S(2)}, u32[]{:S(2)}) %collective-permute-start) | collective-permute-done | bytes 96 | tf_op jit(solution)/shard_map/ppermute | solution.py:22
  7.5 0.5 collective-permute-start.1
  7.9 1.6 %copy-done = f32[2,2,64,2048]{3,2,1,0:T(8,128)S(1)} copy-done((f32[2,2,64,2048]{3,2,1,0:T(8,128)S(1)}, f32[2,2,64,2048]{3,2,1,0:T(8,128)}, u32[]{:S(2)}) %copy-start) | copy-done | bytes 2097176
  9.5 2.2 %shard_map.88 = (f32[16,64,128]{2,1,0:T(8,128)}, f32[16,64,128]{2,1,0:T(8,128)}) custom-call(s32[8,2]{1,0:T(8,128)S(1)} %copy.14.offsets.own.own_offsets, s32[8,2]{1,0:T(8,128)S(1)} %collective-permute-done.far, f32[4,64,2048]{2,1,0:T(8,128)S(1)} %bitcast.5), custom_call_target="tpu_custom_call" | custom-call | bytes 4194304 | tf_op jit(solution)/shard_map/pallas_call | solution.py:350
  11.7 1.1 %collective-permute-start.2 = (f32[16,64,128]{2,1,0:T(8,128)}, f32[16,64,128]{2,1,0:T(8,128)}, u32[]{:S(2)}, u32[]{:S(2)}) collective-permute-start(f32[16,64,128]{2,1,0:T(8,128)} %get-tuple-element.45), channel_id=1, source_target_pairs={{0,1},{1,0},{2,3},{3,2},{4,5},{5,4},{6,7},{7,6},{8,9},{9,8},{10,11... | collective-permute-start | bytes 1572872 | tf_op jit(solution)/shard_map/ppermute | solution.py:361
  12.8 1.1 %collective-permute-start.3 = (f32[16,64,128]{2,1,0:T(8,128)}, f32[16,64,128]{2,1,0:T(8,128)}, u32[]{:S(2)}, u32[]{:S(2)}) collective-permute-start(f32[16,64,128]{2,1,0:T(8,128)} %get-tuple-element.46), channel_id=1, source_target_pairs={{0,15},{1,2},{2,1},{3,4},{4,3},{5,6},{6,5},{7,8},{8,7},{9,10},{10,... | collective-permute-start | bytes 1572872 | tf_op jit(solution)/shard_map/ppermute | solution.py:361
  13.9 0.0 copy-done.5
  14.0 0.2 fusion.1
  14.2 0.0 copy-start.3
  14.3 0.0 copy-start.4
  14.3 0.5 collective-permute-done.1.target.refs_4_
  14.8 0.0 copy-done.1
  14.8 1.3 %shard_map.89 = (f32[16,64,128]{2,1,0:T(8,128)S(1)}, f32[16,64,128]{2,1,0:T(8,128)S(1)}) custom-call(s32[8,2]{1,0:T(8,128)S(1)} %copy.14.offsets.own.own_offsets, s32[8,2]{1,0:T(8,128)S(1)} %collective-permute-done.far, f32[4,64,2048]{2,1,0:T(8,128)S(1)} %bitcast.6), custom_call_target="tpu_custom_call" | custom-call | bytes 4194304 | tf_op jit(solution)/shard_map/pallas_call | solution.py:350
  16.1 1.3 %shard_map.87 = (f32[16,64,128]{2,1,0:T(8,128)S(1)}, f32[16,64,128]{2,1,0:T(8,128)S(1)}, s32[8,2]{1,0:T(8,128)S(1)}) custom-call(f32[9,128,128]{2,1,0:T(8,128)S(1)} %collective-permute-done.1.target.refs_4_, f32[4,64,2048]{2,1,0:T(8,128)S(1)} %bitcast.7), custom_call_target="tpu_custom_call" | custom-call | bytes 4194304 | tf_op jit(solution)/shard_map/pallas_call | solution.py:365
  17.4 0.0 collective-permute-done.2.refs_2_
  17.4 14.3 %collective-permute-done.3.refs_3_ = f32[16,64,128]{2,1,0:T(8,128)} collective-permute-done((f32[16,64,128]{2,1,0:T(8,128)}, f32[16,64,128]{2,1,0:T(8,128)}, u32[]{:S(2)}, u32[]{:S(2)}) %collective-permute-start.3) | collective-permute-done | bytes 524320 | tf_op jit(solution)/shard_map/ppermute | solution.py:361
  31.7 0.0 collective-permute-start.4
  31.7 0.0 collective-permute-start.5
  31.7 0.0 copy-done.3
  31.7 0.0 copy-done.4
  31.7 12.5 %shard_map.90 = (f32[16,64,128]{2,1,0:T(8,128)S(1)}, f32[16,64,128]{2,1,0:T(8,128)S(1)}, f32[16,64,128]{2,1,0:T(8,128)S(1)}, f32[9,128,128]{2,1,0:T(8,128)S(1)}) custom-call(s32[8,2]{1,0:T(8,128)S(1)} %copy.14.offsets.own.own_offsets, s32[8,2]{1,0:T(8,128)S(1)} %get-tuple-element.44.refs_0_.middle, f32[16,64,128]{2,1,0:T(8,128)S(1)} %get-tuple-element.55.refs_1_, ...), custom_call_target="tpu_custom_call" | custom-call | flops 9663676416 | bytes 8388608 | tf_op jit(solution)/shard_map/pallas_call | solution.py:393
  44.2 0.7 collective-permute-start.6
  44.9 1.2 %collective-permute-start.7 = (f32[16,64,128]{2,1,0:T(8,128)S(1)}, f32[16,64,128]{2,1,0:T(8,128)S(1)}, u32[]{:S(2)}, u32[]{:S(2)}) collective-permute-start(f32[16,64,128]{2,1,0:T(8,128)S(1)} %get-tuple-element.62), channel_id=1, source_target_pairs={{0,15},{1,2},{2,1},{3,4},{4,3},{5,6},{6,5},{7,8},{8,7},{9,10},{10,... | collective-permute-start | bytes 1572872 | tf_op jit(solution)/shard_map/ppermute | solution.py:361
  46.1 0.0 collective-permute-done.4.refs_2_
  46.1 0.0 collective-permute-done.5.refs_3_
  46.1 1.2 %shard_map.91 = (f32[16,64,128]{2,1,0:T(8,128)S(1)}, f32[16,64,128]{2,1,0:T(8,128)S(1)}, f32[16,64,128]{2,1,0:T(8,128)S(1)}, f32[8,9,8,128]{3,2,1,0:T(8,128)S(1)}, f32[8,9,8,128]{3,2,1,0:T(8,128)S(1)}) custom-call(s32[8,2]{1,0:T(8,128)S(1)} %copy.14.offsets.own.own_offsets, s32[8,2]{1,0:T(8,128)S(1)} %get-tuple-element.44.refs_0_.middle, ...), custom_call_target="tpu_custom_call" | custom-call | flops 9663676416 | bytes 8388608 | tf_op jit(solution)/shard_map/pallas_call | solution.py:393
  47.3 0.0 collective-permute-done.6.refs_2_
  47.3 11.8 %collective-permute-done.7.refs_3_ = f32[16,64,128]{2,1,0:T(8,128)S(1)} collective-permute-done((f32[16,64,128]{2,1,0:T(8,128)S(1)}, f32[16,64,128]{2,1,0:T(8,128)S(1)}, u32[]{:S(2)}, u32[]{:S(2)}) %collective-permute-start.7) | collective-permute-done | bytes 524320 | tf_op jit(solution)/shard_map/ppermute | solution.py:361
  59.1 2.4 %collective-permute-start.8 = (f32[8,9,8,128]{3,2,1,0:T(8,128)S(1)}, f32[8,9,8,128]{3,2,1,0:T(8,128)S(1)}, u32[]{:S(2)}, u32[]{:S(2)}) collective-permute-start(f32[8,9,8,128]{3,2,1,0:T(8,128)S(1)} %get-tuple-element.64), channel_id=1, source_target_pairs={{0,1},{1,0},{2,3},{3,2},{4,5},{5,4},{6,7},{7,6},{8,9},{9,8},{10,11... | collective-permute-start | bytes 884744 | tf_op jit(solution)/shard_map/ppermute | solution.py:425
  61.5 0.1 collective-permute-start.9
  61.6 0.0 collective-permute-start.10
  61.6 1.1 %collective-permute-done.8 = f32[8,9,8,128]{3,2,1,0:T(8,128)S(1)} collective-permute-done((f32[8,9,8,128]{3,2,1,0:T(8,128)S(1)}, f32[8,9,8,128]{3,2,1,0:T(8,128)S(1)}, u32[]{:S(2)}, u32[]{:S(2)}) %collective-permute-start.8) | collective-permute-done | bytes 294944 | tf_op jit(solution)/shard_map/ppermute | solution.py:425
  62.7 16.3 %all_to_all.10.parts = f32[8,9,8,128]{3,2,1,0:T(8,128)S(1)} all-to-all(f32[8,9,8,128]{3,2,1,0:T(8,128)S(1)} %add.3), channel_id=1, replica_groups=mesh['grp'=2,'chip'=8,'core'=2] {'chip'}, dimensions={0} | all-to-all | bytes 589824 | tf_op jit(solution)/shard_map/all_to_all | solution.py:426
  79.0 0.7 shard_map.92
  79.8 0.0 collective-permute-done.9.refs_4_
  79.8 0.0 collective-permute-done.10.refs_5_
  79.8 3.6 %all-to-all-start.1 = ((f32[8,8,8,128]{3,2,1,0:T(8,128)}), f32[8,8,8,128]{3,2,1,0:T(8,128)S(1)}, u32[]{:S(2)}, u32[]{:S(2)}) async-start(f32[8,8,8,128]{3,2,1,0:T(8,128)} %shard_map.92), calls=%async_computation.1 | async-start | bytes 524288 | tf_op jit(solution)/shard_map/all_to_all | solution.py:437
  83.4 3.8 %shard_map.93 = f32[4,64,2048]{2,1,0:T(8,128)} custom-call(s32[8,2]{1,0:T(8,128)S(1)} %copy.14.offsets.own.own_offsets, s32[8,2]{1,0:T(8,128)S(1)} %get-tuple-element.44.refs_0_.middle, s32[8,2]{1,0:T(8,128)S(1)} %collective-permute-done.far, f32[16,64,128]{2,1,0:T(8,128)S(1)} %get-tuple-element.72.refs_0_, f32[16,64,128]{2,1,0:T(8,128)S(1)} %get-tuple-element.73.refs_1_, ...), custom_call_target="tpu_custom_call" | custom-call | bytes 5242880 | tf_op jit(solution)/shard_map/pallas_call | solution.py:414
  87.2 3.9 %all-to-all-done.1.own = f32[8,8,8,128]{3,2,1,0:T(8,128)S(1)} async-done(((f32[8,8,8,128]{3,2,1,0:T(8,128)}), f32[8,8,8,128]{3,2,1,0:T(8,128)S(1)}, u32[]{:S(2)}, u32[]{:S(2)}) %all-to-all-start.1) | async-done | bytes 262176 | tf_op jit(solution)/shard_map/all_to_all | solution.py:437
  91.1 2.2 %collective-permute-start.11 = (f32[8,8,8,128]{3,2,1,0:T(8,128)S(1)}, f32[8,8,8,128]{3,2,1,0:T(8,128)S(1)}, u32[]{:S(2)}, u32[]{:S(2)}) collective-permute-start(f32[8,8,8,128]{3,2,1,0:T(8,128)S(1)} %all-to-all-done.1.own), channel_id=1, source_target_pairs={{0,1},{1,0},{2,3},{3,2},{4,5},{5,4},{6,7},{7,6},{8,9},{9,8},{10,11... | collective-permute-start | bytes 786440 | tf_op jit(solution)/shard_map/ppermute | solution.py:448
  93.3 1.2 %collective-permute-done.11.other = f32[8,8,8,128]{3,2,1,0:T(8,128)S(1)} collective-permute-done((f32[8,8,8,128]{3,2,1,0:T(8,128)S(1)}, f32[8,8,8,128]{3,2,1,0:T(8,128)S(1)}, u32[]{:S(2)}, u32[]{:S(2)}) %collective-permute-start.11) | collective-permute-done | bytes 262176 | tf_op jit(solution)/shard_map/ppermute | solution.py:448
  94.4 1.5 %shard_map.94 = f32[8,128,128]{2,1,0:T(8,128)} custom-call(s32[8,2]{1,0:T(8,128)S(1)} %copy.14.offsets.own.own_offsets, f32[8,8,8,128]{3,2,1,0:T(8,128)S(1)} %all-to-all-done.1.own, f32[8,8,8,128]{3,2,1,0:T(8,128)S(1)} %collective-permute-done.11.other), custom_call_target="tpu_custom_call" | custom-call | tf_op jit(solution)/shard_map/pallas_call | solution.py:442
  (6 shorter events, 0.1 us)
Async XLA Ops:
  1.4 6.1 %collective-permute-start = (s32[8,2]{1,0:T(8,128)S(1)}, s32[8,2]{1,0:T(8,128)S(1)}, u32[]{:S(2)}, u32[]{:S(2)}) collective-permute-start(s32[8,2]{1,0:T(8,128)S(1)} %copy.14.offsets.own.own_offsets), channel_id=1, source_target_pairs={{0,2},{1,3},{2,4},{3,5},{4,6},{5,7},{6,8},{7,9},{8,10},{9,11},{10,... | collective-permute-start | bytes 200 | tf_op jit(solution)/shard_map/ppermute | solution.py:22
  4.1 1.0 %copy-start.2 = (f32[8,128,128]{2,1,0:T(8,128)S(1)}, f32[8,128,128]{2,1,0:T(8,128)}, u32[]{:S(2)}) copy-start(f32[8,128,128]{2,1,0:T(8,128)} %measured.1) | copy-start | bytes 1572868
  5.1 8.8 %copy-start.5 = (f32[128,128]{1,0:T(8,128)S(1)}, f32[128,128]{1,0:T(8,128)}, u32[]{:S(2)}) copy-start(f32[128,128]{1,0:T(8,128)} %param.9) | copy-start | bytes 196612
  7.5 7.3 %collective-permute-start.1 = (f32[9,128,128]{2,1,0:T(8,128)S(1)}, f32[9,128,128]{2,1,0:T(8,128)S(1)}, u32[]{:S(2)}, u32[]{:S(2)}) collective-permute-start(f32[9,128,128]{2,1,0:T(8,128)S(1)} %shard_map.86), channel_id=1, source_target_pairs={{0,1},{1,2},{2,3},{3,4},{4,5},{5,6},{6,7},{7,8},{8,9},{9,10},{10,1... | collective-permute-start | bytes 1769480 | tf_op jit(solution)/shard_map/ppermute | solution.py:22
  7.9 1.6 %copy-start = (f32[2,2,64,2048]{3,2,1,0:T(8,128)S(1)}, f32[2,2,64,2048]{3,2,1,0:T(8,128)}, u32[]{:S(2)}) copy-start(f32[2,2,64,2048]{3,2,1,0:T(8,128)} %param.7) | copy-start | bytes 6291460
  9.5 5.2 %copy-start.1 = (f32[2,2,64,2048]{3,2,1,0:T(8,128)S(1)}, f32[2,2,64,2048]{3,2,1,0:T(8,128)}, u32[]{:S(2)}) copy-start(f32[2,2,64,2048]{3,2,1,0:T(8,128)} %param.7) | copy-start | bytes 6291460
  11.7 5.7 %collective-permute-start.2 = (f32[16,64,128]{2,1,0:T(8,128)}, f32[16,64,128]{2,1,0:T(8,128)}, u32[]{:S(2)}, u32[]{:S(2)}) collective-permute-start(f32[16,64,128]{2,1,0:T(8,128)} %get-tuple-element.45), channel_id=1, source_target_pairs={{0,1},{1,0},{2,3},{3,2},{4,5},{5,4},{6,7},{7,6},{8,9},{9,8},{10,11... | collective-permute-start | bytes 1572872 | tf_op jit(solution)/shard_map/ppermute | solution.py:361
  12.8 18.9 %collective-permute-start.3 = (f32[16,64,128]{2,1,0:T(8,128)}, f32[16,64,128]{2,1,0:T(8,128)}, u32[]{:S(2)}, u32[]{:S(2)}) collective-permute-start(f32[16,64,128]{2,1,0:T(8,128)} %get-tuple-element.46), channel_id=1, source_target_pairs={{0,15},{1,2},{2,1},{3,4},{4,3},{5,6},{6,5},{7,8},{8,7},{9,10},{10,... | collective-permute-start | bytes 1572872 | tf_op jit(solution)/shard_map/ppermute | solution.py:361
  14.2 17.5 %copy-start.3 = (f32[4,2,128,128]{3,2,1,0:T(8,128)S(1)}, f32[4,2,128,128]{3,2,1,0:T(8,128)}, u32[]{:S(2)}) copy-start(f32[4,2,128,128]{3,2,1,0:T(8,128)} %refs_5_.3) | copy-start | bytes 1572868
  14.3 17.5 %copy-start.4 = (bf16[8,256,256]{2,1,0:T(8,128)(2,1)S(1)}, bf16[8,256,256]{2,1,0:T(8,128)(2,1)}, u32[]{:S(2)}) copy-start(bf16[8,256,256]{2,1,0:T(8,128)(2,1)} %constant.2.clone.refs_7_) | copy-start | bytes 3145732
  31.7 14.4 %collective-permute-start.4 = (f32[16,64,128]{2,1,0:T(8,128)S(1)}, f32[16,64,128]{2,1,0:T(8,128)S(1)}, u32[]{:S(2)}, u32[]{:S(2)}) collective-permute-start(f32[16,64,128]{2,1,0:T(8,128)S(1)} %get-tuple-element.53), channel_id=1, source_target_pairs={{0,1},{1,0},{2,3},{3,2},{4,5},{5,4},{6,7},{7,6},{8,9},{9,8},{10,11... | collective-permute-start | bytes 1572872 | tf_op jit(solution)/shard_map/ppermute | solution.py:361
  31.7 14.4 %collective-permute-start.5 = (f32[16,64,128]{2,1,0:T(8,128)S(1)}, f32[16,64,128]{2,1,0:T(8,128)S(1)}, u32[]{:S(2)}, u32[]{:S(2)}) collective-permute-start(f32[16,64,128]{2,1,0:T(8,128)S(1)} %get-tuple-element.54), channel_id=1, source_target_pairs={{0,15},{1,2},{2,1},{3,4},{4,3},{5,6},{6,5},{7,8},{8,7},{9,10},{10,... | collective-permute-start | bytes 1572872 | tf_op jit(solution)/shard_map/ppermute | solution.py:361
  44.2 3.1 %collective-permute-start.6 = (f32[16,64,128]{2,1,0:T(8,128)S(1)}, f32[16,64,128]{2,1,0:T(8,128)S(1)}, u32[]{:S(2)}, u32[]{:S(2)}) collective-permute-start(f32[16,64,128]{2,1,0:T(8,128)S(1)} %get-tuple-element.61), channel_id=1, source_target_pairs={{0,1},{1,0},{2,3},{3,2},{4,5},{5,4},{6,7},{7,6},{8,9},{9,8},{10,11... | collective-permute-start | bytes 1572872 | tf_op jit(solution)/shard_map/ppermute | solution.py:361
  44.9 14.2 %collective-permute-start.7 = (f32[16,64,128]{2,1,0:T(8,128)S(1)}, f32[16,64,128]{2,1,0:T(8,128)S(1)}, u32[]{:S(2)}, u32[]{:S(2)}) collective-permute-start(f32[16,64,128]{2,1,0:T(8,128)S(1)} %get-tuple-element.62), channel_id=1, source_target_pairs={{0,15},{1,2},{2,1},{3,4},{4,3},{5,6},{6,5},{7,8},{8,7},{9,10},{10,... | collective-permute-start | bytes 1572872 | tf_op jit(solution)/shard_map/ppermute | solution.py:361
  59.1 3.6 %collective-permute-start.8 = (f32[8,9,8,128]{3,2,1,0:T(8,128)S(1)}, f32[8,9,8,128]{3,2,1,0:T(8,128)S(1)}, u32[]{:S(2)}, u32[]{:S(2)}) collective-permute-start(f32[8,9,8,128]{3,2,1,0:T(8,128)S(1)} %get-tuple-element.64), channel_id=1, source_target_pairs={{0,1},{1,0},{2,3},{3,2},{4,5},{5,4},{6,7},{7,6},{8,9},{9,8},{10,11... | collective-permute-start | bytes 884744 | tf_op jit(solution)/shard_map/ppermute | solution.py:425
  61.5 18.3 %collective-permute-start.9 = (f32[16,64,128]{2,1,0:T(8,128)S(1)}, f32[16,64,128]{2,1,0:T(8,128)S(1)}, u32[]{:S(2)}, u32[]{:S(2)}) collective-permute-start(f32[16,64,128]{2,1,0:T(8,128)S(1)} %get-tuple-element.69), channel_id=1, source_target_pairs={{0,1},{1,0},{2,3},{3,2},{4,5},{5,4},{6,7},{7,6},{8,9},{9,8},{10,11... | collective-permute-start | bytes 1572872 | tf_op jit(solution)/shard_map/ppermute | solution.py:361
  61.6 18.2 %collective-permute-start.10 = (f32[16,64,128]{2,1,0:T(8,128)S(1)}, f32[16,64,128]{2,1,0:T(8,128)S(1)}, u32[]{:S(2)}, u32[]{:S(2)}) collective-permute-start(f32[16,64,128]{2,1,0:T(8,128)S(1)} %get-tuple-element.70), channel_id=1, source_target_pairs={{0,15},{1,2},{2,1},{3,4},{4,3},{5,6},{6,5},{7,8},{8,7},{9,10},{10,... | collective-permute-start | bytes 1572872 | tf_op jit(solution)/shard_map/ppermute | solution.py:361
  79.8 11.3 %all-to-all-start.1 = ((f32[8,8,8,128]{3,2,1,0:T(8,128)}), f32[8,8,8,128]{3,2,1,0:T(8,128)S(1)}, u32[]{:S(2)}, u32[]{:S(2)}) async-start(f32[8,8,8,128]{3,2,1,0:T(8,128)} %shard_map.92), calls=%async_computation.1 | async-start | bytes 524288 | tf_op jit(solution)/shard_map/all_to_all | solution.py:437
  91.1 3.4 %collective-permute-start.11 = (f32[8,8,8,128]{3,2,1,0:T(8,128)S(1)}, f32[8,8,8,128]{3,2,1,0:T(8,128)S(1)}, u32[]{:S(2)}, u32[]{:S(2)}) collective-permute-start(f32[8,8,8,128]{3,2,1,0:T(8,128)S(1)} %all-to-all-done.1.own), channel_id=1, source_target_pairs={{0,1},{1,0},{2,3},{3,2},{4,5},{5,4},{6,7},{7,6},{8,9},{9,8},{10,11... | collective-permute-start | bytes 786440 | tf_op jit(solution)/shard_map/ppermute | solution.py:448

commit v8 on v6

--- a/solution.py
+++ b/solution.py
@@ -127,14 +127,16 @@
 
 def pack_kernel(offsets, counts, measured, out):
     slots, _, pixels = measured.shape
+    half = pixels // 2
     for slot in range(slots):
         live = jnp.where(slot < counts[0], 1.0, 0.0).astype(F32)
         for odd in range(2):
-            rows = pl.ds(odd, pixels // 2, stride=2)
-            out[slot, odd * pixels // 2 : (odd + 1) * pixels // 2] = measured[slot, rows] * live
+            row = slot * pixels + odd * half
+            out[row : row + half] = measured[slot, pl.ds(odd, half, stride=2)] * live
         for entry in range(2):
             line = jnp.full((1, pixels), offsets[slot, entry], jnp.int32).astype(F32)
-            out[slots, 2 * slot + entry : 2 * slot + entry + 1] = line
+            row = slots * pixels + 2 * slot + entry
+            out[row : row + 1] = line
 
 
 def middle_kernel(pixels, target, tile, *outs):
@@ -142,8 +144,8 @@
     planes = tile.shape[0]
     for slot in range(offsets.shape[0]):
         for entry in range(2):
-            line = 2 * slot + entry
-            value = target[target.shape[0] - 1, line : line + 1]
+            line = target.shape[0] - 2 * offsets.shape[0] + 2 * slot + entry
+            value = target[line : line + 1]
             offsets[slot, entry] = jnp.max(value).astype(jnp.int32)
     slot = 0
     for part in parts:
@@ -190,28 +192,29 @@
             out[:, :, beside] += jnp.where(lane < shift, part, 0.0)
 
 
-def slot_kernel(first, size, ahead, own_offsets, *refs):
+def slot_kernel(first, size, earlier, own_offsets, *refs):
     offsets, mid, near, cross, target, probe, prop, tables, *refs = refs
     so_far, refs = (refs[0], refs[1:]) if first else (None, refs)
-    given, refs = refs[:ahead], refs[ahead:]
+    earlier, refs = refs[:earlier], refs[earlier:]
     out_near, out_mid, out_cross, *shares = refs[:-5]
     window, patch, grads, exit_wave, far = refs[-5:]
     total = shares.pop()
     modes, _, pixels, _ = probe.shape
     planes, rows = mid.shape[0] // size, mid.shape[1]
-    behind = given[0].shape[0] if given else 0
-    for message, out in zip(given, (out_near, out_cross)):
-        out[:behind] = message[...]
+    behind = 0
+    for strips in earlier:
+        out_near[behind : behind + strips.shape[0]] = strips[...]
+        behind += strips.shape[0]
     even = is_even(own_offsets, rows)
     total[...] = so_far[...] if first else jnp.zeros_like(total)
     held = range(BATCH)
 
     def is_live(at):
-        return jnp.max(target[first + at, :8]) > 0.0
+        return jnp.max(target[pl.ds((first + at) * pixels, 8)]) > 0.0
 
     def leave(slots):
         for at in slots:
-            for out, unit in ((out_near, behind), (out_mid, 0), (out_cross, behind)):
+            for out, unit in ((out_near, behind), (out_mid, 0), (out_cross, 0)):
                 out[pl.ds(unit + at * planes, planes)] = jnp.zeros((planes, rows, pixels), F32)
 
     def visit(slots):
@@ -242,7 +245,7 @@
                 wave = groups[s][m]
                 far[s, m, 0], far[s, m, 1] = wave
                 intensity = intensity + wave[0] * wave[0] + wave[1] * wave[1]
-            misfit = 2.0 * live[s] * (intensity - target[first + at])
+            misfit = 2.0 * live[s] * (intensity - target[pl.ds((first + at) * pixels, pixels)])
             groups[s] = [(misfit * far[s, m, 0], misfit * far[s, m, 1]) for m in all_modes]
         groups = transform(tables, True, groups)
         for s in held:
@@ -267,8 +270,8 @@
         for s, at in enumerate(slots):
             window[...] = jnp.zeros_like(window)
             window[:, pl.ds(starts[s], pixels), :] = grads[s]
-            strip = pl.ds(behind + at * planes, planes)
-            out_near[strip] = jnp.where(even, window[:, 2 * rows :], window[:, :rows])
+            strip = pl.ds(at * planes, planes)
+            out_near[pl.ds(behind + at * planes, planes)] = jnp.where(even, window[:, 2 * rows :], window[:, :rows])
             out_mid[pl.ds(at * planes, planes)] = window[:, rows : 2 * rows]
             out_cross[strip] = jnp.where(even, window[:, :rows], window[:, 2 * rows :])
 
@@ -332,7 +335,7 @@
     chunks = list(zip(starts, CHUNKS))
     target = pl.pallas_call(
         pack_kernel,
-        out_shape=jax.ShapeDtypeStruct((measured.shape[0] + 1, pixels, pixels), F32),
+        out_shape=jax.ShapeDtypeStruct((measured.shape[0] * pixels + offsets.size, pixels), F32),
         in_specs=[in_smem()] * 2 + [in_vmem()],
         out_specs=in_vmem(),
         compiler_params=params,
@@ -379,35 +382,33 @@
 
     share = pixels // peers
     total = ()
-    mid, back, mid_groups, back_groups = [], [], [], []
+    mid, back, groups, to_pair = [], [], [], []
     for index, (first, size) in enumerate(chunks):
-        given = waiting[index + 2] if index + 2 < len(chunks) else ()
-        ahead = CHUNKS[index + 2] * planes if given else 0
         sums = jax.ShapeDtypeStruct((2 * modes + 1, pixels, pixels), F32)
         part = jax.ShapeDtypeStruct((peers // 2, 2 * modes + 1, share, pixels), F32)
-        shares = [part, part] if index == len(CHUNKS) - 1 else []
-        message = units(ahead + size * planes)
+        last = index == len(chunks) - 1
+        message = units(size * planes)
         field = pltpu.VMEM((BATCH, planes, pixels, pixels), F32)
         kept = pltpu.VMEM((BATCH, modes, 2, pixels, pixels), F32)
+        results = [part, part] if last else [sums]
+        earlier = to_pair if last else []
+        near_units = units(sum(CHUNKS) * planes) if last else message
         to_near, to_mid, to_cross, *total = pl.pallas_call(
-            functools.partial(slot_kernel, first, size, len(given)),
-            out_shape=[message, units(size * planes), message] + (shares or [sums]),
-            in_specs=[in_smem()] * 2 + [in_vmem()] * (7 + len(total) + len(given)),
-            out_specs=[in_vmem()] * (3 + (len(shares) or 1)),
-            scratch_shapes=([pltpu.VMEM(sums.shape, F32)] if shares else [])
+            functools.partial(slot_kernel, first, size, len(earlier)),
+            out_shape=[near_units, message, message] + results,
+            in_specs=[in_smem()] * 2 + [in_vmem()] * (7 + len(total) + len(earlier)),
+            out_specs=[in_vmem()] * (3 + len(results)),
+            scratch_shapes=([pltpu.VMEM(sums.shape, F32)] if last else [])
             + [pltpu.VMEM((planes, 3 * tile_rows, pixels), F32), field, field, kept, kept],
             compiler_params=params,
             cost_estimate=pl.CostEstimate(
                 flops=size * 6 * modes * 3 * 16 * pixels**3, bytes_accessed=8 << 20, transcendentals=0
             ),
-        )(offsets, middle, middles[index], *arrived[index], target, probe_modes, prop, tables, *total, *given)
-        mid_groups.append(("mid", first, size, 0))
+        )(offsets, middle, middles[index], *arrived[index], target, probe_modes, prop, tables, *total, *earlier)
+        to_pair.append(to_near)
         mid.append(to_mid)
-        message = swapped(to_near, to_cross)
-        if given:
-            arrived.append(message)
-        back_groups += [(kind, first, size, ahead) for kind in ("near", "cross")]
-        back.append(message)
+        back.append(lax.ppermute(to_cross, ROW, other_pair))
+        groups += [("mid", first, size, 0), ("cross", first, size, 0), ("near", first, size, first * planes)]
 
     def added(groups, strips):
         return pl.pallas_call(
@@ -421,7 +422,9 @@
 
     own, other = total
     own, other, back[:-1] = lax.optimization_barrier((own, other, back[:-1]))
-    both = own + lax.ppermute(other, ROW, pair)
+    other, to_pair = lax.optimization_barrier((lax.ppermute(other, ROW, pair), to_pair[-1]))
+    from_pair = lax.ppermute(to_pair, ROW, pair)
+    both = own + other
     parts = lax.all_to_all(both, "chip", 0, 0)
     spread = pl.pallas_call(
         step_kernel,
@@ -430,8 +433,7 @@
         out_specs=in_vmem(),
         compiler_params=params,
     )(parts)
-    groups = mid_groups + back_groups
-    strips = mid + [part for message in back for part in message]
+    strips = [part for parts in zip(mid, back, [from_pair] * len(mid)) for part in parts]
     spread, strips = lax.optimization_barrier((spread, strips))
     gathered = lax.all_to_all(spread, "chip", 0, 0)
     object_grad = added(groups, strips)

time: 96.4 us -> 95.5 us (level); the launches traced: 95.5 us -> 95.7 us
  local copies, waits for them, and re-layouts: 3.43 us -> 6.29 us
  waiting for transfers between devices: 33.1 us -> 30.9 us
  blocking collectives: 14.9 us -> 17.1 us
  starting transfers between devices: 17.3 us -> 15.2 us
    ppermute x1 -> x4, waiting for transfers between devices: 0.01 us -> 11.9 us  [the longest x2 10.7 us: local(): back.append(lax.ppermute(to_cross, ROW, other_pair))]
    ppermute x4 -> x2, waiting for transfers between devices: 26.4 us -> 14.7 us  [swapped(): lax.ppermute(to_cross, ROW, other_pair)]
    ppermute x1 -> x4, starting transfers between devices: 0.01 us -> 4.53 us  [the longest x1 2.36 us: local(): lax.ppermute(other, ROW, pair)]
    unnamed x13 -> x21, local copies, waits for them, and re-layouts: 3.4 us -> 6.26 us
    all_to_all x1, starting transfers between devices: 6.22 us -> 3.41 us  [local(): gathered = lax.all_to_all(spread, 'chip', 0, 0)]
    ppermute x4 -> x2, starting transfers between devices: 3.57 us -> 1.12 us  [swapped(): lax.ppermute(to_cross, ROW, other_pair)]
    all_to_all x1, blocking collectives: 14.9 us -> 17.1 us  [local(): parts = lax.all_to_all(both, 'chip', 0, 0)]
    all_to_all x1, waiting for transfers between devices: 3.38 us -> 1.39 us  [local(): gathered = lax.all_to_all(spread, 'chip', 0, 0)]
  transfers between devices with their start and end apart: 13 -> 12, of which waited for: 7 -> 7; matrix products, arithmetic and copies ran while one was open for 0% -> 0% of each run, Pallas kernels for 25% -> 24%
where the time goes in v8:
time: 95.5 us; the launch traced here: 95.7 us
  waiting for transfers between devices  30.9 us (32%)
  Pallas kernels  24.5 us (26%)
  blocking collectives  17.1 us (18%)
  starting transfers between devices  15.2 us (16%)
  local copies, waits for them, and re-layouts  6.29 us (7%)
  between operations  1.46 us (2%)
    all_to_all x1, blocking collectives, local(): parts = lax.all_to_all(both, 'chip', 0, 0)  17.1 us
    ppermute x2, waiting for transfers between devices, swapped(): lax.ppermute(to_cross, ROW, other_pair)  14.7 us
    pallas_call x2, Pallas kernels, local(): pl.pallas_call(functools.partial(slot_kernel, first, size, len(earlier)),...  13.1 us
    ppermute x2, waiting for transfers between devices, local(): back.append(lax.ppermute(to_cross, ROW, other_pair))  10.7 us
    unnamed x21, local copies, waits for them, and re-layouts  6.26 us
    pallas_call x1, Pallas kernels, added(): pl.pallas_call(functools.partial(add_kernel, pixels, groups), out_shape=j...  3.78 us
    pallas_call x2, Pallas kernels, strips(): pl.pallas_call(functools.partial(cut_kernel, pixels, chunks), out_shape=s...  3.49 us
    all_to_all x1, starting transfers between devices, local(): gathered = lax.all_to_all(spread, 'chip', 0, 0)  3.41 us
  transfers between devices with their start and end apart: 12, of which 7 were waited for; matrix products, arithmetic and copies ran while one was open for 0% of the time, Pallas kernels for 24%

profile of v8, /device:TPU:1, one launch (start us, length us, event | category | flops | bytes accessed | tf_op | source)
XLA Modules:
  0.0 95.7 jit_solution(12814572216683866744)
XLA Ops:
  0.6 0.8 copy.14.offsets.own.own_offsets
  1.4 2.1 %collective-permute-start = (s32[8,2]{1,0:T(8,128)S(1)}, s32[8,2]{1,0:T(8,128)S(1)}, u32[]{:S(2)}, u32[]{:S(2)}) collective-permute-start(s32[8,2]{1,0:T(8,128)S(1)} %copy.14.offsets.own.own_offsets), channel_id=1, source_target_pairs={{0,2},{1,3},{2,4},{3,5},{4,6},{5,7},{6,8},{7,9},{8,10},{9,11},{10,... | collective-permute-start | bytes 200 | tf_op jit(solution)/shard_map/ppermute | solution.py:21
  4.1 0.0 copy-start.2
  4.1 1.0 %copy-done.2 = f32[8,128,128]{2,1,0:T(8,128)S(1)} copy-done((f32[8,128,128]{2,1,0:T(8,128)S(1)}, f32[8,128,128]{2,1,0:T(8,128)}, u32[]{:S(2)}) %copy-start.2) | copy-done | bytes 524312
  5.2 0.6 shard_map.86
  5.8 1.7 %collective-permute-done.far = s32[8,2]{1,0:T(8,128)S(1)} collective-permute-done((s32[8,2]{1,0:T(8,128)S(1)}, s32[8,2]{1,0:T(8,128)S(1)}, u32[]{:S(2)}, u32[]{:S(2)}) %collective-permute-start) | collective-permute-done | bytes 96 | tf_op jit(solution)/shard_map/ppermute | solution.py:21
  7.5 0.5 collective-permute-start.1
  7.9 1.6 %copy-done = f32[2,2,64,2048]{3,2,1,0:T(8,128)S(1)} copy-done((f32[2,2,64,2048]{3,2,1,0:T(8,128)S(1)}, f32[2,2,64,2048]{3,2,1,0:T(8,128)}, u32[]{:S(2)}) %copy-start) | copy-done | bytes 2097176
  9.5 2.2 %shard_map.88 = (f32[16,64,128]{2,1,0:T(8,128)}, f32[16,64,128]{2,1,0:T(8,128)}) custom-call(s32[8,2]{1,0:T(8,128)S(1)} %copy.14.offsets.own.own_offsets, s32[8,2]{1,0:T(8,128)S(1)} %collective-permute-done.far, f32[4,64,2048]{2,1,0:T(8,128)S(1)} %bitcast.5), custom_call_target="tpu_custom_call" | custom-call | bytes 4194304 | tf_op jit(solution)/shard_map/pallas_call | solution.py:352
  11.7 1.1 %collective-permute-start.2 = (f32[16,64,128]{2,1,0:T(8,128)}, f32[16,64,128]{2,1,0:T(8,128)}, u32[]{:S(2)}, u32[]{:S(2)}) collective-permute-start(f32[16,64,128]{2,1,0:T(8,128)} %get-tuple-element.46), channel_id=1, source_target_pairs={{0,1},{1,0},{2,3},{3,2},{4,5},{5,4},{6,7},{7,6},{8,9},{9,8},{10,11... | collective-permute-start | bytes 1572872 | tf_op jit(solution)/shard_map/ppermute | solution.py:363
  12.8 1.1 %collective-permute-start.3 = (f32[16,64,128]{2,1,0:T(8,128)}, f32[16,64,128]{2,1,0:T(8,128)}, u32[]{:S(2)}, u32[]{:S(2)}) collective-permute-start(f32[16,64,128]{2,1,0:T(8,128)} %get-tuple-element.47), channel_id=1, source_target_pairs={{0,15},{1,2},{2,1},{3,4},{4,3},{5,6},{6,5},{7,8},{8,7},{9,10},{10,... | collective-permute-start | bytes 1572872 | tf_op jit(solution)/shard_map/ppermute | solution.py:363
  13.9 0.0 copy-done.9
  14.0 0.2 fusion.1
  14.2 0.0 copy-start.7
  14.3 0.0 copy-start.8
  14.3 0.0 collective-permute-done.1.target.refs_4_
  14.3 1.3 %shard_map.89 = (f32[16,64,128]{2,1,0:T(8,128)S(1)}, f32[16,64,128]{2,1,0:T(8,128)S(1)}) custom-call(s32[8,2]{1,0:T(8,128)S(1)} %copy.14.offsets.own.own_offsets, s32[8,2]{1,0:T(8,128)S(1)} %collective-permute-done.far, f32[4,64,2048]{2,1,0:T(8,128)S(1)} %bitcast.6), custom_call_target="tpu_custom_call" | custom-call | bytes 4194304 | tf_op jit(solution)/shard_map/pallas_call | solution.py:352
  15.6 1.3 %shard_map.87 = (f32[16,64,128]{2,1,0:T(8,128)S(1)}, f32[16,64,128]{2,1,0:T(8,128)S(1)}, s32[8,2]{1,0:T(8,128)S(1)}) custom-call(f32[1040,128]{1,0:T(8,128)S(1)} %collective-permute-done.1.target.refs_4_, f32[4,64,2048]{2,1,0:T(8,128)S(1)} %bitcast.7), custom_call_target="tpu_custom_call" | custom-call | bytes 4194304 | tf_op jit(solution)/shard_map/pallas_call | solution.py:367
  16.9 0.0 collective-permute-done.2.refs_2_
  16.9 14.2 %collective-permute-done.3.refs_3_ = f32[16,64,128]{2,1,0:T(8,128)} collective-permute-done((f32[16,64,128]{2,1,0:T(8,128)}, f32[16,64,128]{2,1,0:T(8,128)}, u32[]{:S(2)}, u32[]{:S(2)}) %collective-permute-start.3) | collective-permute-done | bytes 524320 | tf_op jit(solution)/shard_map/ppermute | solution.py:363
  31.1 0.0 collective-permute-start.4
  31.1 0.0 collective-permute-start.5
  31.1 0.0 copy-done.7
  31.1 11.9 %shard_map.90 = (f32[16,64,128]{2,1,0:T(8,128)S(1)}, f32[16,64,128]{2,1,0:T(8,128)S(1)}, f32[16,64,128]{2,1,0:T(8,128)S(1)}, f32[9,128,128]{2,1,0:T(8,128)S(1)}) custom-call(s32[8,2]{1,0:T(8,128)S(1)} %copy.14.offsets.own.own_offsets, s32[8,2]{1,0:T(8,128)S(1)} %get-tuple-element.45.refs_0_.middle, f32[16,64,128]{2,1,0:T(8,128)S(1)} %get-tuple-element.56.refs_1_, ...), custom_call_target="tpu_custom_call" | custom-call | flops 9663676416 | bytes 8388608 | tf_op jit(solution)/shard_map/pallas_call | solution.py:396
  43.0 1.8 %collective-permute-start.6 = (f32[16,64,128]{2,1,0:T(8,128)S(1)}, f32[16,64,128]{2,1,0:T(8,128)S(1)}, u32[]{:S(2)}, u32[]{:S(2)}) collective-permute-start(f32[16,64,128]{2,1,0:T(8,128)S(1)} %get-tuple-element.63), channel_id=1, source_target_pairs={{0,15},{1,2},{2,1},{3,4},{4,3},{5,6},{6,5},{7,8},{8,7},{9,10},{10,... | collective-permute-start | bytes 1572872 | tf_op jit(solution)/shard_map/ppermute | solution.py:410
  44.8 0.0 collective-permute-done.4.refs_2_
  44.8 0.5 collective-permute-done.5.refs_3_
  45.3 1.2 %shard_map.91 = (f32[32,64,128]{2,1,0:T(8,128)S(1)}, f32[16,64,128]{2,1,0:T(8,128)S(1)}, f32[16,64,128]{2,1,0:T(8,128)S(1)}, f32[8,9,8,128]{3,2,1,0:T(8,128)S(1)}, f32[8,9,8,128]{3,2,1,0:T(8,128)S(1)}) custom-call(s32[8,2]{1,0:T(8,128)S(1)} %copy.14.offsets.own.own_offsets, s32[8,2]{1,0:T(8,128)S(1)} %get-tuple-element.45.refs_0_.middle, ...), custom_call_target="tpu_custom_call" | custom-call | flops 9663676416 | bytes 8388608 | tf_op jit(solution)/shard_map/pallas_call | solution.py:396
  46.5 0.0 copy-start.3
  46.6 10.7 %collective-permute-done.6.refs_1_ = f32[16,64,128]{2,1,0:T(8,128)S(1)} collective-permute-done((f32[16,64,128]{2,1,0:T(8,128)S(1)}, f32[16,64,128]{2,1,0:T(8,128)S(1)}, u32[]{:S(2)}, u32[]{:S(2)}) %collective-permute-start.6) | collective-permute-done | bytes 524320 | tf_op jit(solution)/shard_map/ppermute | solution.py:410
  57.3 2.4 %collective-permute-start.7 = (f32[8,9,8,128]{3,2,1,0:T(8,128)S(1)}, f32[8,9,8,128]{3,2,1,0:T(8,128)S(1)}, u32[]{:S(2)}, u32[]{:S(2)}) collective-permute-start(f32[8,9,8,128]{3,2,1,0:T(8,128)S(1)} %get-tuple-element.65), channel_id=1, source_target_pairs={{0,1},{1,0},{2,3},{3,2},{4,5},{5,4},{6,7},{7,6},{8,9},{9,8},{10,11... | collective-permute-start | bytes 884744 | tf_op jit(solution)/shard_map/ppermute | solution.py:425
  59.6 1.2 %collective-permute-done.7 = f32[8,9,8,128]{3,2,1,0:T(8,128)S(1)} collective-permute-done((f32[8,9,8,128]{3,2,1,0:T(8,128)S(1)}, f32[8,9,8,128]{3,2,1,0:T(8,128)S(1)}, u32[]{:S(2)}, u32[]{:S(2)}) %collective-permute-start.7) | collective-permute-done | bytes 294944 | tf_op jit(solution)/shard_map/ppermute | solution.py:425
  60.8 0.4 collective-permute-start.8
  61.2 0.0 collective-permute-start.9
  61.3 17.1 %all_to_all.10.parts = f32[8,9,8,128]{3,2,1,0:T(8,128)S(1)} all-to-all(f32[8,9,8,128]{3,2,1,0:T(8,128)S(1)} %add.3), channel_id=1, replica_groups=mesh['grp'=2,'chip'=8,'core'=2] {'chip'}, dimensions={0} | all-to-all | bytes 589824 | tf_op jit(solution)/shard_map/all_to_all | solution.py:428
  78.3 0.7 shard_map.92
  79.1 0.0 collective-permute-done.9.refs_4_
  79.1 0.0 collective-permute-done.8.refs_2_.refs_5_
  79.1 0.8 copy-done.5
  79.9 3.4 %all-to-all-start.1 = ((f32[8,8,8,128]{3,2,1,0:T(8,128)}), f32[8,8,8,128]{3,2,1,0:T(8,128)S(1)}, u32[]{:S(2)}, u32[]{:S(2)}) async-start(f32[8,8,8,128]{3,2,1,0:T(8,128)} %shard_map.92), calls=%async_computation.1 | async-start | bytes 524288 | tf_op jit(solution)/shard_map/all_to_all | solution.py:438
  83.3 0.0 copy-start.4
  83.3 1.0 %copy-done.4 = f32[16,64,128]{2,1,0:T(8,128)S(1)} copy-done((f32[16,64,128]{2,1,0:T(8,128)S(1)}, f32[16,64,128]{2,1,0:T(8,128)}, u32[]{:S(2)}) %copy-start.4) | copy-done | bytes 524312
  84.3 1.0 %copy-done.6 = f32[16,64,128]{2,1,0:T(8,128)S(1)} copy-done((f32[16,64,128]{2,1,0:T(8,128)S(1)}, f32[16,64,128]{2,1,0:T(8,128)}, u32[]{:S(2)}) %copy-start.6) | copy-done | bytes 524312
  85.4 3.8 %shard_map.93 = f32[4,64,2048]{2,1,0:T(8,128)} custom-call(s32[8,2]{1,0:T(8,128)S(1)} %copy.14.offsets.own.own_offsets, s32[8,2]{1,0:T(8,128)S(1)} %get-tuple-element.45.refs_0_.middle, s32[8,2]{1,0:T(8,128)S(1)} %collective-permute-done.far, f32[16,64,128]{2,1,0:T(8,128)S(1)} %get-tuple-element.74.refs_0_, ...), custom_call_target="tpu_custom_call" | custom-call | bytes 5242880 | tf_op jit(solution)/shard_map/pallas_call | solution.py:414
  89.1 1.4 %all-to-all-done.1.own = f32[8,8,8,128]{3,2,1,0:T(8,128)S(1)} async-done(((f32[8,8,8,128]{3,2,1,0:T(8,128)}), f32[8,8,8,128]{3,2,1,0:T(8,128)S(1)}, u32[]{:S(2)}, u32[]{:S(2)}) %all-to-all-start.1) | async-done | bytes 262176 | tf_op jit(solution)/shard_map/all_to_all | solution.py:438
  90.5 2.5 %collective-permute-start.10 = (f32[8,8,8,128]{3,2,1,0:T(8,128)S(1)}, f32[8,8,8,128]{3,2,1,0:T(8,128)S(1)}, u32[]{:S(2)}, u32[]{:S(2)}) collective-permute-start(f32[8,8,8,128]{3,2,1,0:T(8,128)S(1)} %all-to-all-done.1.own), channel_id=1, source_target_pairs={{0,1},{1,0},{2,3},{3,2},{4,5},{5,4},{6,7},{7,6},{8,9},{9,8},{10,11... | collective-permute-start | bytes 786440 | tf_op jit(solution)/shard_map/ppermute | solution.py:449
  93.1 1.2 %collective-permute-done.10.other = f32[8,8,8,128]{3,2,1,0:T(8,128)S(1)} collective-permute-done((f32[8,8,8,128]{3,2,1,0:T(8,128)S(1)}, f32[8,8,8,128]{3,2,1,0:T(8,128)S(1)}, u32[]{:S(2)}, u32[]{:S(2)}) %collective-permute-start.10) | collective-permute-done | bytes 262176 | tf_op jit(solution)/shard_map/ppermute | solution.py:449
  94.2 1.5 %shard_map.94 = f32[8,128,128]{2,1,0:T(8,128)} custom-call(s32[8,2]{1,0:T(8,128)S(1)} %copy.14.offsets.own.own_offsets, f32[8,8,8,128]{3,2,1,0:T(8,128)S(1)} %all-to-all-done.1.own, f32[8,8,8,128]{3,2,1,0:T(8,128)S(1)} %collective-permute-done.10.other), custom_call_target="tpu_custom_call" | custom-call | tf_op jit(solution)/shard_map/pallas_call | solution.py:443
  (12 shorter events, 0.1 us)
Async XLA Ops:
  1.4 6.1 %collective-permute-start = (s32[8,2]{1,0:T(8,128)S(1)}, s32[8,2]{1,0:T(8,128)S(1)}, u32[]{:S(2)}, u32[]{:S(2)}) collective-permute-start(s32[8,2]{1,0:T(8,128)S(1)} %copy.14.offsets.own.own_offsets), channel_id=1, source_target_pairs={{0,2},{1,3},{2,4},{3,5},{4,6},{5,7},{6,8},{7,9},{8,10},{9,11},{10,... | collective-permute-start | bytes 200 | tf_op jit(solution)/shard_map/ppermute | solution.py:21
  4.1 1.0 %copy-start.2 = (f32[8,128,128]{2,1,0:T(8,128)S(1)}, f32[8,128,128]{2,1,0:T(8,128)}, u32[]{:S(2)}) copy-start(f32[8,128,128]{2,1,0:T(8,128)} %measured.1) | copy-start | bytes 1572868
  5.1 8.8 %copy-start.9 = (f32[128,128]{1,0:T(8,128)S(1)}, f32[128,128]{1,0:T(8,128)}, u32[]{:S(2)}) copy-start(f32[128,128]{1,0:T(8,128)} %param.9) | copy-start | bytes 196612
  7.5 6.8 %collective-permute-start.1 = (f32[1040,128]{1,0:T(8,128)S(1)}, f32[1040,128]{1,0:T(8,128)S(1)}, u32[]{:S(2)}, u32[]{:S(2)}) collective-permute-start(f32[1040,128]{1,0:T(8,128)S(1)} %shard_map.86), channel_id=1, source_target_pairs={{0,1},{1,2},{2,3},{3,4},{4,5},{5,6},{6,7},{7,8},{8,9},{9,10},{10,1... | collective-permute-start | bytes 1597448 | tf_op jit(solution)/shard_map/ppermute | solution.py:21
  7.9 1.6 %copy-start = (f32[2,2,64,2048]{3,2,1,0:T(8,128)S(1)}, f32[2,2,64,2048]{3,2,1,0:T(8,128)}, u32[]{:S(2)}) copy-start(f32[2,2,64,2048]{3,2,1,0:T(8,128)} %param.7) | copy-start | bytes 6291460
  9.5 4.7 %copy-start.1 = (f32[2,2,64,2048]{3,2,1,0:T(8,128)S(1)}, f32[2,2,64,2048]{3,2,1,0:T(8,128)}, u32[]{:S(2)}) copy-start(f32[2,2,64,2048]{3,2,1,0:T(8,128)} %param.7) | copy-start | bytes 6291460
  11.7 5.2 %collective-permute-start.2 = (f32[16,64,128]{2,1,0:T(8,128)}, f32[16,64,128]{2,1,0:T(8,128)}, u32[]{:S(2)}, u32[]{:S(2)}) collective-permute-start(f32[16,64,128]{2,1,0:T(8,128)} %get-tuple-element.46), channel_id=1, source_target_pairs={{0,1},{1,0},{2,3},{3,2},{4,5},{5,4},{6,7},{7,6},{8,9},{9,8},{10,11... | collective-permute-start | bytes 1572872 | tf_op jit(solution)/shard_map/ppermute | solution.py:363
  12.8 18.3 %collective-permute-start.3 = (f32[16,64,128]{2,1,0:T(8,128)}, f32[16,64,128]{2,1,0:T(8,128)}, u32[]{:S(2)}, u32[]{:S(2)}) collective-permute-start(f32[16,64,128]{2,1,0:T(8,128)} %get-tuple-element.47), channel_id=1, source_target_pairs={{0,15},{1,2},{2,1},{3,4},{4,3},{5,6},{6,5},{7,8},{8,7},{9,10},{10,... | collective-permute-start | bytes 1572872 | tf_op jit(solution)/shard_map/ppermute | solution.py:363
  14.2 16.8 %copy-start.7 = (f32[4,2,128,128]{3,2,1,0:T(8,128)S(1)}, f32[4,2,128,128]{3,2,1,0:T(8,128)}, u32[]{:S(2)}) copy-start(f32[4,2,128,128]{3,2,1,0:T(8,128)} %refs_5_.3) | copy-start | bytes 1572868
  14.3 16.8 %copy-start.8 = (bf16[8,256,256]{2,1,0:T(8,128)(2,1)S(1)}, bf16[8,256,256]{2,1,0:T(8,128)(2,1)}, u32[]{:S(2)}) copy-start(bf16[8,256,256]{2,1,0:T(8,128)(2,1)} %constant.2.clone.refs_7_) | copy-start | bytes 3145732
  31.1 13.7 %collective-permute-start.4 = (f32[16,64,128]{2,1,0:T(8,128)S(1)}, f32[16,64,128]{2,1,0:T(8,128)S(1)}, u32[]{:S(2)}, u32[]{:S(2)}) collective-permute-start(f32[16,64,128]{2,1,0:T(8,128)S(1)} %get-tuple-element.54), channel_id=1, source_target_pairs={{0,1},{1,0},{2,3},{3,2},{4,5},{5,4},{6,7},{7,6},{8,9},{9,8},{10,11... | collective-permute-start | bytes 1572872 | tf_op jit(solution)/shard_map/ppermute | solution.py:363
  31.1 14.2 %collective-permute-start.5 = (f32[16,64,128]{2,1,0:T(8,128)S(1)}, f32[16,64,128]{2,1,0:T(8,128)S(1)}, u32[]{:S(2)}, u32[]{:S(2)}) collective-permute-start(f32[16,64,128]{2,1,0:T(8,128)S(1)} %get-tuple-element.55), channel_id=1, source_target_pairs={{0,15},{1,2},{2,1},{3,4},{4,3},{5,6},{6,5},{7,8},{8,7},{9,10},{10,... | collective-permute-start | bytes 1572872 | tf_op jit(solution)/shard_map/ppermute | solution.py:363
  43.0 14.3 %collective-permute-start.6 = (f32[16,64,128]{2,1,0:T(8,128)S(1)}, f32[16,64,128]{2,1,0:T(8,128)S(1)}, u32[]{:S(2)}, u32[]{:S(2)}) collective-permute-start(f32[16,64,128]{2,1,0:T(8,128)S(1)} %get-tuple-element.63), channel_id=1, source_target_pairs={{0,15},{1,2},{2,1},{3,4},{4,3},{5,6},{6,5},{7,8},{8,7},{9,10},{10,... | collective-permute-start | bytes 1572872 | tf_op jit(solution)/shard_map/ppermute | solution.py:410
  46.5 32.5 %copy-start.3 = (f32[16,64,128]{2,1,0:T(8,128)}, f32[16,64,128]{2,1,0:T(8,128)S(1)}, u32[]{:S(2)}) copy-start(f32[16,64,128]{2,1,0:T(8,128)S(1)} %get-tuple-element.77.refs_3_) | copy-start | bytes 1572868
  57.3 3.6 %collective-permute-start.7 = (f32[8,9,8,128]{3,2,1,0:T(8,128)S(1)}, f32[8,9,8,128]{3,2,1,0:T(8,128)S(1)}, u32[]{:S(2)}, u32[]{:S(2)}) collective-permute-start(f32[8,9,8,128]{3,2,1,0:T(8,128)S(1)} %get-tuple-element.65), channel_id=1, source_target_pairs={{0,1},{1,0},{2,3},{3,2},{4,5},{5,4},{6,7},{7,6},{8,9},{9,8},{10,11... | collective-permute-start | bytes 884744 | tf_op jit(solution)/shard_map/ppermute | solution.py:425
  60.8 18.2 %collective-permute-start.8 = (f32[32,64,128]{2,1,0:T(8,128)S(1)}, f32[32,64,128]{2,1,0:T(8,128)S(1)}, u32[]{:S(2)}, u32[]{:S(2)}) collective-permute-start(f32[32,64,128]{2,1,0:T(8,128)S(1)} %get-tuple-element.70), channel_id=1, source_target_pairs={{0,1},{1,0},{2,3},{3,2},{4,5},{5,4},{6,7},{7,6},{8,9},{9,8},{10,11... | collective-permute-start | bytes 3145736 | tf_op jit(solution)/shard_map/ppermute | solution.py:426
  61.2 17.8 %collective-permute-start.9 = (f32[16,64,128]{2,1,0:T(8,128)S(1)}, f32[16,64,128]{2,1,0:T(8,128)S(1)}, u32[]{:S(2)}, u32[]{:S(2)}) collective-permute-start(f32[16,64,128]{2,1,0:T(8,128)S(1)} %get-tuple-element.72), channel_id=1, source_target_pairs={{0,15},{1,2},{2,1},{3,4},{4,3},{5,6},{6,5},{7,8},{8,7},{9,10},{10,... | collective-permute-start | bytes 1572872 | tf_op jit(solution)/shard_map/ppermute | solution.py:410
  79.1 0.8 copy-start.5
  79.9 10.7 %all-to-all-start.1 = ((f32[8,8,8,128]{3,2,1,0:T(8,128)}), f32[8,8,8,128]{3,2,1,0:T(8,128)S(1)}, u32[]{:S(2)}, u32[]{:S(2)}) async-start(f32[8,8,8,128]{3,2,1,0:T(8,128)} %shard_map.92), calls=%async_computation.1 | async-start | bytes 524288 | tf_op jit(solution)/shard_map/all_to_all | solution.py:438
  83.3 1.0 %copy-start.4 = (f32[16,64,128]{2,1,0:T(8,128)S(1)}, f32[16,64,128]{2,1,0:T(8,128)}, u32[]{:S(2)}) copy-start(f32[16,64,128]{2,1,0:T(8,128)} %copy-done.3) | copy-start | bytes 1572868
  84.3 1.0 %copy-start.6 = (f32[16,64,128]{2,1,0:T(8,128)S(1)}, f32[16,64,128]{2,1,0:T(8,128)}, u32[]{:S(2)}) copy-start(f32[16,64,128]{2,1,0:T(8,128)} %copy-done.5) | copy-start | bytes 1572868
  90.5 3.7 %collective-permute-start.10 = (f32[8,8,8,128]{3,2,1,0:T(8,128)S(1)}, f32[8,8,8,128]{3,2,1,0:T(8,128)S(1)}, u32[]{:S(2)}, u32[]{:S(2)}) collective-permute-start(f32[8,8,8,128]{3,2,1,0:T(8,128)S(1)} %all-to-all-done.1.own), channel_id=1, source_target_pairs={{0,1},{1,0},{2,3},{3,2},{4,5},{5,4},{6,7},{7,6},{8,9},{9,8},{10,11... | collective-permute-start | bytes 786440 | tf_op jit(solution)/shard_map/ppermute | solution.py:449

commit v9 on v8

--- a/solution.py
+++ b/solution.py
@@ -10,7 +10,7 @@
 
 CHUNKS = (4, 4)
 BATCH = 4
-VMEM_LIMIT = 40 * 1024 * 1024
+VMEM_LIMIT = 32 * 1024 * 1024
 ROW = ("chip", "core")
 F32 = jnp.float32
 BF16 = jnp.bfloat16

time: 95.5 us -> 95.6 us (level); the launches traced: 95.7 us -> 93.8 us
  starting transfers between devices: 15.2 us -> 13.7 us
  blocking collectives: 17.1 us -> 15.9 us
    ppermute x1, starting transfers between devices: 2.36 us -> 0.01 us  [local(): lax.ppermute(other, ROW, pair)]
    ppermute x2, starting transfers between devices: 1.8 us -> 3.2 us  [local(): back.append(lax.ppermute(to_cross, ROW, other_pair))]
    all_to_all x1, blocking collectives: 17.1 us -> 15.9 us  [local(): parts = lax.all_to_all(both, 'chip', 0, 0)]
  transfers between devices with their start and end apart: 12 -> 12, of which waited for: 7 -> 7; matrix products, arithmetic and copies ran while one was open for 0% -> 0% of each run, Pallas kernels for 24% -> 25%
where the time goes in v9:
time: 95.6 us; the launch traced here: 93.8 us
  waiting for transfers between devices  31.5 us (33%)
  Pallas kernels  24.5 us (26%)
  blocking collectives  15.9 us (17%)
  starting transfers between devices  13.7 us (14%)
  local copies, waits for them, and re-layouts  6.29 us (7%)
  between operations  1.46 us (2%)
    all_to_all x1, blocking collectives, local(): parts = lax.all_to_all(both, 'chip', 0, 0)  15.9 us
    ppermute x2, waiting for transfers between devices, swapped(): lax.ppermute(to_cross, ROW, other_pair)  14.7 us
    pallas_call x2, Pallas kernels, local(): pl.pallas_call(functools.partial(slot_kernel, first, size, len(earlier)),...  13.1 us
    ppermute x2, waiting for transfers between devices, local(): back.append(lax.ppermute(to_cross, ROW, other_pair))  10.7 us
    unnamed x21, local copies, waits for them, and re-layouts  6.26 us
    pallas_call x1, Pallas kernels, added(): pl.pallas_call(functools.partial(add_kernel, pixels, groups), out_shape=j...  3.79 us
    pallas_call x2, Pallas kernels, strips(): pl.pallas_call(functools.partial(cut_kernel, pixels, chunks), out_shape=s...  3.49 us
    all_to_all x1, starting transfers between devices, local(): gathered = lax.all_to_all(spread, 'chip', 0, 0)  3.41 us
  transfers between devices with their start and end apart: 12, of which 7 were waited for; matrix products, arithmetic and copies ran while one was open for 0% of the time, Pallas kernels for 25%

profile of v9, /device:TPU:1, one launch (start us, length us, event | category | flops | bytes accessed | tf_op | source)
XLA Modules:
  0.0 93.8 jit_solution(12300190795371893762)
XLA Ops:
  0.6 0.8 copy.14.offsets.own.own_offsets
  1.4 2.1 %collective-permute-start = (s32[8,2]{1,0:T(8,128)S(1)}, s32[8,2]{1,0:T(8,128)S(1)}, u32[]{:S(2)}, u32[]{:S(2)}) collective-permute-start(s32[8,2]{1,0:T(8,128)S(1)} %copy.14.offsets.own.own_offsets), channel_id=1, source_target_pairs={{0,2},{1,3},{2,4},{3,5},{4,6},{5,7},{6,8},{7,9},{8,10},{9,11},{10,... | collective-permute-start | bytes 200 | tf_op jit(solution)/shard_map/ppermute | solution.py:21
  4.1 0.0 copy-start.2
  4.1 1.0 %copy-done.2 = f32[8,128,128]{2,1,0:T(8,128)S(1)} copy-done((f32[8,128,128]{2,1,0:T(8,128)S(1)}, f32[8,128,128]{2,1,0:T(8,128)}, u32[]{:S(2)}) %copy-start.2) | copy-done | bytes 524312
  5.2 0.6 shard_map.86
  5.8 1.7 %collective-permute-done.far = s32[8,2]{1,0:T(8,128)S(1)} collective-permute-done((s32[8,2]{1,0:T(8,128)S(1)}, s32[8,2]{1,0:T(8,128)S(1)}, u32[]{:S(2)}, u32[]{:S(2)}) %collective-permute-start) | collective-permute-done | bytes 96 | tf_op jit(solution)/shard_map/ppermute | solution.py:21
  7.5 0.5 collective-permute-start.1
  7.9 1.6 %copy-done = f32[2,2,64,2048]{3,2,1,0:T(8,128)S(1)} copy-done((f32[2,2,64,2048]{3,2,1,0:T(8,128)S(1)}, f32[2,2,64,2048]{3,2,1,0:T(8,128)}, u32[]{:S(2)}) %copy-start) | copy-done | bytes 2097176
  9.5 2.2 %shard_map.88 = (f32[16,64,128]{2,1,0:T(8,128)}, f32[16,64,128]{2,1,0:T(8,128)}) custom-call(s32[8,2]{1,0:T(8,128)S(1)} %copy.14.offsets.own.own_offsets, s32[8,2]{1,0:T(8,128)S(1)} %collective-permute-done.far, f32[4,64,2048]{2,1,0:T(8,128)S(1)} %bitcast.5), custom_call_target="tpu_custom_call" | custom-call | bytes 4194304 | tf_op jit(solution)/shard_map/pallas_call | solution.py:352
  11.7 1.1 %collective-permute-start.2 = (f32[16,64,128]{2,1,0:T(8,128)}, f32[16,64,128]{2,1,0:T(8,128)}, u32[]{:S(2)}, u32[]{:S(2)}) collective-permute-start(f32[16,64,128]{2,1,0:T(8,128)} %get-tuple-element.46), channel_id=1, source_target_pairs={{0,1},{1,0},{2,3},{3,2},{4,5},{5,4},{6,7},{7,6},{8,9},{9,8},{10,11... | collective-permute-start | bytes 1572872 | tf_op jit(solution)/shard_map/ppermute | solution.py:363
  12.8 1.1 %collective-permute-start.3 = (f32[16,64,128]{2,1,0:T(8,128)}, f32[16,64,128]{2,1,0:T(8,128)}, u32[]{:S(2)}, u32[]{:S(2)}) collective-permute-start(f32[16,64,128]{2,1,0:T(8,128)} %get-tuple-element.47), channel_id=1, source_target_pairs={{0,15},{1,2},{2,1},{3,4},{4,3},{5,6},{6,5},{7,8},{8,7},{9,10},{10,... | collective-permute-start | bytes 1572872 | tf_op jit(solution)/shard_map/ppermute | solution.py:363
  13.9 0.0 copy-done.9
  14.0 0.2 fusion.1
  14.2 0.0 copy-start.7
  14.3 0.0 copy-start.8
  14.3 0.0 collective-permute-done.1.target.refs_4_
  14.3 0.0 copy-done.1
  14.3 1.3 %shard_map.89 = (f32[16,64,128]{2,1,0:T(8,128)S(1)}, f32[16,64,128]{2,1,0:T(8,128)S(1)}) custom-call(s32[8,2]{1,0:T(8,128)S(1)} %copy.14.offsets.own.own_offsets, s32[8,2]{1,0:T(8,128)S(1)} %collective-permute-done.far, f32[4,64,2048]{2,1,0:T(8,128)S(1)} %bitcast.6), custom_call_target="tpu_custom_call" | custom-call | bytes 4194304 | tf_op jit(solution)/shard_map/pallas_call | solution.py:352
  15.6 1.3 %shard_map.87 = (f32[16,64,128]{2,1,0:T(8,128)S(1)}, f32[16,64,128]{2,1,0:T(8,128)S(1)}, s32[8,2]{1,0:T(8,128)S(1)}) custom-call(f32[1040,128]{1,0:T(8,128)S(1)} %collective-permute-done.1.target.refs_4_, f32[4,64,2048]{2,1,0:T(8,128)S(1)} %bitcast.7), custom_call_target="tpu_custom_call" | custom-call | bytes 4194304 | tf_op jit(solution)/shard_map/pallas_call | solution.py:367
  16.9 0.0 collective-permute-done.2.refs_2_
  16.9 14.2 %collective-permute-done.3.refs_3_ = f32[16,64,128]{2,1,0:T(8,128)} collective-permute-done((f32[16,64,128]{2,1,0:T(8,128)}, f32[16,64,128]{2,1,0:T(8,128)}, u32[]{:S(2)}, u32[]{:S(2)}) %collective-permute-start.3) | collective-permute-done | bytes 524320 | tf_op jit(solution)/shard_map/ppermute | solution.py:363
  31.1 0.0 collective-permute-start.4
  31.1 0.0 collective-permute-start.5
  31.1 11.9 %shard_map.90 = (f32[16,64,128]{2,1,0:T(8,128)S(1)}, f32[16,64,128]{2,1,0:T(8,128)S(1)}, f32[16,64,128]{2,1,0:T(8,128)S(1)}, f32[9,128,128]{2,1,0:T(8,128)S(1)}) custom-call(s32[8,2]{1,0:T(8,128)S(1)} %copy.14.offsets.own.own_offsets, s32[8,2]{1,0:T(8,128)S(1)} %get-tuple-element.45.refs_0_.middle, f32[16,64,128]{2,1,0:T(8,128)S(1)} %get-tuple-element.56.refs_1_, ...), custom_call_target="tpu_custom_call" | custom-call | flops 9663676416 | bytes 8388608 | tf_op jit(solution)/shard_map/pallas_call | solution.py:396
  43.0 1.8 %collective-permute-start.6 = (f32[16,64,128]{2,1,0:T(8,128)S(1)}, f32[16,64,128]{2,1,0:T(8,128)S(1)}, u32[]{:S(2)}, u32[]{:S(2)}) collective-permute-start(f32[16,64,128]{2,1,0:T(8,128)S(1)} %get-tuple-element.63), channel_id=1, source_target_pairs={{0,15},{1,2},{2,1},{3,4},{4,3},{5,6},{6,5},{7,8},{8,7},{9,10},{10,... | collective-permute-start | bytes 1572872 | tf_op jit(solution)/shard_map/ppermute | solution.py:410
  44.8 0.0 collective-permute-done.4.refs_2_
  44.8 0.5 collective-permute-done.5.refs_3_
  45.3 1.2 %shard_map.91 = (f32[32,64,128]{2,1,0:T(8,128)S(1)}, f32[16,64,128]{2,1,0:T(8,128)S(1)}, f32[16,64,128]{2,1,0:T(8,128)S(1)}, f32[8,9,8,128]{3,2,1,0:T(8,128)S(1)}, f32[8,9,8,128]{3,2,1,0:T(8,128)S(1)}) custom-call(s32[8,2]{1,0:T(8,128)S(1)} %copy.14.offsets.own.own_offsets, s32[8,2]{1,0:T(8,128)S(1)} %get-tuple-element.45.refs_0_.middle, ...), custom_call_target="tpu_custom_call" | custom-call | flops 9663676416 | bytes 8388608 | tf_op jit(solution)/shard_map/pallas_call | solution.py:396
  46.5 0.0 copy-start.3
  46.6 10.7 %collective-permute-done.6.refs_1_ = f32[16,64,128]{2,1,0:T(8,128)S(1)} collective-permute-done((f32[16,64,128]{2,1,0:T(8,128)S(1)}, f32[16,64,128]{2,1,0:T(8,128)S(1)}, u32[]{:S(2)}, u32[]{:S(2)}) %collective-permute-start.6) | collective-permute-done | bytes 524320 | tf_op jit(solution)/shard_map/ppermute | solution.py:410
  57.3 0.0 collective-permute-start.7
  57.3 1.6 %collective-permute-done.7 = f32[8,9,8,128]{3,2,1,0:T(8,128)S(1)} collective-permute-done((f32[8,9,8,128]{3,2,1,0:T(8,128)S(1)}, f32[8,9,8,128]{3,2,1,0:T(8,128)S(1)}, u32[]{:S(2)}, u32[]{:S(2)}) %collective-permute-start.7) | collective-permute-done | bytes 294944 | tf_op jit(solution)/shard_map/ppermute | solution.py:425
  58.9 0.1 collective-permute-start.8
  59.0 1.4 %collective-permute-start.9 = (f32[16,64,128]{2,1,0:T(8,128)S(1)}, f32[16,64,128]{2,1,0:T(8,128)S(1)}, u32[]{:S(2)}, u32[]{:S(2)}) collective-permute-start(f32[16,64,128]{2,1,0:T(8,128)S(1)} %get-tuple-element.72), channel_id=1, source_target_pairs={{0,15},{1,2},{2,1},{3,4},{4,3},{5,6},{6,5},{7,8},{8,7},{9,10},{10,... | collective-permute-start | bytes 1572872 | tf_op jit(solution)/shard_map/ppermute | solution.py:410
  60.4 15.9 %all_to_all.10.parts = f32[8,9,8,128]{3,2,1,0:T(8,128)S(1)} all-to-all(f32[8,9,8,128]{3,2,1,0:T(8,128)S(1)} %add.3), channel_id=1, replica_groups=mesh['grp'=2,'chip'=8,'core'=2] {'chip'}, dimensions={0} | all-to-all | bytes 589824 | tf_op jit(solution)/shard_map/all_to_all | solution.py:428
  76.4 0.7 shard_map.92
  77.1 0.0 collective-permute-done.9.refs_4_
  77.1 0.0 collective-permute-done.8.refs_2_.refs_5_
  77.1 0.8 copy-done.5
  77.9 3.4 %all-to-all-start.1 = ((f32[8,8,8,128]{3,2,1,0:T(8,128)}), f32[8,8,8,128]{3,2,1,0:T(8,128)S(1)}, u32[]{:S(2)}, u32[]{:S(2)}) async-start(f32[8,8,8,128]{3,2,1,0:T(8,128)} %shard_map.92), calls=%async_computation.1 | async-start | bytes 524288 | tf_op jit(solution)/shard_map/all_to_all | solution.py:438
  81.3 0.0 copy-start.4
  81.3 1.0 %copy-done.4 = f32[16,64,128]{2,1,0:T(8,128)S(1)} copy-done((f32[16,64,128]{2,1,0:T(8,128)S(1)}, f32[16,64,128]{2,1,0:T(8,128)}, u32[]{:S(2)}) %copy-start.4) | copy-done | bytes 524312
  82.4 1.0 %copy-done.6 = f32[16,64,128]{2,1,0:T(8,128)S(1)} copy-done((f32[16,64,128]{2,1,0:T(8,128)S(1)}, f32[16,64,128]{2,1,0:T(8,128)}, u32[]{:S(2)}) %copy-start.6) | copy-done | bytes 524312
  83.4 3.8 %shard_map.93 = f32[4,64,2048]{2,1,0:T(8,128)} custom-call(s32[8,2]{1,0:T(8,128)S(1)} %copy.14.offsets.own.own_offsets, s32[8,2]{1,0:T(8,128)S(1)} %get-tuple-element.45.refs_0_.middle, s32[8,2]{1,0:T(8,128)S(1)} %collective-permute-done.far, f32[16,64,128]{2,1,0:T(8,128)S(1)} %get-tuple-element.74.refs_0_, ...), custom_call_target="tpu_custom_call" | custom-call | bytes 5242880 | tf_op jit(solution)/shard_map/pallas_call | solution.py:414
  87.2 1.7 %all-to-all-done.1.own = f32[8,8,8,128]{3,2,1,0:T(8,128)S(1)} async-done(((f32[8,8,8,128]{3,2,1,0:T(8,128)}), f32[8,8,8,128]{3,2,1,0:T(8,128)S(1)}, u32[]{:S(2)}, u32[]{:S(2)}) %all-to-all-start.1) | async-done | bytes 262176 | tf_op jit(solution)/shard_map/all_to_all | solution.py:438
  88.9 2.2 %collective-permute-start.10 = (f32[8,8,8,128]{3,2,1,0:T(8,128)S(1)}, f32[8,8,8,128]{3,2,1,0:T(8,128)S(1)}, u32[]{:S(2)}, u32[]{:S(2)}) collective-permute-start(f32[8,8,8,128]{3,2,1,0:T(8,128)S(1)} %all-to-all-done.1.own), channel_id=1, source_target_pairs={{0,1},{1,0},{2,3},{3,2},{4,5},{5,4},{6,7},{7,6},{8,9},{9,8},{10,11... | collective-permute-start | bytes 786440 | tf_op jit(solution)/shard_map/ppermute | solution.py:449
  91.1 1.2 %collective-permute-done.10.other = f32[8,8,8,128]{3,2,1,0:T(8,128)S(1)} collective-permute-done((f32[8,8,8,128]{3,2,1,0:T(8,128)S(1)}, f32[8,8,8,128]{3,2,1,0:T(8,128)S(1)}, u32[]{:S(2)}, u32[]{:S(2)}) %collective-permute-start.10) | collective-permute-done | bytes 262176 | tf_op jit(solution)/shard_map/ppermute | solution.py:449
  92.3 1.5 %shard_map.94 = f32[8,128,128]{2,1,0:T(8,128)} custom-call(s32[8,2]{1,0:T(8,128)S(1)} %copy.14.offsets.own.own_offsets, f32[8,8,8,128]{3,2,1,0:T(8,128)S(1)} %all-to-all-done.1.own, f32[8,8,8,128]{3,2,1,0:T(8,128)S(1)} %collective-permute-done.10.other), custom_call_target="tpu_custom_call" | custom-call | tf_op jit(solution)/shard_map/pallas_call | solution.py:443
  (12 shorter events, 0.1 us)
Async XLA Ops:
  1.4 6.1 %collective-permute-start = (s32[8,2]{1,0:T(8,128)S(1)}, s32[8,2]{1,0:T(8,128)S(1)}, u32[]{:S(2)}, u32[]{:S(2)}) collective-permute-start(s32[8,2]{1,0:T(8,128)S(1)} %copy.14.offsets.own.own_offsets), channel_id=1, source_target_pairs={{0,2},{1,3},{2,4},{3,5},{4,6},{5,7},{6,8},{7,9},{8,10},{9,11},{10,... | collective-permute-start | bytes 200 | tf_op jit(solution)/shard_map/ppermute | solution.py:21
  4.1 1.0 %copy-start.2 = (f32[8,128,128]{2,1,0:T(8,128)S(1)}, f32[8,128,128]{2,1,0:T(8,128)}, u32[]{:S(2)}) copy-start(f32[8,128,128]{2,1,0:T(8,128)} %measured.1) | copy-start | bytes 1572868
  5.1 8.8 %copy-start.9 = (f32[128,128]{1,0:T(8,128)S(1)}, f32[128,128]{1,0:T(8,128)}, u32[]{:S(2)}) copy-start(f32[128,128]{1,0:T(8,128)} %param.9) | copy-start | bytes 196612
  7.5 6.8 %collective-permute-start.1 = (f32[1040,128]{1,0:T(8,128)S(1)}, f32[1040,128]{1,0:T(8,128)S(1)}, u32[]{:S(2)}, u32[]{:S(2)}) collective-permute-start(f32[1040,128]{1,0:T(8,128)S(1)} %shard_map.86), channel_id=1, source_target_pairs={{0,1},{1,2},{2,3},{3,4},{4,5},{5,6},{6,7},{7,8},{8,9},{9,10},{10,1... | collective-permute-start | bytes 1597448 | tf_op jit(solution)/shard_map/ppermute | solution.py:21
  7.9 1.6 %copy-start = (f32[2,2,64,2048]{3,2,1,0:T(8,128)S(1)}, f32[2,2,64,2048]{3,2,1,0:T(8,128)}, u32[]{:S(2)}) copy-start(f32[2,2,64,2048]{3,2,1,0:T(8,128)} %param.7) | copy-start | bytes 6291460
  9.5 4.7 %copy-start.1 = (f32[2,2,64,2048]{3,2,1,0:T(8,128)S(1)}, f32[2,2,64,2048]{3,2,1,0:T(8,128)}, u32[]{:S(2)}) copy-start(f32[2,2,64,2048]{3,2,1,0:T(8,128)} %param.7) | copy-start | bytes 6291460
  11.7 5.2 %collective-permute-start.2 = (f32[16,64,128]{2,1,0:T(8,128)}, f32[16,64,128]{2,1,0:T(8,128)}, u32[]{:S(2)}, u32[]{:S(2)}) collective-permute-start(f32[16,64,128]{2,1,0:T(8,128)} %get-tuple-element.46), channel_id=1, source_target_pairs={{0,1},{1,0},{2,3},{3,2},{4,5},{5,4},{6,7},{7,6},{8,9},{9,8},{10,11... | collective-permute-start | bytes 1572872 | tf_op jit(solution)/shard_map/ppermute | solution.py:363
  12.8 18.3 %collective-permute-start.3 = (f32[16,64,128]{2,1,0:T(8,128)}, f32[16,64,128]{2,1,0:T(8,128)}, u32[]{:S(2)}, u32[]{:S(2)}) collective-permute-start(f32[16,64,128]{2,1,0:T(8,128)} %get-tuple-element.47), channel_id=1, source_target_pairs={{0,15},{1,2},{2,1},{3,4},{4,3},{5,6},{6,5},{7,8},{8,7},{9,10},{10,... | collective-permute-start | bytes 1572872 | tf_op jit(solution)/shard_map/ppermute | solution.py:363
  14.2 16.8 %copy-start.7 = (f32[4,2,128,128]{3,2,1,0:T(8,128)S(1)}, f32[4,2,128,128]{3,2,1,0:T(8,128)}, u32[]{:S(2)}) copy-start(f32[4,2,128,128]{3,2,1,0:T(8,128)} %refs_5_.3) | copy-start | bytes 1572868
  14.3 16.8 %copy-start.8 = (bf16[8,256,256]{2,1,0:T(8,128)(2,1)S(1)}, bf16[8,256,256]{2,1,0:T(8,128)(2,1)}, u32[]{:S(2)}) copy-start(bf16[8,256,256]{2,1,0:T(8,128)(2,1)} %constant.2.clone.refs_7_) | copy-start | bytes 3145732
  31.1 13.7 %collective-permute-start.4 = (f32[16,64,128]{2,1,0:T(8,128)S(1)}, f32[16,64,128]{2,1,0:T(8,128)S(1)}, u32[]{:S(2)}, u32[]{:S(2)}) collective-permute-start(f32[16,64,128]{2,1,0:T(8,128)S(1)} %get-tuple-element.54), channel_id=1, source_target_pairs={{0,1},{1,0},{2,3},{3,2},{4,5},{5,4},{6,7},{7,6},{8,9},{9,8},{10,11... | collective-permute-start | bytes 1572872 | tf_op jit(solution)/shard_map/ppermute | solution.py:363
  31.1 14.2 %collective-permute-start.5 = (f32[16,64,128]{2,1,0:T(8,128)S(1)}, f32[16,64,128]{2,1,0:T(8,128)S(1)}, u32[]{:S(2)}, u32[]{:S(2)}) collective-permute-start(f32[16,64,128]{2,1,0:T(8,128)S(1)} %get-tuple-element.55), channel_id=1, source_target_pairs={{0,15},{1,2},{2,1},{3,4},{4,3},{5,6},{6,5},{7,8},{8,7},{9,10},{10,... | collective-permute-start | bytes 1572872 | tf_op jit(solution)/shard_map/ppermute | solution.py:363
  43.0 14.3 %collective-permute-start.6 = (f32[16,64,128]{2,1,0:T(8,128)S(1)}, f32[16,64,128]{2,1,0:T(8,128)S(1)}, u32[]{:S(2)}, u32[]{:S(2)}) collective-permute-start(f32[16,64,128]{2,1,0:T(8,128)S(1)} %get-tuple-element.63), channel_id=1, source_target_pairs={{0,15},{1,2},{2,1},{3,4},{4,3},{5,6},{6,5},{7,8},{8,7},{9,10},{10,... | collective-permute-start | bytes 1572872 | tf_op jit(solution)/shard_map/ppermute | solution.py:410
  46.5 30.6 %copy-start.3 = (f32[16,64,128]{2,1,0:T(8,128)}, f32[16,64,128]{2,1,0:T(8,128)S(1)}, u32[]{:S(2)}) copy-start(f32[16,64,128]{2,1,0:T(8,128)S(1)} %get-tuple-element.77.refs_3_) | copy-start | bytes 1572868
  57.3 1.6 %collective-permute-start.7 = (f32[8,9,8,128]{3,2,1,0:T(8,128)S(1)}, f32[8,9,8,128]{3,2,1,0:T(8,128)S(1)}, u32[]{:S(2)}, u32[]{:S(2)}) collective-permute-start(f32[8,9,8,128]{3,2,1,0:T(8,128)S(1)} %get-tuple-element.65), channel_id=1, source_target_pairs={{0,1},{1,0},{2,3},{3,2},{4,5},{5,4},{6,7},{7,6},{8,9},{9,8},{10,11... | collective-permute-start | bytes 884744 | tf_op jit(solution)/shard_map/ppermute | solution.py:425
  58.9 18.3 %collective-permute-start.8 = (f32[32,64,128]{2,1,0:T(8,128)S(1)}, f32[32,64,128]{2,1,0:T(8,128)S(1)}, u32[]{:S(2)}, u32[]{:S(2)}) collective-permute-start(f32[32,64,128]{2,1,0:T(8,128)S(1)} %get-tuple-element.70), channel_id=1, source_target_pairs={{0,1},{1,0},{2,3},{3,2},{4,5},{5,4},{6,7},{7,6},{8,9},{9,8},{10,11... | collective-permute-start | bytes 3145736 | tf_op jit(solution)/shard_map/ppermute | solution.py:426
  59.0 18.1 %collective-permute-start.9 = (f32[16,64,128]{2,1,0:T(8,128)S(1)}, f32[16,64,128]{2,1,0:T(8,128)S(1)}, u32[]{:S(2)}, u32[]{:S(2)}) collective-permute-start(f32[16,64,128]{2,1,0:T(8,128)S(1)} %get-tuple-element.72), channel_id=1, source_target_pairs={{0,15},{1,2},{2,1},{3,4},{4,3},{5,6},{6,5},{7,8},{8,7},{9,10},{10,... | collective-permute-start | bytes 1572872 | tf_op jit(solution)/shard_map/ppermute | solution.py:410
  77.1 0.8 copy-start.5
  77.9 11.0 %all-to-all-start.1 = ((f32[8,8,8,128]{3,2,1,0:T(8,128)}), f32[8,8,8,128]{3,2,1,0:T(8,128)S(1)}, u32[]{:S(2)}, u32[]{:S(2)}) async-start(f32[8,8,8,128]{3,2,1,0:T(8,128)} %shard_map.92), calls=%async_computation.1 | async-start | bytes 524288 | tf_op jit(solution)/shard_map/all_to_all | solution.py:438
  81.3 1.0 %copy-start.4 = (f32[16,64,128]{2,1,0:T(8,128)S(1)}, f32[16,64,128]{2,1,0:T(8,128)}, u32[]{:S(2)}) copy-start(f32[16,64,128]{2,1,0:T(8,128)} %copy-done.3) | copy-start | bytes 1572868
  82.4 1.0 %copy-start.6 = (f32[16,64,128]{2,1,0:T(8,128)S(1)}, f32[16,64,128]{2,1,0:T(8,128)}, u32[]{:S(2)}) copy-start(f32[16,64,128]{2,1,0:T(8,128)} %copy-done.5) | copy-start | bytes 1572868
  88.9 3.4 %collective-permute-start.10 = (f32[8,8,8,128]{3,2,1,0:T(8,128)S(1)}, f32[8,8,8,128]{3,2,1,0:T(8,128)S(1)}, u32[]{:S(2)}, u32[]{:S(2)}) collective-permute-start(f32[8,8,8,128]{3,2,1,0:T(8,128)S(1)} %all-to-all-done.1.own), channel_id=1, source_target_pairs={{0,1},{1,0},{2,3},{3,2},{4,5},{5,4},{6,7},{7,6},{8,9},{9,8},{10,11... | collective-permute-start | bytes 786440 | tf_op jit(solution)/shard_map/ppermute | solution.py:449

commit v10 on v9

--- a/solution.py
+++ b/solution.py
@@ -433,8 +433,8 @@
         out_specs=in_vmem(),
         compiler_params=params,
     )(parts)
+    spread, back = lax.optimization_barrier((spread, back))
     strips = [part for parts in zip(mid, back, [from_pair] * len(mid)) for part in parts]
-    spread, strips = lax.optimization_barrier((spread, strips))
     gathered = lax.all_to_all(spread, "chip", 0, 0)
     object_grad = added(groups, strips)
     gathered, object_grad = lax.optimization_barrier((gathered, object_grad))

time: 95.6 us -> 95.6 us (level)
  starting transfers between devices: 13.7 us -> 15.9 us
  waiting for transfers between devices: 31.5 us -> 30.2 us
  Pallas kernels: 24.5 us -> 25.5 us
    all_to_all x1, starting transfers between devices: 3.41 us -> 5.1 us  [local(): gathered = lax.all_to_all(spread, 'chip', 0, 0)]
    pallas_call x2, Pallas kernels: 13.1 us -> 14.1 us  [local(): pl.pallas_call(functools.partial(slot_kernel, first, size, len(earlier)),...]
where the time goes in v10:
time: 95.6 us; the launch traced here: 94.4 us
  waiting for transfers between devices  30.2 us (32%)
  Pallas kernels  25.5 us (27%)
  starting transfers between devices  15.9 us (17%)
  blocking collectives  15.6 us (16%)
  local copies, waits for them, and re-layouts  5.51 us (6%)
  between operations  1.43 us (1%)
    all_to_all x1, blocking collectives, local(): parts = lax.all_to_all(both, 'chip', 0, 0)  15.6 us
    ppermute x2, waiting for transfers between devices, swapped(): lax.ppermute(to_cross, ROW, other_pair)  14.7 us
    pallas_call x2, Pallas kernels, local(): pl.pallas_call(functools.partial(slot_kernel, first, size, len(earlier)),...  14.1 us
    ppermute x2, waiting for transfers between devices, local(): back.append(lax.ppermute(to_cross, ROW, other_pair))  9.78 us
    unnamed x21, local copies, waits for them, and re-layouts  5.49 us
    all_to_all x1, starting transfers between devices, local(): gathered = lax.all_to_all(spread, 'chip', 0, 0)  5.1 us
    pallas_call x1, Pallas kernels, added(): pl.pallas_call(functools.partial(add_kernel, pixels, groups), out_shape=j...  3.78 us
    pallas_call x2, Pallas kernels, strips(): pl.pallas_call(functools.partial(cut_kernel, pixels, chunks), out_shape=s...  3.48 us
  transfers between devices with their start and end apart: 12, of which 7 were waited for; matrix products, arithmetic and copies ran while one was open for 0% of the time, Pallas kernels for 25%

profile of v10, /device:TPU:1, one launch (start us, length us, event | category | flops | bytes accessed | tf_op | source)
XLA Modules:
  0.0 94.4 jit_solution(2218900162407065994)
XLA Ops:
  0.6 0.8 copy.14.offsets.own.own_offsets
  1.4 2.1 %collective-permute-start = (s32[8,2]{1,0:T(8,128)S(1)}, s32[8,2]{1,0:T(8,128)S(1)}, u32[]{:S(2)}, u32[]{:S(2)}) collective-permute-start(s32[8,2]{1,0:T(8,128)S(1)} %copy.14.offsets.own.own_offsets), channel_id=1, source_target_pairs={{0,2},{1,3},{2,4},{3,5},{4,6},{5,7},{6,8},{7,9},{8,10},{9,11},{10,... | collective-permute-start | bytes 200 | tf_op jit(solution)/shard_map/ppermute | solution.py:21
  4.1 0.0 copy-start.2
  4.1 1.0 %copy-done.2 = f32[8,128,128]{2,1,0:T(8,128)S(1)} copy-done((f32[8,128,128]{2,1,0:T(8,128)S(1)}, f32[8,128,128]{2,1,0:T(8,128)}, u32[]{:S(2)}) %copy-start.2) | copy-done | bytes 524312
  5.2 0.6 shard_map.86
  5.8 1.7 %collective-permute-done.far = s32[8,2]{1,0:T(8,128)S(1)} collective-permute-done((s32[8,2]{1,0:T(8,128)S(1)}, s32[8,2]{1,0:T(8,128)S(1)}, u32[]{:S(2)}, u32[]{:S(2)}) %collective-permute-start) | collective-permute-done | bytes 96 | tf_op jit(solution)/shard_map/ppermute | solution.py:21
  7.5 0.5 collective-permute-start.1
  7.9 1.6 %copy-done = f32[2,2,64,2048]{3,2,1,0:T(8,128)S(1)} copy-done((f32[2,2,64,2048]{3,2,1,0:T(8,128)S(1)}, f32[2,2,64,2048]{3,2,1,0:T(8,128)}, u32[]{:S(2)}) %copy-start) | copy-done | bytes 2097176
  9.5 2.2 %shard_map.88 = (f32[16,64,128]{2,1,0:T(8,128)}, f32[16,64,128]{2,1,0:T(8,128)}) custom-call(s32[8,2]{1,0:T(8,128)S(1)} %copy.14.offsets.own.own_offsets, s32[8,2]{1,0:T(8,128)S(1)} %collective-permute-done.far, f32[4,64,2048]{2,1,0:T(8,128)S(1)} %bitcast.5), custom_call_target="tpu_custom_call" | custom-call | bytes 4194304 | tf_op jit(solution)/shard_map/pallas_call | solution.py:352
  11.7 1.1 %collective-permute-start.2 = (f32[16,64,128]{2,1,0:T(8,128)}, f32[16,64,128]{2,1,0:T(8,128)}, u32[]{:S(2)}, u32[]{:S(2)}) collective-permute-start(f32[16,64,128]{2,1,0:T(8,128)} %get-tuple-element.42), channel_id=1, source_target_pairs={{0,1},{1,0},{2,3},{3,2},{4,5},{5,4},{6,7},{7,6},{8,9},{9,8},{10,11... | collective-permute-start | bytes 1572872 | tf_op jit(solution)/shard_map/ppermute | solution.py:363
  12.8 1.1 %collective-permute-start.3 = (f32[16,64,128]{2,1,0:T(8,128)}, f32[16,64,128]{2,1,0:T(8,128)}, u32[]{:S(2)}, u32[]{:S(2)}) collective-permute-start(f32[16,64,128]{2,1,0:T(8,128)} %get-tuple-element.43), channel_id=1, source_target_pairs={{0,15},{1,2},{2,1},{3,4},{4,3},{5,6},{6,5},{7,8},{8,7},{9,10},{10,... | collective-permute-start | bytes 1572872 | tf_op jit(solution)/shard_map/ppermute | solution.py:363
  13.9 0.0 copy-done.9
  14.0 0.2 fusion.1
  14.2 0.0 copy-start.7
  14.3 0.0 copy-start.8
  14.3 0.0 collective-permute-done.1.target.refs_4_
  14.3 0.0 copy-done.1
  14.3 1.3 %shard_map.89 = (f32[16,64,128]{2,1,0:T(8,128)S(1)}, f32[16,64,128]{2,1,0:T(8,128)S(1)}) custom-call(s32[8,2]{1,0:T(8,128)S(1)} %copy.14.offsets.own.own_offsets, s32[8,2]{1,0:T(8,128)S(1)} %collective-permute-done.far, f32[4,64,2048]{2,1,0:T(8,128)S(1)} %bitcast.6), custom_call_target="tpu_custom_call" | custom-call | bytes 4194304 | tf_op jit(solution)/shard_map/pallas_call | solution.py:352
  15.6 1.3 %shard_map.87 = (f32[16,64,128]{2,1,0:T(8,128)S(1)}, f32[16,64,128]{2,1,0:T(8,128)S(1)}, s32[8,2]{1,0:T(8,128)S(1)}) custom-call(f32[1040,128]{1,0:T(8,128)S(1)} %collective-permute-done.1.target.refs_4_, f32[4,64,2048]{2,1,0:T(8,128)S(1)} %bitcast.7), custom_call_target="tpu_custom_call" | custom-call | bytes 4194304 | tf_op jit(solution)/shard_map/pallas_call | solution.py:367
  16.9 0.0 collective-permute-done.2.refs_2_
  16.9 14.2 %collective-permute-done.3.refs_3_ = f32[16,64,128]{2,1,0:T(8,128)} collective-permute-done((f32[16,64,128]{2,1,0:T(8,128)}, f32[16,64,128]{2,1,0:T(8,128)}, u32[]{:S(2)}, u32[]{:S(2)}) %collective-permute-start.3) | collective-permute-done | bytes 524320 | tf_op jit(solution)/shard_map/ppermute | solution.py:363
  31.1 0.0 collective-permute-start.4
  31.1 0.0 collective-permute-start.5
  31.1 0.0 copy-done.7
  31.1 0.0 copy-done.8
  31.1 11.9 %shard_map.90 = (f32[16,64,128]{2,1,0:T(8,128)S(1)}, f32[16,64,128]{2,1,0:T(8,128)S(1)}, f32[16,64,128]{2,1,0:T(8,128)S(1)}, f32[9,128,128]{2,1,0:T(8,128)S(1)}) custom-call(s32[8,2]{1,0:T(8,128)S(1)} %copy.14.offsets.own.own_offsets, s32[8,2]{1,0:T(8,128)S(1)} %get-tuple-element.41.refs_0_.middle, f32[16,64,128]{2,1,0:T(8,128)S(1)} %get-tuple-element.52.refs_1_, ...), custom_call_target="tpu_custom_call" | custom-call | flops 9663676416 | bytes 8388608 | tf_op jit(solution)/shard_map/pallas_call | solution.py:396
  43.0 1.8 %collective-permute-start.6 = (f32[16,64,128]{2,1,0:T(8,128)S(1)}, f32[16,64,128]{2,1,0:T(8,128)S(1)}, u32[]{:S(2)}, u32[]{:S(2)}) collective-permute-start(f32[16,64,128]{2,1,0:T(8,128)S(1)} %get-tuple-element.59), channel_id=1, source_target_pairs={{0,15},{1,2},{2,1},{3,4},{4,3},{5,6},{6,5},{7,8},{8,7},{9,10},{10,... | collective-permute-start | bytes 1572872 | tf_op jit(solution)/shard_map/ppermute | solution.py:410
  44.8 0.0 collective-permute-done.4.refs_2_
  44.8 0.5 collective-permute-done.5.refs_3_
  45.3 2.2 %shard_map.91 = (f32[32,64,128]{2,1,0:T(8,128)}, f32[16,64,128]{2,1,0:T(8,128)S(1)}, f32[16,64,128]{2,1,0:T(8,128)S(1)}, f32[8,9,8,128]{3,2,1,0:T(8,128)S(1)}, f32[8,9,8,128]{3,2,1,0:T(8,128)S(1)}) custom-call(s32[8,2]{1,0:T(8,128)S(1)} %copy.14.offsets.own.own_offsets, s32[8,2]{1,0:T(8,128)S(1)} %get-tuple-element.41.refs_0_.middle, ...), custom_call_target="tpu_custom_call" | custom-call | flops 9663676416 | bytes 8388608 | tf_op jit(solution)/shard_map/pallas_call | solution.py:396
  47.5 9.8 %collective-permute-done.6.refs_1_ = f32[16,64,128]{2,1,0:T(8,128)S(1)} collective-permute-done((f32[16,64,128]{2,1,0:T(8,128)S(1)}, f32[16,64,128]{2,1,0:T(8,128)S(1)}, u32[]{:S(2)}, u32[]{:S(2)}) %collective-permute-start.6) | collective-permute-done | bytes 524320 | tf_op jit(solution)/shard_map/ppermute | solution.py:410
  57.3 0.0 collective-permute-start.7
  57.3 1.6 %collective-permute-done.7 = f32[8,9,8,128]{3,2,1,0:T(8,128)S(1)} collective-permute-done((f32[8,9,8,128]{3,2,1,0:T(8,128)S(1)}, f32[8,9,8,128]{3,2,1,0:T(8,128)S(1)}, u32[]{:S(2)}, u32[]{:S(2)}) %collective-permute-start.7) | collective-permute-done | bytes 294944 | tf_op jit(solution)/shard_map/ppermute | solution.py:425
  58.9 0.1 collective-permute-start.9
  59.0 1.4 %collective-permute-start.8 = (f32[16,64,128]{2,1,0:T(8,128)S(1)}, f32[16,64,128]{2,1,0:T(8,128)S(1)}, u32[]{:S(2)}, u32[]{:S(2)}) collective-permute-start(f32[16,64,128]{2,1,0:T(8,128)S(1)} %get-tuple-element.65), channel_id=1, source_target_pairs={{0,15},{1,2},{2,1},{3,4},{4,3},{5,6},{6,5},{7,8},{8,7},{9,10},{10,... | collective-permute-start | bytes 1572872 | tf_op jit(solution)/shard_map/ppermute | solution.py:410
  60.5 15.6 %all_to_all.10.parts = f32[8,9,8,128]{3,2,1,0:T(8,128)S(1)} all-to-all(f32[8,9,8,128]{3,2,1,0:T(8,128)S(1)} %add.3), channel_id=1, replica_groups=mesh['grp'=2,'chip'=8,'core'=2] {'chip'}, dimensions={0} | all-to-all | bytes 589824 | tf_op jit(solution)/shard_map/all_to_all | solution.py:428
  76.0 0.7 shard_map.92
  76.8 0.0 collective-permute-done.8.refs_4_
  76.8 5.1 %all-to-all-start.1 = ((f32[8,8,8,128]{3,2,1,0:T(8,128)}), f32[8,8,8,128]{3,2,1,0:T(8,128)S(1)}, u32[]{:S(2)}, u32[]{:S(2)}) async-start(f32[8,8,8,128]{3,2,1,0:T(8,128)} %shard_map.92), calls=%async_computation.1 | async-start | bytes 524288 | tf_op jit(solution)/shard_map/all_to_all | solution.py:438
  81.9 0.0 collective-permute-done.9.refs_2_.refs_5_
  81.9 0.0 copy-start.4
  81.9 1.0 %copy-done.4 = f32[16,64,128]{2,1,0:T(8,128)S(1)} copy-done((f32[16,64,128]{2,1,0:T(8,128)S(1)}, f32[16,64,128]{2,1,0:T(8,128)}, u32[]{:S(2)}) %copy-start.4) | copy-done | bytes 524312
  83.0 1.0 %copy-done.6 = f32[16,64,128]{2,1,0:T(8,128)S(1)} copy-done((f32[16,64,128]{2,1,0:T(8,128)S(1)}, f32[16,64,128]{2,1,0:T(8,128)}, u32[]{:S(2)}) %copy-start.6) | copy-done | bytes 524312
  84.0 3.8 %shard_map.93 = f32[4,64,2048]{2,1,0:T(8,128)} custom-call(s32[8,2]{1,0:T(8,128)S(1)} %copy.14.offsets.own.own_offsets, s32[8,2]{1,0:T(8,128)S(1)} %get-tuple-element.41.refs_0_.middle, s32[8,2]{1,0:T(8,128)S(1)} %collective-permute-done.far, f32[16,64,128]{2,1,0:T(8,128)S(1)} %get-tuple-element.67.refs_0_, ...), custom_call_target="tpu_custom_call" | custom-call | bytes 5242880 | tf_op jit(solution)/shard_map/pallas_call | solution.py:414
  87.8 1.3 %all-to-all-done.1.own = f32[8,8,8,128]{3,2,1,0:T(8,128)S(1)} async-done(((f32[8,8,8,128]{3,2,1,0:T(8,128)}), f32[8,8,8,128]{3,2,1,0:T(8,128)S(1)}, u32[]{:S(2)}, u32[]{:S(2)}) %all-to-all-start.1) | async-done | bytes 262176 | tf_op jit(solution)/shard_map/all_to_all | solution.py:438
  89.1 2.7 %collective-permute-start.10 = (f32[8,8,8,128]{3,2,1,0:T(8,128)S(1)}, f32[8,8,8,128]{3,2,1,0:T(8,128)S(1)}, u32[]{:S(2)}, u32[]{:S(2)}) collective-permute-start(f32[8,8,8,128]{3,2,1,0:T(8,128)S(1)} %all-to-all-done.1.own), channel_id=1, source_target_pairs={{0,1},{1,0},{2,3},{3,2},{4,5},{5,4},{6,7},{7,6},{8,9},{9,8},{10,11... | collective-permute-start | bytes 786440 | tf_op jit(solution)/shard_map/ppermute | solution.py:449
  91.8 1.2 %collective-permute-done.10.other = f32[8,8,8,128]{3,2,1,0:T(8,128)S(1)} collective-permute-done((f32[8,8,8,128]{3,2,1,0:T(8,128)S(1)}, f32[8,8,8,128]{3,2,1,0:T(8,128)S(1)}, u32[]{:S(2)}, u32[]{:S(2)}) %collective-permute-start.10) | collective-permute-done | bytes 262176 | tf_op jit(solution)/shard_map/ppermute | solution.py:449
  92.9 1.5 %shard_map.94 = f32[8,128,128]{2,1,0:T(8,128)} custom-call(s32[8,2]{1,0:T(8,128)S(1)} %copy.14.offsets.own.own_offsets, f32[8,8,8,128]{3,2,1,0:T(8,128)S(1)} %all-to-all-done.1.own, f32[8,8,8,128]{3,2,1,0:T(8,128)S(1)} %collective-permute-done.10.other), custom_call_target="tpu_custom_call" | custom-call | tf_op jit(solution)/shard_map/pallas_call | solution.py:443
  (12 shorter events, 0.1 us)
Async XLA Ops:
  1.4 6.1 %collective-permute-start = (s32[8,2]{1,0:T(8,128)S(1)}, s32[8,2]{1,0:T(8,128)S(1)}, u32[]{:S(2)}, u32[]{:S(2)}) collective-permute-start(s32[8,2]{1,0:T(8,128)S(1)} %copy.14.offsets.own.own_offsets), channel_id=1, source_target_pairs={{0,2},{1,3},{2,4},{3,5},{4,6},{5,7},{6,8},{7,9},{8,10},{9,11},{10,... | collective-permute-start | bytes 200 | tf_op jit(solution)/shard_map/ppermute | solution.py:21
  4.1 1.0 %copy-start.2 = (f32[8,128,128]{2,1,0:T(8,128)S(1)}, f32[8,128,128]{2,1,0:T(8,128)}, u32[]{:S(2)}) copy-start(f32[8,128,128]{2,1,0:T(8,128)} %measured.1) | copy-start | bytes 1572868
  5.1 8.8 %copy-start.9 = (f32[128,128]{1,0:T(8,128)S(1)}, f32[128,128]{1,0:T(8,128)}, u32[]{:S(2)}) copy-start(f32[128,128]{1,0:T(8,128)} %param.9) | copy-start | bytes 196612
  7.5 6.8 %collective-permute-start.1 = (f32[1040,128]{1,0:T(8,128)S(1)}, f32[1040,128]{1,0:T(8,128)S(1)}, u32[]{:S(2)}, u32[]{:S(2)}) collective-permute-start(f32[1040,128]{1,0:T(8,128)S(1)} %shard_map.86), channel_id=1, source_target_pairs={{0,1},{1,2},{2,3},{3,4},{4,5},{5,6},{6,7},{7,8},{8,9},{9,10},{10,1... | collective-permute-start | bytes 1597448 | tf_op jit(solution)/shard_map/ppermute | solution.py:21
  7.9 1.6 %copy-start = (f32[2,2,64,2048]{3,2,1,0:T(8,128)S(1)}, f32[2,2,64,2048]{3,2,1,0:T(8,128)}, u32[]{:S(2)}) copy-start(f32[2,2,64,2048]{3,2,1,0:T(8,128)} %param.7) | copy-start | bytes 6291460
  9.5 4.7 %copy-start.1 = (f32[2,2,64,2048]{3,2,1,0:T(8,128)S(1)}, f32[2,2,64,2048]{3,2,1,0:T(8,128)}, u32[]{:S(2)}) copy-start(f32[2,2,64,2048]{3,2,1,0:T(8,128)} %param.7) | copy-start | bytes 6291460
  11.7 5.2 %collective-permute-start.2 = (f32[16,64,128]{2,1,0:T(8,128)}, f32[16,64,128]{2,1,0:T(8,128)}, u32[]{:S(2)}, u32[]{:S(2)}) collective-permute-start(f32[16,64,128]{2,1,0:T(8,128)} %get-tuple-element.42), channel_id=1, source_target_pairs={{0,1},{1,0},{2,3},{3,2},{4,5},{5,4},{6,7},{7,6},{8,9},{9,8},{10,11... | collective-permute-start | bytes 1572872 | tf_op jit(solution)/shard_map/ppermute | solution.py:363
  12.8 18.3 %collective-permute-start.3 = (f32[16,64,128]{2,1,0:T(8,128)}, f32[16,64,128]{2,1,0:T(8,128)}, u32[]{:S(2)}, u32[]{:S(2)}) collective-permute-start(f32[16,64,128]{2,1,0:T(8,128)} %get-tuple-element.43), channel_id=1, source_target_pairs={{0,15},{1,2},{2,1},{3,4},{4,3},{5,6},{6,5},{7,8},{8,7},{9,10},{10,... | collective-permute-start | bytes 1572872 | tf_op jit(solution)/shard_map/ppermute | solution.py:363
  14.2 16.8 %copy-start.7 = (f32[4,2,128,128]{3,2,1,0:T(8,128)S(1)}, f32[4,2,128,128]{3,2,1,0:T(8,128)}, u32[]{:S(2)}) copy-start(f32[4,2,128,128]{3,2,1,0:T(8,128)} %refs_5_.3) | copy-start | bytes 1572868
  14.3 16.8 %copy-start.8 = (bf16[8,256,256]{2,1,0:T(8,128)(2,1)S(1)}, bf16[8,256,256]{2,1,0:T(8,128)(2,1)}, u32[]{:S(2)}) copy-start(bf16[8,256,256]{2,1,0:T(8,128)(2,1)} %constant.2.clone.refs_7_) | copy-start | bytes 3145732
  31.1 13.7 %collective-permute-start.4 = (f32[16,64,128]{2,1,0:T(8,128)S(1)}, f32[16,64,128]{2,1,0:T(8,128)S(1)}, u32[]{:S(2)}, u32[]{:S(2)}) collective-permute-start(f32[16,64,128]{2,1,0:T(8,128)S(1)} %get-tuple-element.50), channel_id=1, source_target_pairs={{0,1},{1,0},{2,3},{3,2},{4,5},{5,4},{6,7},{7,6},{8,9},{9,8},{10,11... | collective-permute-start | bytes 1572872 | tf_op jit(solution)/shard_map/ppermute | solution.py:363
  31.1 14.2 %collective-permute-start.5 = (f32[16,64,128]{2,1,0:T(8,128)S(1)}, f32[16,64,128]{2,1,0:T(8,128)S(1)}, u32[]{:S(2)}, u32[]{:S(2)}) collective-permute-start(f32[16,64,128]{2,1,0:T(8,128)S(1)} %get-tuple-element.51), channel_id=1, source_target_pairs={{0,15},{1,2},{2,1},{3,4},{4,3},{5,6},{6,5},{7,8},{8,7},{9,10},{10,... | collective-permute-start | bytes 1572872 | tf_op jit(solution)/shard_map/ppermute | solution.py:363
  43.0 14.3 %collective-permute-start.6 = (f32[16,64,128]{2,1,0:T(8,128)S(1)}, f32[16,64,128]{2,1,0:T(8,128)S(1)}, u32[]{:S(2)}, u32[]{:S(2)}) collective-permute-start(f32[16,64,128]{2,1,0:T(8,128)S(1)} %get-tuple-element.59), channel_id=1, source_target_pairs={{0,15},{1,2},{2,1},{3,4},{4,3},{5,6},{6,5},{7,8},{8,7},{9,10},{10,... | collective-permute-start | bytes 1572872 | tf_op jit(solution)/shard_map/ppermute | solution.py:410
  47.5 29.3 %copy-start.3 = (f32[16,64,128]{2,1,0:T(8,128)}, f32[16,64,128]{2,1,0:T(8,128)S(1)}, u32[]{:S(2)}) copy-start(f32[16,64,128]{2,1,0:T(8,128)S(1)} %get-tuple-element.70.refs_3_) | copy-start | bytes 1572868
  57.3 1.6 %collective-permute-start.7 = (f32[8,9,8,128]{3,2,1,0:T(8,128)S(1)}, f32[8,9,8,128]{3,2,1,0:T(8,128)S(1)}, u32[]{:S(2)}, u32[]{:S(2)}) collective-permute-start(f32[8,9,8,128]{3,2,1,0:T(8,128)S(1)} %get-tuple-element.61), channel_id=1, source_target_pairs={{0,1},{1,0},{2,3},{3,2},{4,5},{5,4},{6,7},{7,6},{8,9},{9,8},{10,11... | collective-permute-start | bytes 884744 | tf_op jit(solution)/shard_map/ppermute | solution.py:425
  58.9 23.0 %collective-permute-start.9 = (f32[32,64,128]{2,1,0:T(8,128)}, f32[32,64,128]{2,1,0:T(8,128)S(1)}, u32[]{:S(2)}, u32[]{:S(2)}) collective-permute-start(f32[32,64,128]{2,1,0:T(8,128)} %get-tuple-element.69), channel_id=1, source_target_pairs={{0,1},{1,0},{2,3},{3,2},{4,5},{5,4},{6,7},{7,6},{8,9},{9,8},{10,11... | collective-permute-start | bytes 3145736 | tf_op jit(solution)/shard_map/ppermute | solution.py:426
  59.0 17.8 %collective-permute-start.8 = (f32[16,64,128]{2,1,0:T(8,128)S(1)}, f32[16,64,128]{2,1,0:T(8,128)S(1)}, u32[]{:S(2)}, u32[]{:S(2)}) collective-permute-start(f32[16,64,128]{2,1,0:T(8,128)S(1)} %get-tuple-element.65), channel_id=1, source_target_pairs={{0,15},{1,2},{2,1},{3,4},{4,3},{5,6},{6,5},{7,8},{8,7},{9,10},{10,... | collective-permute-start | bytes 1572872 | tf_op jit(solution)/shard_map/ppermute | solution.py:410
  76.8 5.1 %copy-start.5 = (f32[16,64,128]{2,1,0:T(8,128)}, f32[16,64,128]{2,1,0:T(8,128)S(1)}, u32[]{:S(2)}) copy-start(f32[16,64,128]{2,1,0:T(8,128)S(1)} %collective-permute-done.8.refs_4_) | copy-start | bytes 1572868
  76.8 12.3 %all-to-all-start.1 = ((f32[8,8,8,128]{3,2,1,0:T(8,128)}), f32[8,8,8,128]{3,2,1,0:T(8,128)S(1)}, u32[]{:S(2)}, u32[]{:S(2)}) async-start(f32[8,8,8,128]{3,2,1,0:T(8,128)} %shard_map.92), calls=%async_computation.1 | async-start | bytes 524288 | tf_op jit(solution)/shard_map/all_to_all | solution.py:438
  81.9 1.0 %copy-start.4 = (f32[16,64,128]{2,1,0:T(8,128)S(1)}, f32[16,64,128]{2,1,0:T(8,128)}, u32[]{:S(2)}) copy-start(f32[16,64,128]{2,1,0:T(8,128)} %copy-done.3) | copy-start | bytes 1572868
  83.0 1.0 %copy-start.6 = (f32[16,64,128]{2,1,0:T(8,128)S(1)}, f32[16,64,128]{2,1,0:T(8,128)}, u32[]{:S(2)}) copy-start(f32[16,64,128]{2,1,0:T(8,128)} %copy-done.5) | copy-start | bytes 1572868
  89.1 3.9 %collective-permute-start.10 = (f32[8,8,8,128]{3,2,1,0:T(8,128)S(1)}, f32[8,8,8,128]{3,2,1,0:T(8,128)S(1)}, u32[]{:S(2)}, u32[]{:S(2)}) collective-permute-start(f32[8,8,8,128]{3,2,1,0:T(8,128)S(1)} %all-to-all-done.1.own), channel_id=1, source_target_pairs={{0,1},{1,0},{2,3},{3,2},{4,5},{5,4},{6,7},{7,6},{8,9},{9,8},{10,11... | collective-permute-start | bytes 786440 | tf_op jit(solution)/shard_map/ppermute | solution.py:449
